TPU v7x, 256 devices: a whole 4x4x8 slice. The times are simulated.
256 devices in a mesh: lo: 16 (over z_hi, x, core), hi: 16 (over z_lo, y).
Axes of the slice: x: 4, y: 4, z: 8 (z_hi: 2, z_lo: 4; z = z_hi * 4 + z_lo), core: 2. Of those that a mesh axis runs over, the one named last changes fastest.
Arguments:
- queries: bfloat16 [65536, 512], P(('hi', 'lo')), may hold values from -20 to 20
- keys: bfloat16 [65536, 512], P(('hi', 'lo')), may hold values from -20 to 20
- values: bfloat16 [65536, 512], P(('hi', 'lo')), may hold values from -20 to 20
- cotangent: bfloat16 [65536, 512], P(('hi', 'lo')), may hold values from -6 to 6
Outputs:
- mixed: bfloat16 [65536, 512], P(('hi', 'lo'))
- grad_queries: bfloat16 [65536, 512], P(('hi', 'lo'))
- grad_keys: bfloat16 [65536, 512], P(('hi', 'lo'))
- grad_values: bfloat16 [65536, 512], P(('hi', 'lo'))
All inputs are finite; a program needn't handle non-finite values.
Results may differ from a plain program's by a relative error of at most 0.007.
Values may be sent and summed in bfloat16 or wider, within the bound.
No kernel may reach another device: no remote copies, remote signals or barrier semaphores. Data moves between devices by JAX's collectives and lax.ppermute only.
A program may use at most 64 MiB of HBM per device.

v0:
```python
import functools

import jax
import jax.numpy as jnp
import numpy as np
from jax import lax
from jax.experimental import pallas as pl
from jax.experimental.pallas import tpu as pltpu
from jax.sharding import PartitionSpec as P

F32 = jnp.float32
BF16 = jnp.bfloat16
D = 512
TOK = 256
PAIRS = 4
LANES = 128
SCALE = 64**-0.5
NT = (((1,), (1,)), ((), ()))
TN = (((0,), (0,)), ((), ()))


def flip(value, axis, mask):
    return lax.ppermute(value, axis, [(source, source ^ mask) for source in range(16)])


def reversed_bits(number, bits):
    return int(format(number, f"0{bits}b")[::-1], 2) if bits else 0


def token_pooling():
    table = np.zeros((104, TOK), np.float32)
    for base, bits in ((0, 6), (64, 5), (96, 3)):
        span = TOK >> bits
        for place in range(1 << bits):
            row = reversed_bits(place, bits)
            table[base + place, row * span : (row + 1) * span] = 1.0 / span
    return table


def group_pooling():
    table = np.zeros((64, 224), np.float32)

    def put(column, row, core, half, across, weight):
        table[row * 16 + core * 8 + half * 4 + across, column] = weight

    for core in range(2):
        for place in range(16):
            put(core * 16 + place, place % 4, core, 0, 0, 0.25)
            put(96 + core * 16 + place, place % 4, core, 0, 2, 0.25)
            put(128 + core * 16 + place, place % 4, core, 0, 3, 0.25)
        for place in range(32):
            put(32 + core * 32 + place, place % 4, core, 0, 1, 0.125)
        for across in range(4):
            for place in range(8):
                put(160 + across * 16 + core * 8 + place, place % 4, core, 1, across, 0.5)
    return table


def two_heads(block):
    first = lax.broadcasted_iota(jnp.int32, block.shape, 1) < 64
    zero = jnp.zeros_like(block)
    return jnp.concatenate([jnp.where(first, block, zero), jnp.where(first, zero, block)], axis=0)


def dot(left, right, dims=(((1,), (0,)), ((), ()))):
    return lax.dot_general(left, right, dims, preferred_element_type=F32)


def pool_kernel(table_ref, keys_ref, values_ref, zero_ref, one_ref, three_ref):
    for half, ref in enumerate((keys_ref, values_ref)):
        pooled = dot(table_ref[...], ref[...]).astype(BF16)
        columns = slice(half * D, (half + 1) * D)
        zero_ref[:, columns] = pooled[:64]
        one_ref[:, columns] = pooled[64:96]
        three_ref[:, columns] = pooled[96:104]


def stats_kernel(q_ref, do_ref, k_ref, v_ref, out_ref):
    q2 = two_heads(q_ref[...] * SCALE)
    d2 = two_heads(do_ref[...])
    scores = dot(k_ref[...], q2, NT)
    dprobs = dot(v_ref[...], d2, NT)
    largest = jnp.max(scores, axis=0, keepdims=True)
    expsc = jnp.exp(scores - largest)
    out_ref[0, 0:1] = largest
    out_ref[0, 1:2] = jnp.sum(expsc, axis=0, keepdims=True)
    out_ref[0, 2:3] = jnp.sum(expsc * dprobs, axis=0, keepdims=True)


def top_kernel(q_ref, do_ref, k_ref, v_ref, own_ref, low_ref, gk_ref, gv_ref, out_ref):
    q2 = two_heads(q_ref[...] * SCALE)
    d2 = two_heads(do_ref[...])
    scores = dot(k_ref[...], q2, NT)
    dprobs = dot(v_ref[...], d2, NT)
    own_largest, low_largest = own_ref[0, 0:1], low_ref[0, 0:1]
    largest = jnp.maximum(
        jnp.max(scores, axis=0, keepdims=True), jnp.maximum(own_largest, low_largest)
    )
    expsc = jnp.exp(scores - largest)
    own_part, low_part = jnp.exp(own_largest - largest), jnp.exp(low_largest - largest)
    total = (
        jnp.sum(expsc, axis=0, keepdims=True)
        + own_ref[0, 1:2] * own_part
        + low_ref[0, 1:2] * low_part
    )
    inner = (
        jnp.sum(expsc * dprobs, axis=0, keepdims=True)
        + own_ref[0, 2:3] * own_part
        + low_ref[0, 2:3] * low_part
    )
    share = 1.0 / total
    inner = inner * share
    out_ref[0, 0:1] = largest
    out_ref[0, 1:2] = share
    out_ref[0, 2:3] = inner
    probs = expsc * share
    dscores = (probs * (dprobs - inner)).astype(BF16)
    gk_ref[...] = dot(dscores, q2).astype(gk_ref.dtype)
    gv_ref[...] = dot(probs.astype(BF16), d2).astype(gv_ref.dtype)


def backward(q2, d2, k, v, stats_ref):
    scores = dot(k, q2, NT)
    dprobs = dot(v, d2, NT)
    probs = jnp.exp(scores - stats_ref[0, 0:1]) * stats_ref[0, 1:2]
    dscores = (probs * (dprobs - stats_ref[0, 2:3])).astype(BF16)
    weights = probs.astype(BF16)
    mixed_t = dot(v, weights, TN)
    gq_t = dot(k, dscores, TN)
    return weights, dscores, mixed_t, gq_t


def low_kernel(q_ref, do_ref, k_ref, v_ref, stats_ref, gk_ref, gv_ref, mixed_ref, gq_ref):
    q2 = two_heads(q_ref[...] * SCALE)
    d2 = two_heads(do_ref[...])
    weights, dscores, mixed_t, gq_t = backward(q2, d2, k_ref[...], v_ref[...], stats_ref)
    gk_ref[...] = dot(dscores, q2)
    gv_ref[...] = dot(weights, d2)
    mixed_ref[0] = mixed_t
    gq_ref[0] = gq_t


def own_kernel(
    q_ref, do_ref, k_ref, v_ref, tk_ref, tv_ref, stats_ref, low_mixed_ref, low_gq_ref,
    gk_ref, gv_ref, mixed_ref, gq_ref,
):
    q2 = two_heads(q_ref[...] * SCALE)
    d2 = two_heads(do_ref[...])
    weights, dscores, mixed_t, gq_t = backward(q2, d2, k_ref[...], v_ref[...], stats_ref)
    gk_ref[...] = dot(dscores, q2)
    gv_ref[...] = dot(weights, d2)
    unused_w, unused_d, top_mixed, top_gq = backward(q2, d2, tk_ref[...], tv_ref[...], stats_ref)

    def pick(both):
        return jnp.concatenate([both[:64, :TOK], both[64:, TOK:]], axis=0).T

    mixed_ref[...] = pick(mixed_t + top_mixed + low_mixed_ref[0]).astype(BF16)
    gq_ref[...] = pick((gq_t + top_gq + low_gq_ref[0]) * SCALE).astype(BF16)


def finish_kernel(table_ref, gk_ref, gv_ref, zero_ref, three_ref, keys_ref, values_ref):
    for half, (ref, out_ref) in enumerate(((gk_ref, keys_ref), (gv_ref, values_ref))):
        columns = slice(half * D, (half + 1) * D)
        rows = jnp.concatenate([zero_ref[:, columns], three_ref[:, columns].astype(F32)], axis=0)
        high = rows.astype(BF16)
        low = (rows - high.astype(F32)).astype(BF16)
        spread = dot(table_ref[...], high) + dot(table_ref[...], low)
        out_ref[...] = (ref[...] + spread).astype(BF16)


def rows_of_pair(rows, shift=0):
    return pl.BlockSpec((rows, LANES), lambda pair: (0, pair + shift))


def per_pair(rows, columns):
    return pl.BlockSpec((1, rows, columns), lambda pair: (pair, 0, 0))


STATS = jax.ShapeDtypeStruct((PAIRS, 8, 2 * TOK), F32)
STATS_SPEC = per_pair(8, 2 * TOK)
PARTIAL = jax.ShapeDtypeStruct((PAIRS, LANES, 2 * TOK), F32)
PARTIAL_SPEC = per_pair(LANES, 2 * TOK)
QUERY_SPECS = [rows_of_pair(TOK), rows_of_pair(TOK)]


def call(kernel, in_specs, out_specs, out_shape, flops, name):
    return pl.pallas_call(
        kernel,
        grid=(PAIRS,),
        in_specs=in_specs,
        out_specs=out_specs,
        out_shape=out_shape,
        compiler_params=pltpu.CompilerParams(vmem_limit_bytes=40 * 2**20),
        cost_estimate=pl.CostEstimate(flops=flops, bytes_accessed=2**20, transcendentals=0),
        name=name,
    )


def matmul_cost(keys, count):
    return 2 * count * keys * 2 * TOK * LANES * PAIRS


def own_stats(queries, cotangent, keys, values):
    return call(
        stats_kernel,
        QUERY_SPECS + [rows_of_pair(TOK), rows_of_pair(TOK)],
        STATS_SPEC, STATS, matmul_cost(TOK, 2), "own_stats",
    )(queries, cotangent, keys, values)


def low_stats(queries, cotangent, low):
    rows = low.shape[0]
    return call(
        stats_kernel,
        QUERY_SPECS + [rows_of_pair(rows), rows_of_pair(rows, PAIRS)],
        STATS_SPEC, STATS, matmul_cost(rows, 2), "low_stats",
    )(queries, cotangent, low, low)


def top_part(queries, cotangent, top, own, low):
    rows = top.shape[0]
    return call(
        top_kernel,
        QUERY_SPECS + [rows_of_pair(rows), rows_of_pair(rows, PAIRS), STATS_SPEC, STATS_SPEC],
        [rows_of_pair(rows), rows_of_pair(rows), STATS_SPEC],
        [jax.ShapeDtypeStruct((rows, D), BF16)] * 2 + [STATS],
        matmul_cost(rows, 4), "top_part",
    )(queries, cotangent, top, top, own, low)


def low_part(queries, cotangent, low, stats):
    rows = low.shape[0]
    return call(
        low_kernel,
        QUERY_SPECS + [rows_of_pair(rows), rows_of_pair(rows, PAIRS), STATS_SPEC],
        [rows_of_pair(rows), rows_of_pair(rows), PARTIAL_SPEC, PARTIAL_SPEC],
        [jax.ShapeDtypeStruct((rows, D), F32)] * 2 + [PARTIAL] * 2,
        matmul_cost(rows, 6), "low_part",
    )(queries, cotangent, low, low, stats)


def own_part(queries, cotangent, keys, values, top, stats, low_mixed, low_gq):
    rows = top.shape[0]
    return call(
        own_kernel,
        QUERY_SPECS
        + [rows_of_pair(TOK), rows_of_pair(TOK), rows_of_pair(rows), rows_of_pair(rows, PAIRS)]
        + [STATS_SPEC, PARTIAL_SPEC, PARTIAL_SPEC],
        [rows_of_pair(TOK)] * 4,
        [jax.ShapeDtypeStruct((TOK, D), F32)] * 2 + [jax.ShapeDtypeStruct((TOK, D), BF16)] * 2,
        matmul_cost(TOK, 6) + matmul_cost(rows, 4), "own_part",
    )(queries, cotangent, keys, values, top, top, stats, low_mixed, low_gq)


def whole(kernel, out_shape, name):
    return pl.pallas_call(kernel, out_shape=out_shape, name=name)


def halves(rows, parts=1):
    count, width = rows.shape
    split = rows.reshape(parts, 2, count // (2 * parts), width).astype(F32)
    return (0.5 * (split[:, 0] + split[:, 1])).astype(BF16).reshape(count // 2, width)


def spread(gradient, parts=1):
    count, width = gradient.shape
    split = (0.5 * gradient).reshape(parts, 1, count // parts, width)
    return jnp.concatenate([split, split], axis=1).reshape(2 * count, width)


def joined(*blocks):
    return jnp.concatenate(blocks, axis=0)


def shards(queries, keys, values, cotangent):
    pooling = token_pooling()
    grouping = group_pooling()
    wide = lambda rows: jax.ShapeDtypeStruct((rows, 2 * D), BF16)

    zero, one, three = whole(pool_kernel, [wide(64), wide(32), wide(8)], "pool")(
        jnp.asarray(pooling, BF16), keys, values
    )
    far = flip(three, "lo", 8)
    sec0 = flip(zero, "lo", 1)
    far_pair = joined(far, flip(far, "lo", 1))
    own = own_stats(queries, cotangent, keys, values)
    level1 = joined(one, halves(sec0))
    level2 = halves(level1, 2)
    short = joined(level2, far_pair)
    x1 = flip(joined(level1, far_pair), "lo", 2)
    x2 = flip(short, "lo", 4)
    x3 = flip(short, "lo", 6)
    sec3 = joined(far_pair, x1[64:], x2[32:], x3[32:])
    level4 = dot(
        jnp.asarray(grouping, BF16), joined(level2, x1[:64], x2[:32], x3[:32], sec3)
    ).astype(BF16)
    level5 = halves(level4)
    y1 = flip(level4, "hi", 1)
    y2 = flip(level5, "hi", 2)
    y3 = flip(level5, "hi", 3)
    level6 = joined(halves(level5), halves(halves(y1)), halves(y2), halves(y3))
    level7 = halves(level6, 4)
    low = joined(sec0, x1[:64], x2[:32], x3[:32], sec3, y1, y2, y3)
    z1 = flip(level6, "hi", 4)
    z2 = flip(level7, "hi", 8)
    z3 = flip(level7, "hi", 12)
    low_stat = low_stats(queries, cotangent, low)
    top = joined(z1, z2, z3)

    top_gk, top_gv, stats = top_part(queries, cotangent, top, own, low_stat)
    top_g = jnp.concatenate([top_gk, top_gv], axis=1)
    b1 = flip(top_g[:64], "hi", 4)
    b2 = flip(top_g[64:96], "hi", 8)
    b3 = flip(top_g[96:], "hi", 12)
    low_gk, low_gv, low_mixed, low_gq = low_part(queries, cotangent, low, stats)
    low_g = jnp.concatenate([low_gk, low_gv], axis=1)
    g6 = b1.astype(F32) + spread(b2.astype(F32) + b3.astype(F32), 4)
    b1 = flip((low_g[256:320] + spread(spread(g6[16:32]))).astype(BF16), "hi", 1)
    b2 = flip((low_g[320:352] + spread(g6[32:48])).astype(BF16), "hi", 2)
    b3 = flip((low_g[352:384] + spread(g6[48:64])).astype(BF16), "hi", 3)
    g5 = spread(g6[:16]) + b2.astype(F32) + b3.astype(F32)
    g4 = b1.astype(F32) + spread(g5)
    own_gk, own_gv, mixed, grad_queries = own_part(
        queries, cotangent, keys, values, top, stats, low_mixed, low_gq
    )
    g = dot(jnp.asarray(grouping.T, BF16), g4.astype(BF16))
    g3 = low_g[192:256] + g[160:224]
    b1 = flip(joined(low_g[64:128] + g[32:96], g3[16:32]).astype(BF16), "lo", 2)
    b2 = flip(joined(low_g[128:160] + g[96:128], g3[32:48]).astype(BF16), "lo", 4)
    b3 = flip(joined(low_g[160:192] + g[128:160], g3[48:64]).astype(BF16), "lo", 6)
    b1, b2, b3 = b1.astype(F32), b2.astype(F32), b3.astype(F32)
    g2 = g[:32] + b2[:32] + b3[:32]
    far_g = g3[:16] + b1[64:] + b2[32:] + b3[32:]
    g1 = b1[:64] + spread(g2, 2)
    back = flip(joined(low_g[:64] + spread(g1[32:]), far_g[8:]).astype(BF16), "lo", 1).astype(F32)
    g0 = back[:64] + spread(g1[:32])
    last = flip((far_g[:8] + back[64:]).astype(BF16), "lo", 8)
    unpool = np.concatenate([pooling[:64], pooling[96:]], axis=0).T
    grad_keys, grad_values = whole(
        finish_kernel, [jax.ShapeDtypeStruct((TOK, D), BF16)] * 2, "finish"
    )(jnp.asarray(unpool, BF16), own_gk, own_gv, g0, last)
    return (mixed, grad_queries, grad_keys, grad_values)


def solution(mesh):
    spec = P(("hi", "lo"), None)
    return jax.shard_map(
        shards, mesh=mesh, in_specs=(spec,) * 4, out_specs=(spec,) * 4, check_vma=False
    )
```

profile of v0, /device:TPU:1, one launch (start us, length us, event | category | flops | bytes accessed | tf_op | source)
XLA Modules:
  0.0 96.4 jit_solution(13980956471118054955)
XLA Ops:
  0.6 1.9 %pool.1 = (bf16[64,1024]{1,0:T(8,128)(2,1)}, bf16[32,1024]{1,0:T(8,128)(2,1)}, bf16[8,1024]{1,0:T(8,128)(2,1)}) custom-call(bf16[104,256]{1,0:T(8,128)(2,1)} %constant.6.clone.table_ref, bf16[256,512]{1,0:T(8,128)(2,1)} %k_ref.3, bf16[256,512]{1,0:T(8,128)(2,1)} %v_ref.3), custom_call_target="tpu_custom_call" | custom-call | tf_op jit(solution)/shard_map/pool/pallas_call | solution.py:280
  2.6 7.7 %collective-permute-start.1 = (bf16[8,1024]{1,0:T(8,128)(2,1)}, bf16[8,1024]{1,0:T(8,128)(2,1)S(1)}, u32[]{:S(2)}, u32[]{:S(2)}) collective-permute-start(bf16[8,1024]{1,0:T(8,128)(2,1)} %get-tuple-element.22), channel_id=1, source_target_pairs={{0,128},{16,144},{32,160},{48,176},{64,192},{80,208},{96,224},{112... | collective-permute-start | bytes 49160 | tf_op jit(solution)/shard_map/ppermute | solution.py:23
  10.3 1.0 collective-permute-start
  11.3 0.9 copy-done
  12.2 0.9 copy-done.2
  13.2 0.9 copy-done.4
  14.1 0.9 copy-done.5
  15.1 1.7 %own_stats.1.own_ref = f32[4,8,512]{2,1,0:T(8,128)S(1)} custom-call(bf16[256,512]{1,0:T(8,128)(2,1)S(1)} %copy-done, bf16[256,512]{1,0:T(8,128)(2,1)S(1)} %copy-done.2, bf16[256,512]{1,0:T(8,128)(2,1)S(1)} %copy-done.4, bf16[256,512]{1,0:T(8,128)(2,1)S(1)} %copy-done.5), custom_call_target="tpu_custom_call" | custom-call | flops 268435456 | bytes 1048576 | tf_op jit(solution)/shard_map/own_stats/pallas_call | solution.py:204
  17.3 0.8 collective-permute-done.2
  18.1 2.6 %collective-permute-start.5 = (bf16[48,1024]{1,0:T(8,128)(2,1)S(1)}, bf16[48,1024]{1,0:T(8,128)(2,1)S(1)}, u32[]{:S(2)}, u32[]{:S(2)}) collective-permute-start(bf16[48,1024]{1,0:T(8,128)(2,1)S(1)} %pad_maximum_fusion.14), channel_id=1, source_target_pairs={{0,96},{16,112},{32,64},{48,80},{64,32},{80,48},{96,0},{112,16},{1... | collective-permute-start | bytes 294920 | tf_op jit(solution)/shard_map/ppermute | solution.py:23
  20.7 0.5 collective-permute-start.4
  21.8 2.8 %collective-permute-done.5 = bf16[48,1024]{1,0:T(8,128)(2,1)S(1)} collective-permute-done((bf16[48,1024]{1,0:T(8,128)(2,1)S(1)}, bf16[48,1024]{1,0:T(8,128)(2,1)S(1)}, u32[]{:S(2)}, u32[]{:S(2)}) %collective-permute-start.5) | collective-permute-done | bytes 98336 | tf_op jit(solution)/shard_map/ppermute | solution.py:23
  24.9 1.2 %collective-permute-done.4 = bf16[48,1024]{1,0:T(8,128)(2,1)S(1)} collective-permute-done((bf16[48,1024]{1,0:T(8,128)(2,1)S(1)}, bf16[48,1024]{1,0:T(8,128)(2,1)S(1)}, u32[]{:S(2)}, u32[]{:S(2)}) %collective-permute-start.4) | collective-permute-done | bytes 98336 | tf_op jit(solution)/shard_map/ppermute | solution.py:23
  26.5 1.1 %collective-permute-done.3 = bf16[80,1024]{1,0:T(8,128)(2,1)S(1)} collective-permute-done((bf16[80,1024]{1,0:T(8,128)(2,1)S(1)}, bf16[80,1024]{1,0:T(8,128)(2,1)S(1)}, u32[]{:S(2)}, u32[]{:S(2)}) %collective-permute-start.3) | collective-permute-done | bytes 163872 | tf_op jit(solution)/shard_map/ppermute | solution.py:23
  28.1 3.0 %collective-permute-start.7 = (bf16[32,1024]{1,0:T(8,128)(2,1)S(1)}, bf16[32,1024]{1,0:T(8,128)(2,1)S(1)}, u32[]{:S(2)}, u32[]{:S(2)}) collective-permute-start(bf16[32,1024]{1,0:T(8,128)(2,1)S(1)} %fusion.81), channel_id=1, source_target_pairs={{0,2},{1,3},{2,0},{3,1},{4,6},{5,7},{6,4},{7,5},{8,10},{9,11},{10,... | collective-permute-start | bytes 196616 | tf_op jit(solution)/shard_map/ppermute | solution.py:23
  31.1 0.8 collective-permute-start.8
  32.1 0.7 collective-permute-done.7
  32.8 2.6 %collective-permute-done.8 = bf16[32,1024]{1,0:T(8,128)(2,1)S(1)} collective-permute-done((bf16[32,1024]{1,0:T(8,128)(2,1)S(1)}, bf16[32,1024]{1,0:T(8,128)(2,1)S(1)}, u32[]{:S(2)}, u32[]{:S(2)}) %collective-permute-start.8) | collective-permute-done | bytes 65568 | tf_op jit(solution)/shard_map/ppermute | solution.py:23
  35.5 0.7 collective-permute-done.6
  36.3 0.8 collective-permute-start.9
  37.2 1.3 %collective-permute-start.10 = (bf16[32,1024]{1,0:T(8,128)(2,1)S(1)}, bf16[32,1024]{1,0:T(8,128)(2,1)S(1)}, u32[]{:S(2)}, u32[]{:S(2)}) collective-permute-start(bf16[32,1024]{1,0:T(8,128)(2,1)S(1)} %fusion.33), channel_id=1, source_target_pairs={{0,8},{1,9},{2,10},{3,11},{4,12},{5,13},{6,14},{7,15},{8,0},{9,1},... | collective-permute-start | bytes 196616 | tf_op jit(solution)/shard_map/ppermute | solution.py:23
  38.6 1.6 %collective-permute-start.11 = (bf16[32,1024]{1,0:T(8,128)(2,1)S(1)}, bf16[32,1024]{1,0:T(8,128)(2,1)S(1)}, u32[]{:S(2)}, u32[]{:S(2)}) collective-permute-start(bf16[32,1024]{1,0:T(8,128)(2,1)S(1)} %fusion.33), channel_id=1, source_target_pairs={{0,12},{1,13},{2,14},{3,15},{4,8},{5,9},{6,10},{7,11},{8,4},{9,5},... | collective-permute-start | bytes 196616 | tf_op jit(solution)/shard_map/ppermute | solution.py:23
  40.2 2.2 %low_stats.1.low_ref = f32[4,8,512]{2,1,0:T(8,128)S(1)} custom-call(bf16[256,512]{1,0:T(8,128)(2,1)S(1)} %copy-done, bf16[256,512]{1,0:T(8,128)(2,1)S(1)} %copy-done.2, bf16[384,1024]{1,0:T(8,128)(2,1)S(1)} %constant_dynamic-update-slice_fusion.3.k_ref.v_ref, bf16[384,1024]{1,0:T(8,128)(2,1)S(1)} %constant_dynamic-update-slice_fusion.3.k_ref.v_ref), custom_call_target="tpu_custom_call" | custom-call | flops 402653184 | bytes 1048576 | tf_op jit(solution)/shard_map/low_stats/pallas_call | solution.py:213
  42.4 1.7 %collective-permute-done.11 = bf16[32,1024]{1,0:T(8,128)(2,1)S(1)} collective-permute-done((bf16[32,1024]{1,0:T(8,128)(2,1)S(1)}, bf16[32,1024]{1,0:T(8,128)(2,1)S(1)}, u32[]{:S(2)}, u32[]{:S(2)}) %collective-permute-start.11) | collective-permute-done | bytes 65568 | tf_op jit(solution)/shard_map/ppermute | solution.py:23
  44.2 2.3 %top_part.1 = (bf16[128,512]{1,0:T(8,128)(2,1)S(1)}, bf16[128,512]{1,0:T(8,128)(2,1)S(1)}, f32[4,8,512]{2,1,0:T(8,128)S(1)}) custom-call(bf16[256,512]{1,0:T(8,128)(2,1)S(1)} %copy-done.1, bf16[256,512]{1,0:T(8,128)(2,1)S(1)} %copy-done.3, bf16[128,1024]{1,0:T(8,128)(2,1)S(1)} %constant_dynamic-update-slice_fusion.k_ref.v_ref.tk_ref.tv_ref, ...), custom_call_target="tpu_custom_call" | custom-call | flops 268435456 | bytes 1048576 | tf_op jit(solution)/shard_map/top_part/pallas_call | solution.py:222
  46.6 3.5 %low_part.1 = (f32[384,512]{1,0:T(8,128)S(1)}, f32[384,512]{1,0:T(8,128)S(1)}, f32[4,128,512]{2,1,0:T(8,128)S(1)}, f32[4,128,512]{2,1,0:T(8,128)S(1)}) custom-call(bf16[256,512]{1,0:T(8,128)(2,1)S(1)} %copy-done.1, bf16[256,512]{1,0:T(8,128)(2,1)S(1)} %copy-done.3, bf16[384,1024]{1,0:T(8,128)(2,1)S(1)} %constant_dynamic-update-slice_fusion.3.k_ref.v_ref, ...), custom_call_target="tpu_custom_call" | custom-call | flops 1207959552 | bytes 1048576 | tf_op jit(solution)/shard_map/low_part/pallas_call | solution.py:233
  50.1 1.7 %collective-permute-start.14 = (bf16[32,1024]{1,0:T(8,128)(2,1)S(1)}, bf16[32,1024]{1,0:T(8,128)(2,1)S(1)}, u32[]{:S(2)}, u32[]{:S(2)}) collective-permute-start(bf16[32,1024]{1,0:T(8,128)(2,1)S(1)} %get-tuple-element.50), channel_id=1, source_target_pairs={{0,12},{1,13},{2,14},{3,15},{4,8},{5,9},{6,10},{7,11},{8,4},{9,5},... | collective-permute-start | bytes 196616 | tf_op jit(solution)/shard_map/ppermute | solution.py:23
  51.8 2.0 %collective-permute-start.12 = (bf16[64,1024]{1,0:T(8,128)(2,1)S(1)}, bf16[64,1024]{1,0:T(8,128)(2,1)S(1)}, u32[]{:S(2)}, u32[]{:S(2)}) collective-permute-start(bf16[64,1024]{1,0:T(8,128)(2,1)S(1)} %slice.283), channel_id=1, source_target_pairs={{0,4},{1,5},{2,6},{3,7},{4,0},{5,1},{6,2},{7,3},{8,12},{9,13},{10,... | collective-permute-start | bytes 393224 | tf_op jit(solution)/shard_map/ppermute | solution.py:23
  53.8 1.3 %collective-permute-done.14 = bf16[32,1024]{1,0:T(8,128)(2,1)S(1)} collective-permute-done((bf16[32,1024]{1,0:T(8,128)(2,1)S(1)}, bf16[32,1024]{1,0:T(8,128)(2,1)S(1)}, u32[]{:S(2)}, u32[]{:S(2)}) %collective-permute-start.14) | collective-permute-done | bytes 65568 | tf_op jit(solution)/shard_map/ppermute | solution.py:23
  55.1 2.0 %collective-permute-done.13 = bf16[32,1024]{1,0:T(8,128)(2,1)S(1)} collective-permute-done((bf16[32,1024]{1,0:T(8,128)(2,1)S(1)}, bf16[32,1024]{1,0:T(8,128)(2,1)S(1)}, u32[]{:S(2)}, u32[]{:S(2)}) %collective-permute-start.13) | collective-permute-done | bytes 65568 | tf_op jit(solution)/shard_map/ppermute | solution.py:23
  57.3 1.9 %collective-permute-start.17 = (bf16[32,1024]{1,0:T(8,128)(2,1)S(1)}, bf16[32,1024]{1,0:T(8,128)(2,1)S(1)}, u32[]{:S(2)}, u32[]{:S(2)}) collective-permute-start(bf16[32,1024]{1,0:T(8,128)(2,1)S(1)} %get-tuple-element.42), channel_id=1, source_target_pairs={{0,3},{1,2},{2,1},{3,0},{4,7},{5,6},{6,5},{7,4},{8,11},{9,10},{10,... | collective-permute-start | bytes 196616 | tf_op jit(solution)/shard_map/ppermute | solution.py:23
  59.2 0.6 collective-permute-start.16
  59.9 1.1 %collective-permute-start.15 = (bf16[64,1024]{1,0:T(8,128)(2,1)S(1)}, bf16[64,1024]{1,0:T(8,128)(2,1)S(1)}, u32[]{:S(2)}, u32[]{:S(2)}) collective-permute-start(bf16[64,1024]{1,0:T(8,128)(2,1)S(1)} %fusion.8), channel_id=1, source_target_pairs={{0,1},{1,0},{2,3},{3,2},{4,5},{5,4},{6,7},{7,6},{8,9},{9,8},{10,11... | collective-permute-start | bytes 393224 | tf_op jit(solution)/shard_map/ppermute | solution.py:23
  61.0 0.9 collective-permute-done.17
  61.9 1.9 %collective-permute-done.16 = bf16[32,1024]{1,0:T(8,128)(2,1)S(1)} collective-permute-done((bf16[32,1024]{1,0:T(8,128)(2,1)S(1)}, bf16[32,1024]{1,0:T(8,128)(2,1)S(1)}, u32[]{:S(2)}, u32[]{:S(2)}) %collective-permute-start.16) | collective-permute-done | bytes 65568 | tf_op jit(solution)/shard_map/ppermute | solution.py:23
  64.4 2.5 %collective-permute-start.20 = (bf16[48,1024]{1,0:T(8,128)(2,1)S(1)}, bf16[48,1024]{1,0:T(8,128)(2,1)S(1)}, u32[]{:S(2)}, u32[]{:S(2)}) collective-permute-start(bf16[48,1024]{1,0:T(8,128)(2,1)S(1)} %pad_maximum_fusion.16), channel_id=1, source_target_pairs={{0,96},{16,112},{32,64},{48,80},{64,32},{80,48},{96,0},{112,16},{1... | collective-permute-start | bytes 294920 | tf_op jit(solution)/shard_map/ppermute | solution.py:23
  66.9 0.7 collective-permute-start.19
  67.9 1.6 %collective-permute-done.20 = bf16[48,1024]{1,0:T(8,128)(2,1)S(1)} collective-permute-done((bf16[48,1024]{1,0:T(8,128)(2,1)S(1)}, bf16[48,1024]{1,0:T(8,128)(2,1)S(1)}, u32[]{:S(2)}, u32[]{:S(2)}) %collective-permute-start.20) | collective-permute-done | bytes 98336 | tf_op jit(solution)/shard_map/ppermute | solution.py:23
  69.5 2.4 %collective-permute-done.19 = bf16[48,1024]{1,0:T(8,128)(2,1)S(1)} collective-permute-done((bf16[48,1024]{1,0:T(8,128)(2,1)S(1)}, bf16[48,1024]{1,0:T(8,128)(2,1)S(1)}, u32[]{:S(2)}, u32[]{:S(2)}) %collective-permute-start.19) | collective-permute-done | bytes 98336 | tf_op jit(solution)/shard_map/ppermute | solution.py:23
  72.3 7.9 %collective-permute-start.21 = (bf16[72,1024]{1,0:T(8,128)(2,1)S(1)}, bf16[72,1024]{1,0:T(8,128)(2,1)S(1)}, u32[]{:S(2)}, u32[]{:S(2)}) collective-permute-start(bf16[72,1024]{1,0:T(8,128)(2,1)S(1)} %pad_maximum_fusion.8), channel_id=1, source_target_pairs={{0,16},{16,0},{32,48},{48,32},{64,80},{80,64},{96,112},{112,96},{1... | collective-permute-start | bytes 442376 | tf_op jit(solution)/shard_map/ppermute | solution.py:23
  80.2 4.9 %own_part.1 = (f32[256,512]{1,0:T(8,128)S(1)}, f32[256,512]{1,0:T(8,128)S(1)}, bf16[256,512]{1,0:T(8,128)(2,1)}, bf16[256,512]{1,0:T(8,128)(2,1)}) custom-call(bf16[256,512]{1,0:T(8,128)(2,1)S(1)} %copy-done.1, bf16[256,512]{1,0:T(8,128)(2,1)S(1)} %copy-done.3, bf16[256,512]{1,0:T(8,128)(2,1)S(1)} %copy-done.4, bf16[256,512]{1,0:T(8,128)(2,1)S(1)} %copy-done.5, ...), custom_call_target="tpu_custom_call" | custom-call | flops 1073741824 | bytes 1048576 | tf_op jit(solution)/shard_map/own_part/pallas_call | solution.py:244
  85.1 0.8 copy-done.6
  85.9 0.8 copy-done.7
  86.8 1.6 %collective-permute-start.22 = (bf16[8,1024]{1,0:T(8,128)(2,1)S(1)}, bf16[8,1024]{1,0:T(8,128)(2,1)S(1)}, u32[]{:S(2)}, u32[]{:S(2)}) collective-permute-start(bf16[8,1024]{1,0:T(8,128)(2,1)S(1)} %fusion.54), channel_id=1, source_target_pairs={{0,128},{16,144},{32,160},{48,176},{64,192},{80,208},{96,224},{112... | collective-permute-start | bytes 49160 | tf_op jit(solution)/shard_map/ppermute | solution.py:23
  88.4 0.7 slice_add_fusion.zero_ref
  89.2 4.2 %collective-permute-done.22.three_ref = bf16[8,1024]{1,0:T(8,128)(2,1)S(1)} collective-permute-done((bf16[8,1024]{1,0:T(8,128)(2,1)S(1)}, bf16[8,1024]{1,0:T(8,128)(2,1)S(1)}, u32[]{:S(2)}, u32[]{:S(2)}) %collective-permute-start.22) | collective-permute-done | bytes 16416 | tf_op jit(solution)/shard_map/ppermute | solution.py:23
  93.4 0.6 copy-done.12
  94.0 2.4 %finish.1 = (bf16[256,512]{1,0:T(8,128)(2,1)}, bf16[256,512]{1,0:T(8,128)(2,1)}) custom-call(bf16[256,72]{1,0:T(8,128)(2,1)} %constant.9.clone.table_ref, f32[256,512]{1,0:T(8,128)} %copy-done.6, f32[256,512]{1,0:T(8,128)} %copy-done.7, f32[64,1024]{1,0:T(8,128)} %slice_add_fusion.zero_ref, bf16[8,1024]{1,0:T(8,128)(2,1)} %copy-done.12), custom_call_target="tpu_custom_call" | custom-call | tf_op jit(solution)/shard_map/finish/pallas_call | solution.py:339
  (135 shorter events, 4.0 us)
Async XLA Ops:
  0.6 16.3 %copy-start.16 = (bf16[64,8]{1,0:T(8,128)(2,1)S(1)}, bf16[64,8]{1,0:T(8,128)(2,1)}, u32[]{:S(2)}) copy-start(bf16[64,8]{1,0:T(8,128)(2,1)} %constant.23) | copy-start | bytes 3076
  2.6 14.2 %collective-permute-start.1 = (bf16[8,1024]{1,0:T(8,128)(2,1)}, bf16[8,1024]{1,0:T(8,128)(2,1)S(1)}, u32[]{:S(2)}, u32[]{:S(2)}) collective-permute-start(bf16[8,1024]{1,0:T(8,128)(2,1)} %get-tuple-element.22), channel_id=1, source_target_pairs={{0,128},{16,144},{32,160},{48,176},{64,192},{80,208},{96,224},{112... | collective-permute-start | bytes 49160 | tf_op jit(solution)/shard_map/ppermute | solution.py:23
  10.3 6.8 %collective-permute-start = (bf16[64,1024]{1,0:T(8,128)(2,1)}, bf16[64,1024]{1,0:T(8,128)(2,1)S(1)}, u32[]{:S(2)}, u32[]{:S(2)}) collective-permute-start(bf16[64,1024]{1,0:T(8,128)(2,1)} %get-tuple-element.21), channel_id=1, source_target_pairs={{0,16},{16,0},{32,48},{48,32},{64,80},{80,64},{96,112},{112,96},{1... | collective-permute-start | bytes 393224 | tf_op jit(solution)/shard_map/ppermute | solution.py:23
  11.3 0.9 copy-start
  12.2 0.9 copy-start.2
  13.2 0.9 copy-start.4
  14.1 0.9 copy-start.5
  15.1 2.1 %copy-start.8 = (bf16[32,1024]{1,0:T(8,128)(2,1)S(1)}, bf16[32,1024]{1,0:T(8,128)(2,1)}, u32[]{:S(2)}) copy-start(bf16[32,1024]{1,0:T(8,128)(2,1)} %get-tuple-element.20) | copy-start | bytes 196612
  15.1 6.5 %copy-start.19 = (bf16[64,32]{1,0:T(8,128)(2,1)S(1)}, bf16[64,32]{1,0:T(8,128)(2,1)}, u32[]{:S(2)}) copy-start(bf16[64,32]{1,0:T(8,128)(2,1)} %constant.4) | copy-start | bytes 12292
  16.8 7.8 %copy-start.18 = (bf16[64,32]{1,0:T(8,128)(2,1)S(1)}, bf16[64,32]{1,0:T(8,128)(2,1)}, u32[]{:S(2)}) copy-start(bf16[64,32]{1,0:T(8,128)(2,1)} %constant.22) | copy-start | bytes 12292
  16.8 1.3 %collective-permute-start.2 = (bf16[8,1024]{1,0:T(8,128)(2,1)S(1)}, bf16[8,1024]{1,0:T(8,128)(2,1)S(1)}, u32[]{:S(2)}, u32[]{:S(2)}) collective-permute-start(bf16[8,1024]{1,0:T(8,128)(2,1)S(1)} %collective-permute-done.1), channel_id=1, source_target_pairs={{0,16},{16,0},{32,48},{48,32},{64,80},{80,64},{96,112},{112,96},{1... | collective-permute-start | bytes 49160 | tf_op jit(solution)/shard_map/ppermute | solution.py:23
  17.1 7.6 %copy-start.15 = (bf16[64,16]{1,0:T(8,128)(2,1)S(1)}, bf16[64,16]{1,0:T(8,128)(2,1)}, u32[]{:S(2)}) copy-start(bf16[64,16]{1,0:T(8,128)(2,1)} %constant.27) | copy-start | bytes 6148
  17.2 9.0 %copy-start.17 = (bf16[64,32]{1,0:T(8,128)(2,1)S(1)}, bf16[64,32]{1,0:T(8,128)(2,1)}, u32[]{:S(2)}) copy-start(bf16[64,32]{1,0:T(8,128)(2,1)} %constant.21) | copy-start | bytes 12292
  17.2 9.1 %copy-start.14 = (bf16[64,16]{1,0:T(8,128)(2,1)S(1)}, bf16[64,16]{1,0:T(8,128)(2,1)}, u32[]{:S(2)}) copy-start(bf16[64,16]{1,0:T(8,128)(2,1)} %constant.26) | copy-start | bytes 6148
  17.2 10.3 %copy-start.13 = (bf16[64,16]{1,0:T(8,128)(2,1)S(1)}, bf16[64,16]{1,0:T(8,128)(2,1)}, u32[]{:S(2)}) copy-start(bf16[64,16]{1,0:T(8,128)(2,1)} %constant.25) | copy-start | bytes 6148
  17.3 10.4 %copy-start.11 = (bf16[64,64]{1,0:T(8,128)(2,1)S(1)}, bf16[64,64]{1,0:T(8,128)(2,1)}, u32[]{:S(2)}) copy-start(bf16[64,64]{1,0:T(8,128)(2,1)} %constant.20) | copy-start | bytes 24580
  18.1 6.4 %collective-permute-start.5 = (bf16[48,1024]{1,0:T(8,128)(2,1)S(1)}, bf16[48,1024]{1,0:T(8,128)(2,1)S(1)}, u32[]{:S(2)}, u32[]{:S(2)}) collective-permute-start(bf16[48,1024]{1,0:T(8,128)(2,1)S(1)} %pad_maximum_fusion.14), channel_id=1, source_target_pairs={{0,96},{16,112},{32,64},{48,80},{64,32},{80,48},{96,0},{112,16},{1... | collective-permute-start | bytes 294920 | tf_op jit(solution)/shard_map/ppermute | solution.py:23
  20.7 5.4 %collective-permute-start.4 = (bf16[48,1024]{1,0:T(8,128)(2,1)S(1)}, bf16[48,1024]{1,0:T(8,128)(2,1)S(1)}, u32[]{:S(2)}, u32[]{:S(2)}) collective-permute-start(bf16[48,1024]{1,0:T(8,128)(2,1)S(1)} %pad_maximum_fusion.14), channel_id=1, source_target_pairs={{0,64},{16,80},{32,96},{48,112},{64,0},{80,16},{96,32},{112,48},{1... | collective-permute-start | bytes 294920 | tf_op jit(solution)/shard_map/ppermute | solution.py:23
  21.2 6.3 %collective-permute-start.3 = (bf16[80,1024]{1,0:T(8,128)(2,1)S(1)}, bf16[80,1024]{1,0:T(8,128)(2,1)S(1)}, u32[]{:S(2)}, u32[]{:S(2)}) collective-permute-start(bf16[80,1024]{1,0:T(8,128)(2,1)S(1)} %pad_maximum_fusion.6), channel_id=1, source_target_pairs={{0,32},{16,48},{32,0},{48,16},{64,96},{80,112},{96,64},{112,80},{1... | collective-permute-start | bytes 491528 | tf_op jit(solution)/shard_map/ppermute | solution.py:23
  21.7 6.1 %copy-start.10 = (bf16[64,8]{1,0:T(8,128)(2,1)S(1)}, bf16[64,8]{1,0:T(8,128)(2,1)}, u32[]{:S(2)}) copy-start(bf16[64,8]{1,0:T(8,128)(2,1)} %constant.24) | copy-start | bytes 3076
  28.1 4.7 %collective-permute-start.7 = (bf16[32,1024]{1,0:T(8,128)(2,1)S(1)}, bf16[32,1024]{1,0:T(8,128)(2,1)S(1)}, u32[]{:S(2)}, u32[]{:S(2)}) collective-permute-start(bf16[32,1024]{1,0:T(8,128)(2,1)S(1)} %fusion.81), channel_id=1, source_target_pairs={{0,2},{1,3},{2,0},{3,1},{4,6},{5,7},{6,4},{7,5},{8,10},{9,11},{10,... | collective-permute-start | bytes 196616 | tf_op jit(solution)/shard_map/ppermute | solution.py:23
  31.1 4.3 %collective-permute-start.8 = (bf16[32,1024]{1,0:T(8,128)(2,1)S(1)}, bf16[32,1024]{1,0:T(8,128)(2,1)S(1)}, u32[]{:S(2)}, u32[]{:S(2)}) collective-permute-start(bf16[32,1024]{1,0:T(8,128)(2,1)S(1)} %fusion.81), channel_id=1, source_target_pairs={{0,3},{1,2},{2,1},{3,0},{4,7},{5,6},{6,5},{7,4},{8,11},{9,10},{10,... | collective-permute-start | bytes 196616 | tf_op jit(solution)/shard_map/ppermute | solution.py:23
  31.9 4.3 %collective-permute-start.6 = (bf16[64,1024]{1,0:T(8,128)(2,1)S(1)}, bf16[64,1024]{1,0:T(8,128)(2,1)S(1)}, u32[]{:S(2)}, u32[]{:S(2)}) collective-permute-start(bf16[64,1024]{1,0:T(8,128)(2,1)S(1)} %bitcast.109), channel_id=1, source_target_pairs={{0,1},{1,0},{2,3},{3,2},{4,5},{5,4},{6,7},{7,6},{8,9},{9,8},{10,11... | collective-permute-start | bytes 393224 | tf_op jit(solution)/shard_map/ppermute | solution.py:23
  36.3 6.0 %collective-permute-start.9 = (bf16[64,1024]{1,0:T(8,128)(2,1)S(1)}, bf16[64,1024]{1,0:T(8,128)(2,1)S(1)}, u32[]{:S(2)}, u32[]{:S(2)}) collective-permute-start(bf16[64,1024]{1,0:T(8,128)(2,1)S(1)} %pad_maximum_fusion.10), channel_id=1, source_target_pairs={{0,4},{1,5},{2,6},{3,7},{4,0},{5,1},{6,2},{7,3},{8,12},{9,13},{10,... | collective-permute-start | bytes 393224 | tf_op jit(solution)/shard_map/ppermute | solution.py:23
  37.2 7.0 %copy-start.1 = (bf16[256,512]{1,0:T(8,128)(2,1)S(1)}, bf16[256,512]{1,0:T(8,128)(2,1)}, u32[]{:S(2)}) copy-start(bf16[256,512]{1,0:T(8,128)(2,1)} %q_ref.9) | copy-start | bytes 786436
  37.2 6.9 %copy-start.3 = (bf16[256,512]{1,0:T(8,128)(2,1)S(1)}, bf16[256,512]{1,0:T(8,128)(2,1)}, u32[]{:S(2)}) copy-start(bf16[256,512]{1,0:T(8,128)(2,1)} %do_ref.9) | copy-start | bytes 786436
  37.2 5.2 %collective-permute-start.10 = (bf16[32,1024]{1,0:T(8,128)(2,1)S(1)}, bf16[32,1024]{1,0:T(8,128)(2,1)S(1)}, u32[]{:S(2)}, u32[]{:S(2)}) collective-permute-start(bf16[32,1024]{1,0:T(8,128)(2,1)S(1)} %fusion.33), channel_id=1, source_target_pairs={{0,8},{1,9},{2,10},{3,11},{4,12},{5,13},{6,14},{7,15},{8,0},{9,1},... | collective-permute-start | bytes 196616 | tf_op jit(solution)/shard_map/ppermute | solution.py:23
  38.6 5.6 %collective-permute-start.11 = (bf16[32,1024]{1,0:T(8,128)(2,1)S(1)}, bf16[32,1024]{1,0:T(8,128)(2,1)S(1)}, u32[]{:S(2)}, u32[]{:S(2)}) collective-permute-start(bf16[32,1024]{1,0:T(8,128)(2,1)S(1)} %fusion.33), channel_id=1, source_target_pairs={{0,12},{1,13},{2,14},{3,15},{4,8},{5,9},{6,10},{7,11},{8,4},{9,5},... | collective-permute-start | bytes 196616 | tf_op jit(solution)/shard_map/ppermute | solution.py:23
  50.1 5.0 %collective-permute-start.14 = (bf16[32,1024]{1,0:T(8,128)(2,1)S(1)}, bf16[32,1024]{1,0:T(8,128)(2,1)S(1)}, u32[]{:S(2)}, u32[]{:S(2)}) collective-permute-start(bf16[32,1024]{1,0:T(8,128)(2,1)S(1)} %get-tuple-element.50), channel_id=1, source_target_pairs={{0,12},{1,13},{2,14},{3,15},{4,8},{5,9},{6,10},{7,11},{8,4},{9,5},... | collective-permute-start | bytes 196616 | tf_op jit(solution)/shard_map/ppermute | solution.py:23
  51.8 5.3 %collective-permute-start.13 = (bf16[32,1024]{1,0:T(8,128)(2,1)S(1)}, bf16[32,1024]{1,0:T(8,128)(2,1)S(1)}, u32[]{:S(2)}, u32[]{:S(2)}) collective-permute-start(bf16[32,1024]{1,0:T(8,128)(2,1)S(1)} %get-tuple-element.49), channel_id=1, source_target_pairs={{0,8},{1,9},{2,10},{3,11},{4,12},{5,13},{6,14},{7,15},{8,0},{9,1},... | collective-permute-start | bytes 196616 | tf_op jit(solution)/shard_map/ppermute | solution.py:23
  51.8 5.4 %collective-permute-start.12 = (bf16[64,1024]{1,0:T(8,128)(2,1)S(1)}, bf16[64,1024]{1,0:T(8,128)(2,1)S(1)}, u32[]{:S(2)}, u32[]{:S(2)}) collective-permute-start(bf16[64,1024]{1,0:T(8,128)(2,1)S(1)} %slice.283), channel_id=1, source_target_pairs={{0,4},{1,5},{2,6},{3,7},{4,0},{5,1},{6,2},{7,3},{8,12},{9,13},{10,... | collective-permute-start | bytes 393224 | tf_op jit(solution)/shard_map/ppermute | solution.py:23
  57.3 6.7 %copy-start.9 = (bf16[224,64]{1,0:T(8,128)(2,1)S(1)}, bf16[224,64]{1,0:T(8,128)(2,1)}, u32[]{:S(2)}) copy-start(bf16[224,64]{1,0:T(8,128)(2,1)} %constant.8.clone) | copy-start | bytes 86020
  57.3 4.6 %collective-permute-start.17 = (bf16[32,1024]{1,0:T(8,128)(2,1)S(1)}, bf16[32,1024]{1,0:T(8,128)(2,1)S(1)}, u32[]{:S(2)}, u32[]{:S(2)}) collective-permute-start(bf16[32,1024]{1,0:T(8,128)(2,1)S(1)} %get-tuple-element.42), channel_id=1, source_target_pairs={{0,3},{1,2},{2,1},{3,0},{4,7},{5,6},{6,5},{7,4},{8,11},{9,10},{10,... | collective-permute-start | bytes 196616 | tf_op jit(solution)/shard_map/ppermute | solution.py:23
  59.2 4.6 %collective-permute-start.16 = (bf16[32,1024]{1,0:T(8,128)(2,1)S(1)}, bf16[32,1024]{1,0:T(8,128)(2,1)S(1)}, u32[]{:S(2)}, u32[]{:S(2)}) collective-permute-start(bf16[32,1024]{1,0:T(8,128)(2,1)S(1)} %get-tuple-element.41), channel_id=1, source_target_pairs={{0,2},{1,3},{2,0},{3,1},{4,6},{5,7},{6,4},{7,5},{8,10},{9,11},{10,... | collective-permute-start | bytes 196616 | tf_op jit(solution)/shard_map/ppermute | solution.py:23
  59.9 4.0 %collective-permute-start.15 = (bf16[64,1024]{1,0:T(8,128)(2,1)S(1)}, bf16[64,1024]{1,0:T(8,128)(2,1)S(1)}, u32[]{:S(2)}, u32[]{:S(2)}) collective-permute-start(bf16[64,1024]{1,0:T(8,128)(2,1)S(1)} %fusion.8), channel_id=1, source_target_pairs={{0,1},{1,0},{2,3},{3,2},{4,5},{5,4},{6,7},{7,6},{8,9},{9,8},{10,11... | collective-permute-start | bytes 393224 | tf_op jit(solution)/shard_map/ppermute | solution.py:23
  64.4 5.1 %collective-permute-start.20 = (bf16[48,1024]{1,0:T(8,128)(2,1)S(1)}, bf16[48,1024]{1,0:T(8,128)(2,1)S(1)}, u32[]{:S(2)}, u32[]{:S(2)}) collective-permute-start(bf16[48,1024]{1,0:T(8,128)(2,1)S(1)} %pad_maximum_fusion.16), channel_id=1, source_target_pairs={{0,96},{16,112},{32,64},{48,80},{64,32},{80,48},{96,0},{112,16},{1... | collective-permute-start | bytes 294920 | tf_op jit(solution)/shard_map/ppermute | solution.py:23
  66.9 5.1 %collective-permute-start.19 = (bf16[48,1024]{1,0:T(8,128)(2,1)S(1)}, bf16[48,1024]{1,0:T(8,128)(2,1)S(1)}, u32[]{:S(2)}, u32[]{:S(2)}) collective-permute-start(bf16[48,1024]{1,0:T(8,128)(2,1)S(1)} %pad_maximum_fusion.15), channel_id=1, source_target_pairs={{0,64},{16,80},{32,96},{48,112},{64,0},{80,16},{96,32},{112,48},{1... | collective-permute-start | bytes 294920 | tf_op jit(solution)/shard_map/ppermute | solution.py:23
  67.6 4.5 %collective-permute-start.18 = (bf16[80,1024]{1,0:T(8,128)(2,1)S(1)}, bf16[80,1024]{1,0:T(8,128)(2,1)S(1)}, u32[]{:S(2)}, u32[]{:S(2)}) collective-permute-start(bf16[80,1024]{1,0:T(8,128)(2,1)S(1)} %pad_maximum_fusion.7), channel_id=1, source_target_pairs={{0,32},{16,48},{32,0},{48,16},{64,96},{80,112},{96,64},{112,80},{1... | collective-permute-start | bytes 491528 | tf_op jit(solution)/shard_map/ppermute | solution.py:23
  72.3 14.4 %collective-permute-start.21 = (bf16[72,1024]{1,0:T(8,128)(2,1)S(1)}, bf16[72,1024]{1,0:T(8,128)(2,1)S(1)}, u32[]{:S(2)}, u32[]{:S(2)}) collective-permute-start(bf16[72,1024]{1,0:T(8,128)(2,1)S(1)} %pad_maximum_fusion.8), channel_id=1, source_target_pairs={{0,16},{16,0},{32,48},{48,32},{64,80},{80,64},{96,112},{112,96},{1... | collective-permute-start | bytes 442376 | tf_op jit(solution)/shard_map/ppermute | solution.py:23
  85.1 0.8 copy-start.6
  85.9 0.8 copy-start.7
  86.8 6.6 %collective-permute-start.22 = (bf16[8,1024]{1,0:T(8,128)(2,1)S(1)}, bf16[8,1024]{1,0:T(8,128)(2,1)S(1)}, u32[]{:S(2)}, u32[]{:S(2)}) collective-permute-start(bf16[8,1024]{1,0:T(8,128)(2,1)S(1)} %fusion.54), channel_id=1, source_target_pairs={{0,128},{16,144},{32,160},{48,176},{64,192},{80,208},{96,224},{112... | collective-permute-start | bytes 49160 | tf_op jit(solution)/shard_map/ppermute | solution.py:23
  93.4 0.6 copy-start.12
where the time goes:
time: 96.6 us; the launch traced here: 96.4 us
  starting transfers between devices  40.1 us (42%)
  waiting for transfers between devices  26 us (27%)
  Pallas kernels  19 us (20%)
  local copies, waits for them, and re-layouts  6.4 us (7%)
  other arithmetic  1.76 us (2%)
  matrix products  1.68 us (2%)
  between operations  1.52 us (2%)
    ppermute x23, starting transfers between devices, flip(): lax.ppermute(value, axis, [(source, source ^ mask) for source in range(16)])  40.1 us
    ppermute x23, waiting for transfers between devices, flip(): lax.ppermute(value, axis, [(source, source ^ mask) for source in range(16)])  26 us
    unnamed x55, local copies, waits for them, and re-layouts  6.24 us
    pallas_call x1, Pallas kernels, own_part(): call(own_kernel, QUERY_SPECS + [rows_of_pair(TOK), rows_of_pair(TOK), row...  4.9 us
    pallas_call x1, Pallas kernels, low_part(): call(low_kernel, QUERY_SPECS + [rows_of_pair(rows), rows_of_pair(rows, PA...  3.48 us
    pallas_call x1, Pallas kernels, shards(): whole(finish_kernel, [jax.ShapeDtypeStruct((TOK, D), BF16)] * 2, 'finish')  2.43 us
    pallas_call x1, Pallas kernels, top_part(): call(top_kernel, QUERY_SPECS + [rows_of_pair(rows), rows_of_pair(rows, PA...  2.31 us
    pallas_call x1, Pallas kernels, low_stats(): call(stats_kernel, QUERY_SPECS + [rows_of_pair(rows), rows_of_pair(rows,...  2.18 us
  transfers between devices with their start and end apart: 23, of which 15 were waited for; matrix products, arithmetic and copies ran while one was open for 2% of the time, Pallas kernels for 9%

commit v1 on v0

v1 whole, which is shorter than its diff:
```python
import functools

import jax
import jax.numpy as jnp
import numpy as np
from jax import lax
from jax.experimental import pallas as pl
from jax.experimental.pallas import tpu as pltpu
from jax.sharding import PartitionSpec as P

F32 = jnp.float32
BF16 = jnp.bfloat16
D = 512
TOK = 256
PAIRS = 4
LANES = 128
SCALE = 64**-0.5
NT = (((1,), (1,)), ((), ()))
TN = (((0,), (0,)), ((), ()))


def flip(value, axis, mask):
    return lax.ppermute(value, axis, [(source, source ^ mask) for source in range(16)])


def reversed_bits(number, bits):
    return int(format(number, f"0{bits}b")[::-1], 2) if bits else 0


def token_pooling():
    table = np.zeros((104, TOK), np.float32)
    for base, bits in ((0, 6), (64, 5), (96, 3)):
        span = TOK >> bits
        for place in range(1 << bits):
            row = reversed_bits(place, bits) if bits > 3 else place
            table[base + place, row * span : (row + 1) * span] = 1.0 / span
    return table


def group_pooling():
    table = np.zeros((64, 224), np.float32)

    def put(column, row, core, half, across, weight):
        table[row * 16 + core * 8 + half * 4 + across, column] = weight

    for core in range(2):
        for place in range(16):
            put(core * 16 + place, place % 4, core, 0, 0, 0.25)
            put(96 + core * 16 + place, place % 4, core, 0, 2, 0.25)
            put(128 + core * 16 + place, place % 4, core, 0, 3, 0.25)
        for place in range(32):
            put(32 + core * 32 + place, place % 4, core, 0, 1, 0.125)
        for across in range(4):
            for place in range(8):
                row = reversed_bits(place >> 1, 2)
                put(160 + across * 16 + core * 8 + place, row, core, 1, across, 0.5)
    return table


def two_heads(block):
    first = lax.broadcasted_iota(jnp.int32, block.shape, 1) < 64
    zero = jnp.zeros_like(block)
    return jnp.concatenate([jnp.where(first, block, zero), jnp.where(first, zero, block)], axis=0)


def dot(left, right, dims=(((1,), (0,)), ((), ()))):
    return lax.dot_general(left, right, dims, preferred_element_type=F32)


def pool_kernel(table_ref, keys_ref, values_ref, zero_ref, one_ref, three_ref):
    for half, ref in enumerate((keys_ref, values_ref)):
        pooled = dot(table_ref[...], ref[...]).astype(BF16)
        columns = slice(half * D, (half + 1) * D)
        zero_ref[:, columns] = pooled[:64]
        one_ref[:, columns] = pooled[64:96]
        three_ref[:, columns] = pooled[96:104]


def stats_kernel(count, q_ref, do_ref, *refs):
    q2 = two_heads(q_ref[...] * SCALE)
    d2 = two_heads(do_ref[...])
    scores = jnp.concatenate([dot(ref[...], q2, NT) for ref in refs[:count]], axis=0)
    dprobs = jnp.concatenate([dot(ref[...], d2, NT) for ref in refs[count : 2 * count]], axis=0)
    out_ref = refs[-1]
    largest = jnp.max(scores, axis=0, keepdims=True)
    expsc = jnp.exp(scores - largest)
    out_ref[0, 0:1] = largest
    out_ref[0, 1:2] = jnp.sum(expsc, axis=0, keepdims=True)
    out_ref[0, 2:3] = jnp.sum(expsc * dprobs, axis=0, keepdims=True)


def top_kernel(q_ref, do_ref, k_ref, v_ref, low_ref, gk_ref, gv_ref, out_ref):
    q2 = two_heads(q_ref[...] * SCALE)
    d2 = two_heads(do_ref[...])
    scores = dot(k_ref[...], q2, NT)
    dprobs = dot(v_ref[...], d2, NT)
    low_largest = low_ref[0, 0:1]
    largest = jnp.maximum(jnp.max(scores, axis=0, keepdims=True), low_largest)
    expsc = jnp.exp(scores - largest)
    low_part = jnp.exp(low_largest - largest)
    total = jnp.sum(expsc, axis=0, keepdims=True) + low_ref[0, 1:2] * low_part
    inner = jnp.sum(expsc * dprobs, axis=0, keepdims=True) + low_ref[0, 2:3] * low_part
    share = 1.0 / total
    inner = inner * share
    out_ref[0, 0:1] = largest
    out_ref[0, 1:2] = share
    out_ref[0, 2:3] = inner
    probs = expsc * share
    dscores = (probs * (dprobs - inner)).astype(BF16)
    gk_ref[...] = dot(dscores, q2).astype(gk_ref.dtype)
    gv_ref[...] = dot(probs.astype(BF16), d2).astype(gv_ref.dtype)


def backward(q2, d2, k, v, stats_ref):
    scores = dot(k, q2, NT)
    dprobs = dot(v, d2, NT)
    probs = jnp.exp(scores - stats_ref[0, 0:1]) * stats_ref[0, 1:2]
    dscores = (probs * (dprobs - stats_ref[0, 2:3])).astype(BF16)
    weights = probs.astype(BF16)
    return weights, dscores, dot(v, weights, TN), dot(k, dscores, TN)


def grads_kernel(wanted, first, last, q_ref, do_ref, stats_ref, *refs):
    refs = list(refs)
    q2 = two_heads(q_ref[...] * SCALE)
    d2 = two_heads(do_ref[...])
    blocks = [(refs.pop(0), refs.pop(0)) for unused in wanted]
    before = [] if first else [refs.pop(0), refs.pop(0)]
    refs.pop(0)
    mixed_ref, gq_ref = refs.pop(0), refs.pop(0)
    mixed, gq = 0.0, 0.0
    for want, (k_ref, v_ref) in zip(wanted, blocks):
        weights, dscores, mixed_t, gq_t = backward(q2, d2, k_ref[...], v_ref[...], stats_ref)
        mixed, gq = mixed + mixed_t, gq + gq_t
        if want:
            gk_ref, gv_ref = refs.pop(0), refs.pop(0)
            gk_ref[...] = dot(dscores, q2)
            gv_ref[...] = dot(weights, d2)

    def pick(both):
        return jnp.concatenate([both[:64, :TOK], both[64:, TOK:]], axis=0)

    mixed, gq = pick(mixed), pick(gq)
    if before:
        mixed, gq = mixed + before[0][0], gq + before[1][0]
    if last:
        mixed_ref[...] = mixed.T.astype(BF16)
        gq_ref[...] = (gq * SCALE).T.astype(BF16)
    else:
        mixed_ref[0] = mixed
        gq_ref[0] = gq


def finish_kernel(table_ref, gk_ref, gv_ref, zero_ref, keys_ref, values_ref):
    for half, (ref, out_ref) in enumerate(((gk_ref, keys_ref), (gv_ref, values_ref))):
        rows = zero_ref[:, half * D : (half + 1) * D]
        high = rows.astype(BF16)
        low = (rows - high.astype(F32)).astype(BF16)
        out_ref[...] = ref[...] + dot(table_ref[...], high) + dot(table_ref[...], low)


def rows_of_pair(rows, shift=0):
    return pl.BlockSpec((rows, LANES), lambda pair: (0, pair + shift))


def per_pair(rows, columns):
    return pl.BlockSpec((1, rows, columns), lambda pair: (pair, 0, 0))


STATS = jax.ShapeDtypeStruct((PAIRS, 8, 2 * TOK), F32)
STATS_SPEC = per_pair(8, 2 * TOK)
PARTIAL = jax.ShapeDtypeStruct((PAIRS, LANES, TOK), F32)
PARTIAL_SPEC = per_pair(LANES, TOK)
QUERY_SPECS = [rows_of_pair(TOK), rows_of_pair(TOK)]


def call(kernel, in_specs, out_specs, out_shape, flops, name):
    return pl.pallas_call(
        kernel,
        grid=(PAIRS,),
        in_specs=in_specs,
        out_specs=out_specs,
        out_shape=out_shape,
        compiler_params=pltpu.CompilerParams(vmem_limit_bytes=40 * 2**20),
        cost_estimate=pl.CostEstimate(flops=flops, bytes_accessed=2**20, transcendentals=0),
        name=name,
    )


def matmul_cost(keys, count):
    return 2 * count * keys * 2 * TOK * LANES * PAIRS


def key_specs(block):
    keys, values = block
    return [rows_of_pair(keys.shape[0]), rows_of_pair(keys.shape[0], PAIRS if keys is values else 0)]


def low_stats(queries, cotangent, blocks):
    specs = [key_specs(block) for block in blocks]
    rows = sum(block[0].shape[0] for block in blocks)
    return call(
        functools.partial(stats_kernel, len(blocks)),
        QUERY_SPECS + [spec[0] for spec in specs] + [spec[1] for spec in specs],
        STATS_SPEC, STATS, matmul_cost(rows, 2), "low_stats",
    )(queries, cotangent, *[block[0] for block in blocks], *[block[1] for block in blocks])


def top_part(queries, cotangent, top, low):
    rows = top.shape[0]
    return call(
        top_kernel,
        QUERY_SPECS + key_specs((top, top)) + [STATS_SPEC],
        [rows_of_pair(rows), rows_of_pair(rows), STATS_SPEC],
        [jax.ShapeDtypeStruct((rows, D), BF16)] * 2 + [STATS],
        matmul_cost(rows, 4), "top_part",
    )(queries, cotangent, top, top, low)


def grads_part(queries, cotangent, stats, blocks, wanted, before, after, last, name):
    in_specs = QUERY_SPECS + [STATS_SPEC]
    operands = [queries, cotangent, stats]
    out_specs = [rows_of_pair(TOK)] * 2 if last else [PARTIAL_SPEC] * 2
    out_shape = [jax.ShapeDtypeStruct((TOK, D), BF16)] * 2 if last else [PARTIAL] * 2
    for block, want in zip(blocks, wanted):
        in_specs = in_specs + key_specs(block)
        operands += block
        if want:
            rows = block[0].shape[0]
            out_specs = out_specs + [rows_of_pair(rows)] * 2
            out_shape = out_shape + [jax.ShapeDtypeStruct((rows, D), F32)] * 2
    in_specs = in_specs + [PARTIAL_SPEC] * len(before) + [pl.BlockSpec((8, LANES), lambda pair: (0, 0))]
    operands += [*before, after]
    rows = sum(block[0].shape[0] for block in blocks)
    return call(
        functools.partial(grads_kernel, wanted, not before, last),
        in_specs, out_specs, out_shape, matmul_cost(rows, 6), name,
    )(*operands)


def whole(kernel, out_shape, name):
    return pl.pallas_call(kernel, out_shape=out_shape, name=name)


def halves(rows, parts=1):
    count, width = rows.shape
    split = rows.reshape(parts, 2, count // (2 * parts), width).astype(F32)
    return (0.5 * (split[:, 0] + split[:, 1])).astype(BF16).reshape(count // 2, width)


def spread(gradient, parts=1):
    count, width = gradient.shape
    split = (0.5 * gradient).reshape(parts, 1, count // parts, width)
    return jnp.concatenate([split, split], axis=1).reshape(2 * count, width)


def joined(*blocks):
    return jnp.concatenate(blocks, axis=0)


def both(gk, gv, rows=slice(None)):
    return jnp.concatenate([gk[rows], gv[rows]], axis=1)


def shards(queries, keys, values, cotangent):
    pooling = token_pooling()
    grouping = group_pooling()
    wide = lambda rows: jax.ShapeDtypeStruct((rows, 2 * D), BF16)

    zero, one, three = whole(pool_kernel, [wide(64), wide(32), wide(8)], "pool")(
        jnp.asarray(pooling, BF16), keys, values
    )
    far = flip(three, "lo", 8)
    sec0 = flip(zero, "lo", 1)
    far_pair = joined(far, flip(far, "lo", 1))
    level1 = joined(one, halves(sec0))
    level2 = halves(level1, 2)
    short = joined(level2, far_pair)
    x1 = flip(joined(level1, far_pair), "lo", 2)
    x2 = flip(short, "lo", 4)
    x3 = flip(short, "lo", 6)
    sec3 = joined(far_pair, x1[64:], x2[32:], x3[32:])
    low_x = joined(x1[:64], x2[:32], x3[:32], sec3)
    level4 = dot(jnp.asarray(grouping, BF16), joined(level2, low_x)).astype(BF16)
    level5 = halves(level4)
    y1 = flip(level4, "hi", 1)
    y2 = flip(level5, "hi", 2)
    y3 = flip(level5, "hi", 3)
    low_y = joined(y1, y2, y3)
    level6 = joined(halves(level5), halves(halves(y1)), halves(y2), halves(y3))
    level7 = halves(level6, 4)
    z1 = flip(level6, "hi", 4)
    z2 = flip(level7, "hi", 8)
    z3 = flip(level7, "hi", 12)
    own, sec0_block = (keys, values), (sec0, sec0)
    low = low_stats(queries, cotangent, [own, sec0_block, (low_x, low_x), (low_y, low_y)])
    top = joined(z1, z2, z3)

    top_gk, top_gv, stats = top_part(queries, cotangent, top, low)
    top_g = both(top_gk, top_gv)
    b1 = flip(top_g[:64], "hi", 4)
    b2 = flip(top_g[64:96], "hi", 8)
    b3 = flip(top_g[96:], "hi", 12)
    mixed, gq, gk, gv = grads_part(
        queries, cotangent, stats, [(low_y, low_y), (top, top)], (True, False), [], stats[0],
        False, "y_grads",
    )
    y_g = both(gk, gv)
    g6 = b1.astype(F32) + spread(b2.astype(F32) + b3.astype(F32), 4)
    b1 = flip((y_g[:64] + spread(spread(g6[16:32]))).astype(BF16), "hi", 1)
    b2 = flip((y_g[64:96] + spread(g6[32:48])).astype(BF16), "hi", 2)
    b3 = flip((y_g[96:] + spread(g6[48:64])).astype(BF16), "hi", 3)
    mixed, gq, gk, gv = grads_part(
        queries, cotangent, stats, [(low_x, low_x)], (True,), [mixed, gq], g6, False, "x_grads"
    )
    x_g = both(gk, gv)
    g5 = spread(g6[:16]) + b2.astype(F32) + b3.astype(F32)
    g4 = b1.astype(F32) + spread(g5)
    g = dot(jnp.asarray(grouping.T, BF16), g4.astype(BF16))
    x_g = x_g + g[32:]
    b1 = flip(joined(x_g[:64], x_g[144:160]).astype(BF16), "lo", 2)
    b2 = flip(joined(x_g[64:96], x_g[160:176]).astype(BF16), "lo", 4)
    b3 = flip(joined(x_g[96:128], x_g[176:]).astype(BF16), "lo", 6)
    mixed, grad_queries, gk, gv, own_gk, own_gv = grads_part(
        queries, cotangent, stats, [sec0_block, own], (True, True), [mixed, gq], g4, True, "own_grads"
    )
    b1, b2, b3 = b1.astype(F32), b2.astype(F32), b3.astype(F32)
    g2 = g[:32] + b2[:32] + b3[:32]
    far_g = x_g[128:144] + b1[64:] + b2[32:] + b3[32:]
    g1 = b1[:64] + spread(g2, 2)
    back = flip(joined(both(gk, gv) + spread(g1[32:]), far_g[8:]).astype(BF16), "lo", 1).astype(F32)
    g0 = back[:64] + spread(g1[:32])
    last = flip((far_g[:8] + back[64:]).astype(BF16), "lo", 8).astype(F32)
    near_keys, near_values = whole(
        finish_kernel, [jax.ShapeDtypeStruct((TOK, D), F32)] * 2, "finish"
    )(jnp.asarray(pooling[:64].T, BF16), own_gk, own_gv, g0)

    def add_last(near, part):
        blocks = near.reshape(8, TOK // 8, D) + (part * (8 / TOK))[:, None, :]
        return blocks.astype(BF16).reshape(TOK, D)

    return (mixed, grad_queries, add_last(near_keys, last[:, :D]), add_last(near_values, last[:, D:]))


def solution(mesh):
    spec = P(("hi", "lo"), None)
    return jax.shard_map(
        shards, mesh=mesh, in_specs=(spec,) * 4, out_specs=(spec,) * 4, check_vma=False
    )
```

time: 96.6 us -> 92.2 us (0.954)
  waiting for transfers between devices: 26 us -> 16.5 us
  starting transfers between devices: 40.1 us -> 43.8 us
  local copies, waits for them, and re-layouts: 6.4 us -> 3.12 us
  other arithmetic: 1.76 us -> 4.38 us
  Pallas kernels: 19 us -> 20.7 us
    ppermute x23, waiting for transfers between devices: 26 us -> 16.5 us  [flip(): lax.ppermute(value, axis, [(source, source ^ mask) for source in range(16)])]
    ppermute x23, starting transfers between devices: 40.1 us -> 43.8 us  [flip(): lax.ppermute(value, axis, [(source, source ^ mask) for source in range(16)])]
    unnamed x55 -> x49, local copies, waits for them, and re-layouts: 6.24 us -> 2.98 us
    convert_element_type x5 -> x7, other arithmetic: 0.12 us -> 2.69 us  [the longest x2 2.59 us: add_last(): return blocks.astype(BF16).reshape(TOK, D)]
    pallas_call x6, Pallas kernels: 17 us -> 18.7 us  [the longest x3 10.6 us: grads_part(): call(functools.partial(grads_kernel, wanted, not before, last), in_specs,...]
  transfers between devices with their start and end apart: 23 -> 23, of which waited for: 15 -> 12; matrix products, arithmetic and copies ran while one was open for 2% -> 3% of each run, Pallas kernels for 9% -> 14%
where the time goes in v1:
time: 92.2 us; the launch traced here: 91.6 us
  starting transfers between devices  43.8 us (48%)
  Pallas kernels  20.7 us (22%)
  waiting for transfers between devices  16.5 us (18%)
  other arithmetic  4.38 us (5%)
  local copies, waits for them, and re-layouts  3.12 us (3%)
  matrix products  1.68 us (2%)
  between operations  1.55 us (2%)
    ppermute x23, starting transfers between devices, flip(): lax.ppermute(value, axis, [(source, source ^ mask) for source in range(16)])  43.8 us
    ppermute x23, waiting for transfers between devices, flip(): lax.ppermute(value, axis, [(source, source ^ mask) for source in range(16)])  16.5 us
    pallas_call x3, Pallas kernels, grads_part(): call(functools.partial(grads_kernel, wanted, not before, last), in_specs,...  10.6 us
    pallas_call x1, Pallas kernels, low_stats(): call(functools.partial(stats_kernel, len(blocks)), QUERY_SPECS + [spec[0]...  3.3 us
    unnamed x49, local copies, waits for them, and re-layouts  2.98 us
    convert_element_type x2, other arithmetic, add_last(): return blocks.astype(BF16).reshape(TOK, D)  2.59 us
    pallas_call x1, Pallas kernels, shards(): whole(finish_kernel, [jax.ShapeDtypeStruct((TOK, D), F32)] * 2, 'finish')  2.54 us
    pallas_call x1, Pallas kernels, top_part(): call(top_kernel, QUERY_SPECS + key_specs((top, top)) + [STATS_SPEC], [row...  2.3 us
  transfers between devices with their start and end apart: 23, of which 12 were waited for; matrix products, arithmetic and copies ran while one was open for 3% of the time, Pallas kernels for 14%

profile of v1, /device:TPU:1, one launch (start us, length us, event | category | flops | bytes accessed | tf_op | source)
XLA Modules:
  0.0 91.6 jit_solution(8423350183482467297)
XLA Ops:
  0.6 1.9 %pool.1 = (bf16[64,1024]{1,0:T(8,128)(2,1)}, bf16[32,1024]{1,0:T(8,128)(2,1)}, bf16[8,1024]{1,0:T(8,128)(2,1)}) custom-call(bf16[104,256]{1,0:T(8,128)(2,1)} %constant.8.clone.table_ref, bf16[256,512]{1,0:T(8,128)(2,1)} %refs_2_.1, bf16[256,512]{1,0:T(8,128)(2,1)} %refs_3_.1), custom_call_target="tpu_custom_call" | custom-call | tf_op jit(solution)/shard_map/pool/pallas_call | solution.py:270
  2.6 7.7 %collective-permute-start.1 = (bf16[8,1024]{1,0:T(8,128)(2,1)}, bf16[8,1024]{1,0:T(8,128)(2,1)S(1)}, u32[]{:S(2)}, u32[]{:S(2)}) collective-permute-start(bf16[8,1024]{1,0:T(8,128)(2,1)} %get-tuple-element.28), channel_id=1, source_target_pairs={{0,128},{16,144},{32,160},{48,176},{64,192},{80,208},{96,224},{112... | collective-permute-start | bytes 49160 | tf_op jit(solution)/shard_map/ppermute | solution.py:23
  10.3 1.0 %collective-permute-start = (bf16[64,1024]{1,0:T(8,128)(2,1)}, bf16[64,1024]{1,0:T(8,128)(2,1)S(1)}, u32[]{:S(2)}, u32[]{:S(2)}) collective-permute-start(bf16[64,1024]{1,0:T(8,128)(2,1)} %get-tuple-element.27), channel_id=1, source_target_pairs={{0,16},{16,0},{32,48},{48,32},{64,80},{80,64},{96,112},{112,96},{1... | collective-permute-start | bytes 393224 | tf_op jit(solution)/shard_map/ppermute | solution.py:23
  11.3 0.4 collective-permute-done.1
  11.7 2.0 %collective-permute-start.2 = (bf16[8,1024]{1,0:T(8,128)(2,1)S(1)}, bf16[8,1024]{1,0:T(8,128)(2,1)S(1)}, u32[]{:S(2)}, u32[]{:S(2)}) collective-permute-start(bf16[8,1024]{1,0:T(8,128)(2,1)S(1)} %collective-permute-done.1), channel_id=1, source_target_pairs={{0,16},{16,0},{32,48},{48,32},{64,80},{80,64},{96,112},{112,96},{1... | collective-permute-start | bytes 49160 | tf_op jit(solution)/shard_map/ppermute | solution.py:23
  13.9 0.8 copy-done.7
  14.8 2.1 %collective-permute-start.5 = (bf16[48,1024]{1,0:T(8,128)(2,1)S(1)}, bf16[48,1024]{1,0:T(8,128)(2,1)S(1)}, u32[]{:S(2)}, u32[]{:S(2)}) collective-permute-start(bf16[48,1024]{1,0:T(8,128)(2,1)S(1)} %pad_maximum_fusion.14), channel_id=1, source_target_pairs={{0,96},{16,112},{32,64},{48,80},{64,32},{80,48},{96,0},{112,16},{1... | collective-permute-start | bytes 294920 | tf_op jit(solution)/shard_map/ppermute | solution.py:23
  16.9 0.5 collective-permute-start.4
  17.5 0.8 collective-permute-start.3
  18.5 2.1 %collective-permute-done.5 = bf16[48,1024]{1,0:T(8,128)(2,1)S(1)} collective-permute-done((bf16[48,1024]{1,0:T(8,128)(2,1)S(1)}, bf16[48,1024]{1,0:T(8,128)(2,1)S(1)}, u32[]{:S(2)}, u32[]{:S(2)}) %collective-permute-start.5) | collective-permute-done | bytes 98336 | tf_op jit(solution)/shard_map/ppermute | solution.py:23
  20.9 1.5 %collective-permute-done.4 = bf16[48,1024]{1,0:T(8,128)(2,1)S(1)} collective-permute-done((bf16[48,1024]{1,0:T(8,128)(2,1)S(1)}, bf16[48,1024]{1,0:T(8,128)(2,1)S(1)}, u32[]{:S(2)}, u32[]{:S(2)}) %collective-permute-start.4) | collective-permute-done | bytes 98336 | tf_op jit(solution)/shard_map/ppermute | solution.py:23
  22.8 1.5 %collective-permute-done.3 = bf16[80,1024]{1,0:T(8,128)(2,1)S(1)} collective-permute-done((bf16[80,1024]{1,0:T(8,128)(2,1)S(1)}, bf16[80,1024]{1,0:T(8,128)(2,1)S(1)}, u32[]{:S(2)}, u32[]{:S(2)}) %collective-permute-start.3) | collective-permute-done | bytes 163872 | tf_op jit(solution)/shard_map/ppermute | solution.py:23
  24.7 0.5 copy-done.9
  25.4 2.5 %collective-permute-start.7 = (bf16[32,1024]{1,0:T(8,128)(2,1)S(1)}, bf16[32,1024]{1,0:T(8,128)(2,1)S(1)}, u32[]{:S(2)}, u32[]{:S(2)}) collective-permute-start(bf16[32,1024]{1,0:T(8,128)(2,1)S(1)} %fusion.81), channel_id=1, source_target_pairs={{0,2},{1,3},{2,0},{3,1},{4,6},{5,7},{6,4},{7,5},{8,10},{9,11},{10,... | collective-permute-start | bytes 196616 | tf_op jit(solution)/shard_map/ppermute | solution.py:23
  28.0 0.8 collective-permute-start.8
  29.0 1.2 %collective-permute-done.7 = bf16[32,1024]{1,0:T(8,128)(2,1)S(1)} collective-permute-done((bf16[32,1024]{1,0:T(8,128)(2,1)S(1)}, bf16[32,1024]{1,0:T(8,128)(2,1)S(1)}, u32[]{:S(2)}, u32[]{:S(2)}) %collective-permute-start.7) | collective-permute-done | bytes 65568 | tf_op jit(solution)/shard_map/ppermute | solution.py:23
  30.2 2.3 %collective-permute-done.8 = bf16[32,1024]{1,0:T(8,128)(2,1)S(1)} collective-permute-done((bf16[32,1024]{1,0:T(8,128)(2,1)S(1)}, bf16[32,1024]{1,0:T(8,128)(2,1)S(1)}, u32[]{:S(2)}, u32[]{:S(2)}) %collective-permute-start.8) | collective-permute-done | bytes 65568 | tf_op jit(solution)/shard_map/ppermute | solution.py:23
  32.5 0.8 collective-permute-done.6
  33.4 0.8 collective-permute-start.9
  34.4 2.7 %collective-permute-start.10 = (bf16[32,1024]{1,0:T(8,128)(2,1)S(1)}, bf16[32,1024]{1,0:T(8,128)(2,1)S(1)}, u32[]{:S(2)}, u32[]{:S(2)}) collective-permute-start(bf16[32,1024]{1,0:T(8,128)(2,1)S(1)} %fusion.34), channel_id=1, source_target_pairs={{0,8},{1,9},{2,10},{3,11},{4,12},{5,13},{6,14},{7,15},{8,0},{9,1},... | collective-permute-start | bytes 196616 | tf_op jit(solution)/shard_map/ppermute | solution.py:23
  37.3 3.3 %low_stats.1.low_ref = f32[4,8,512]{2,1,0:T(8,128)S(1)} custom-call(bf16[256,512]{1,0:T(8,128)(2,1)S(1)} %copy-done, bf16[256,512]{1,0:T(8,128)(2,1)S(1)} %copy-done.1, bf16[256,512]{1,0:T(8,128)(2,1)S(1)} %copy-done.2, bf16[64,1024]{1,0:T(8,128)(2,1)S(1)} %collective-permute-done.refs_1_.refs_5_.refs_0_, ...), custom_call_target="tpu_custom_call" | custom-call | flops 671088640 | bytes 1048576 | tf_op jit(solution)/shard_map/low_stats/pallas_call | solution.py:202
  40.7 2.0 %collective-permute-done.11 = bf16[32,1024]{1,0:T(8,128)(2,1)S(1)} collective-permute-done((bf16[32,1024]{1,0:T(8,128)(2,1)S(1)}, bf16[32,1024]{1,0:T(8,128)(2,1)S(1)}, u32[]{:S(2)}, u32[]{:S(2)}) %collective-permute-start.11) | collective-permute-done | bytes 65568 | tf_op jit(solution)/shard_map/ppermute | solution.py:23
  42.7 2.3 %top_part.1 = (bf16[128,512]{1,0:T(8,128)(2,1)S(1)}, bf16[128,512]{1,0:T(8,128)(2,1)S(1)}, f32[4,8,512]{2,1,0:T(8,128)S(1)}) custom-call(bf16[256,512]{1,0:T(8,128)(2,1)S(1)} %copy-done, bf16[256,512]{1,0:T(8,128)(2,1)S(1)} %copy-done.1, bf16[128,1024]{1,0:T(8,128)(2,1)S(1)} %constant_dynamic-update-slice_fusion.k_ref.v_ref.refs_2_.refs_3_, ...), custom_call_target="tpu_custom_call" | custom-call | flops 268435456 | bytes 1048576 | tf_op jit(solution)/shard_map/top_part/pallas_call | solution.py:211
  45.1 3.3 %y_grads.1 = (f32[4,128,256]{2,1,0:T(8,128)S(1)}, f32[4,128,256]{2,1,0:T(8,128)S(1)}, f32[128,512]{1,0:T(8,128)S(1)}, f32[128,512]{1,0:T(8,128)S(1)}) custom-call(bf16[256,512]{1,0:T(8,128)(2,1)S(1)} %copy-done, bf16[256,512]{1,0:T(8,128)(2,1)S(1)} %copy-done.1, f32[4,8,512]{2,1,0:T(8,128)S(1)} %get-tuple-element.29.stats_ref, ...), custom_call_target="tpu_custom_call" | custom-call | flops 805306368 | bytes 1048576 | tf_op jit(solution)/shard_map/y_grads/pallas_call | solution.py:235
  48.4 1.4 %collective-permute-start.14 = (bf16[32,1024]{1,0:T(8,128)(2,1)S(1)}, bf16[32,1024]{1,0:T(8,128)(2,1)S(1)}, u32[]{:S(2)}, u32[]{:S(2)}) collective-permute-start(bf16[32,1024]{1,0:T(8,128)(2,1)S(1)} %get-tuple-element.64), channel_id=1, source_target_pairs={{0,12},{1,13},{2,14},{3,15},{4,8},{5,9},{6,10},{7,11},{8,4},{9,5},... | collective-permute-start | bytes 196616 | tf_op jit(solution)/shard_map/ppermute | solution.py:23
  49.8 2.2 %collective-permute-start.12 = (bf16[64,1024]{1,0:T(8,128)(2,1)S(1)}, bf16[64,1024]{1,0:T(8,128)(2,1)S(1)}, u32[]{:S(2)}, u32[]{:S(2)}) collective-permute-start(bf16[64,1024]{1,0:T(8,128)(2,1)S(1)} %slice.272), channel_id=1, source_target_pairs={{0,4},{1,5},{2,6},{3,7},{4,0},{5,1},{6,2},{7,3},{8,12},{9,13},{10,... | collective-permute-start | bytes 393224 | tf_op jit(solution)/shard_map/ppermute | solution.py:23
  52.1 1.4 %collective-permute-done.14 = bf16[32,1024]{1,0:T(8,128)(2,1)S(1)} collective-permute-done((bf16[32,1024]{1,0:T(8,128)(2,1)S(1)}, bf16[32,1024]{1,0:T(8,128)(2,1)S(1)}, u32[]{:S(2)}, u32[]{:S(2)}) %collective-permute-start.14) | collective-permute-done | bytes 65568 | tf_op jit(solution)/shard_map/ppermute | solution.py:23
  53.5 2.0 %collective-permute-done.13 = bf16[32,1024]{1,0:T(8,128)(2,1)S(1)} collective-permute-done((bf16[32,1024]{1,0:T(8,128)(2,1)S(1)}, bf16[32,1024]{1,0:T(8,128)(2,1)S(1)}, u32[]{:S(2)}, u32[]{:S(2)}) %collective-permute-start.13) | collective-permute-done | bytes 65568 | tf_op jit(solution)/shard_map/ppermute | solution.py:23
  55.8 1.6 %collective-permute-start.17 = (bf16[32,1024]{1,0:T(8,128)(2,1)S(1)}, bf16[32,1024]{1,0:T(8,128)(2,1)S(1)}, u32[]{:S(2)}, u32[]{:S(2)}) collective-permute-start(bf16[32,1024]{1,0:T(8,128)(2,1)S(1)} %get-tuple-element.51), channel_id=1, source_target_pairs={{0,3},{1,2},{2,1},{3,0},{4,7},{5,6},{6,5},{7,4},{8,11},{9,10},{10,... | collective-permute-start | bytes 196616 | tf_op jit(solution)/shard_map/ppermute | solution.py:23
  57.4 0.7 collective-permute-start.16
  58.2 1.3 %collective-permute-start.15 = (bf16[64,1024]{1,0:T(8,128)(2,1)S(1)}, bf16[64,1024]{1,0:T(8,128)(2,1)S(1)}, u32[]{:S(2)}, u32[]{:S(2)}) collective-permute-start(bf16[64,1024]{1,0:T(8,128)(2,1)S(1)} %fusion.9), channel_id=1, source_target_pairs={{0,1},{1,0},{2,3},{3,2},{4,5},{5,4},{6,7},{7,6},{8,9},{9,8},{10,11... | collective-permute-start | bytes 393224 | tf_op jit(solution)/shard_map/ppermute | solution.py:23
  59.5 2.5 %x_grads.1 = (f32[4,128,256]{2,1,0:T(8,128)S(1)}, f32[4,128,256]{2,1,0:T(8,128)S(1)}, f32[192,512]{1,0:T(8,128)S(1)}, f32[192,512]{1,0:T(8,128)S(1)}) custom-call(bf16[256,512]{1,0:T(8,128)(2,1)S(1)} %copy-done, bf16[256,512]{1,0:T(8,128)(2,1)S(1)} %copy-done.1, f32[4,8,512]{2,1,0:T(8,128)S(1)} %get-tuple-element.29.stats_ref, ...), custom_call_target="tpu_custom_call" | custom-call | flops 603979776 | bytes 1048576 | tf_op jit(solution)/shard_map/x_grads/pallas_call | solution.py:235
  62.1 0.2 collective-permute-done.15
  62.4 0.5 copy-done.8
  62.9 0.2 fusion.30
  63.4 2.8 %collective-permute-start.20 = (bf16[48,1024]{1,0:T(8,128)(2,1)S(1)}, bf16[48,1024]{1,0:T(8,128)(2,1)S(1)}, u32[]{:S(2)}, u32[]{:S(2)}) collective-permute-start(bf16[48,1024]{1,0:T(8,128)(2,1)S(1)} %pad_maximum_fusion.16), channel_id=1, source_target_pairs={{0,96},{16,112},{32,64},{48,80},{64,32},{80,48},{96,0},{112,16},{1... | collective-permute-start | bytes 294920 | tf_op jit(solution)/shard_map/ppermute | solution.py:23
  66.2 0.5 collective-permute-start.19
  66.7 0.3 collective-permute-start.18
  67.0 4.8 %own_grads.1 = (bf16[256,512]{1,0:T(8,128)(2,1)}, bf16[256,512]{1,0:T(8,128)(2,1)}, f32[64,512]{1,0:T(8,128)S(1)}, f32[64,512]{1,0:T(8,128)S(1)}, f32[256,512]{1,0:T(8,128)S(1)}, /*index=5*/f32[256,512]{1,0:T(8,128)S(1)}) custom-call(bf16[256,512]{1,0:T(8,128)(2,1)S(1)} %copy-done, bf16[256,512]{1,0:T(8,128)(2,1)S(1)} %copy-done.1, ...), custom_call_target="tpu_custom_call" | custom-call | flops 1006632960 | bytes 1048576 | tf_op jit(solution)/shard_map/own_grads/pallas_call | solution.py:235
  71.8 0.7 copy-done.4
  72.5 0.2 copy-done.5
  73.0 7.4 %collective-permute-start.21 = (bf16[72,1024]{1,0:T(8,128)(2,1)S(1)}, bf16[72,1024]{1,0:T(8,128)(2,1)S(1)}, u32[]{:S(2)}, u32[]{:S(2)}) collective-permute-start(bf16[72,1024]{1,0:T(8,128)(2,1)S(1)} %pad_maximum_fusion.8), channel_id=1, source_target_pairs={{0,16},{16,0},{32,48},{48,32},{64,80},{80,64},{96,112},{112,96},{1... | collective-permute-start | bytes 442376 | tf_op jit(solution)/shard_map/ppermute | solution.py:23
  80.4 1.0 %collective-permute-done.21 = bf16[72,1024]{1,0:T(8,128)(2,1)S(1)} collective-permute-done((bf16[72,1024]{1,0:T(8,128)(2,1)S(1)}, bf16[72,1024]{1,0:T(8,128)(2,1)S(1)}, u32[]{:S(2)}, u32[]{:S(2)}) %collective-permute-start.21) | collective-permute-done | bytes 147488 | tf_op jit(solution)/shard_map/ppermute | solution.py:23
  81.4 4.3 %collective-permute-start.22 = (bf16[8,1024]{1,0:T(8,128)(2,1)S(1)}, bf16[8,1024]{1,0:T(8,128)(2,1)S(1)}, u32[]{:S(2)}, u32[]{:S(2)}) collective-permute-start(bf16[8,1024]{1,0:T(8,128)(2,1)S(1)} %fusion.55), channel_id=1, source_target_pairs={{0,128},{16,144},{32,160},{48,176},{64,192},{80,208},{96,224},{112... | collective-permute-start | bytes 49160 | tf_op jit(solution)/shard_map/ppermute | solution.py:23
  85.7 0.7 slice_add_fusion.1.zero_ref
  86.5 2.5 %finish.1 = (f32[256,512]{1,0:T(8,128)}, f32[256,512]{1,0:T(8,128)}) custom-call(bf16[256,64]{1,0:T(8,128)(2,1)} %constant.4.clone.table_ref, f32[256,512]{1,0:T(8,128)} %copy-done.4, f32[256,512]{1,0:T(8,128)} %copy-done.5, f32[64,1024]{1,0:T(8,128)} %slice_add_fusion.1.zero_ref), custom_call_target="tpu_custom_call" | custom-call | tf_op jit(solution)/shard_map/finish/pallas_call | solution.py:334
  89.0 1.8 %fusion.8 = bf16[256,512]{1,0:T(8,128)(2,1)} fusion(f32[256,512]{1,0:T(8,128)} %get-tuple-element.46, f32[8,512]{1,0:T(8,128)S(1)} %get-tuple-element.66), kind=kLoop, calls=%fused_computation.13 | loop fusion | flops 262144 | bytes 802816 | tf_op jit(solution)/shard_map/convert_element_type | solution.py:340
  90.9 0.7 fusion.7
  (136 shorter events, 3.2 us)
Async XLA Ops:
  0.6 13.1 %copy-start.14 = (bf16[64,8]{1,0:T(8,128)(2,1)S(1)}, bf16[64,8]{1,0:T(8,128)(2,1)}, u32[]{:S(2)}) copy-start(bf16[64,8]{1,0:T(8,128)(2,1)} %constant.25) | copy-start | bytes 3076
  2.6 9.1 %collective-permute-start.1 = (bf16[8,1024]{1,0:T(8,128)(2,1)}, bf16[8,1024]{1,0:T(8,128)(2,1)S(1)}, u32[]{:S(2)}, u32[]{:S(2)}) collective-permute-start(bf16[8,1024]{1,0:T(8,128)(2,1)} %get-tuple-element.28), channel_id=1, source_target_pairs={{0,128},{16,144},{32,160},{48,176},{64,192},{80,208},{96,224},{112... | collective-permute-start | bytes 49160 | tf_op jit(solution)/shard_map/ppermute | solution.py:23
  10.3 3.5 %collective-permute-start = (bf16[64,1024]{1,0:T(8,128)(2,1)}, bf16[64,1024]{1,0:T(8,128)(2,1)S(1)}, u32[]{:S(2)}, u32[]{:S(2)}) collective-permute-start(bf16[64,1024]{1,0:T(8,128)(2,1)} %get-tuple-element.27), channel_id=1, source_target_pairs={{0,16},{16,0},{32,48},{48,32},{64,80},{80,64},{96,112},{112,96},{1... | collective-permute-start | bytes 393224 | tf_op jit(solution)/shard_map/ppermute | solution.py:23
  11.7 3.1 %collective-permute-start.2 = (bf16[8,1024]{1,0:T(8,128)(2,1)S(1)}, bf16[8,1024]{1,0:T(8,128)(2,1)S(1)}, u32[]{:S(2)}, u32[]{:S(2)}) collective-permute-start(bf16[8,1024]{1,0:T(8,128)(2,1)S(1)} %collective-permute-done.1), channel_id=1, source_target_pairs={{0,16},{16,0},{32,48},{48,32},{64,80},{80,64},{96,112},{112,96},{1... | collective-permute-start | bytes 49160 | tf_op jit(solution)/shard_map/ppermute | solution.py:23
  13.9 0.8 copy-start.7
  14.8 3.5 %copy-start.17 = (bf16[64,32]{1,0:T(8,128)(2,1)S(1)}, bf16[64,32]{1,0:T(8,128)(2,1)}, u32[]{:S(2)}) copy-start(bf16[64,32]{1,0:T(8,128)(2,1)} %constant.5) | copy-start | bytes 12292
  14.8 5.7 %collective-permute-start.5 = (bf16[48,1024]{1,0:T(8,128)(2,1)S(1)}, bf16[48,1024]{1,0:T(8,128)(2,1)S(1)}, u32[]{:S(2)}, u32[]{:S(2)}) collective-permute-start(bf16[48,1024]{1,0:T(8,128)(2,1)S(1)} %pad_maximum_fusion.14), channel_id=1, source_target_pairs={{0,96},{16,112},{32,64},{48,80},{64,32},{80,48},{96,0},{112,16},{1... | collective-permute-start | bytes 294920 | tf_op jit(solution)/shard_map/ppermute | solution.py:23
  16.9 5.6 %collective-permute-start.4 = (bf16[48,1024]{1,0:T(8,128)(2,1)S(1)}, bf16[48,1024]{1,0:T(8,128)(2,1)S(1)}, u32[]{:S(2)}, u32[]{:S(2)}) collective-permute-start(bf16[48,1024]{1,0:T(8,128)(2,1)S(1)} %pad_maximum_fusion.14), channel_id=1, source_target_pairs={{0,64},{16,80},{32,96},{48,112},{64,0},{80,16},{96,32},{112,48},{1... | collective-permute-start | bytes 294920 | tf_op jit(solution)/shard_map/ppermute | solution.py:23
  17.5 3.1 %copy-start.16 = (bf16[64,32]{1,0:T(8,128)(2,1)S(1)}, bf16[64,32]{1,0:T(8,128)(2,1)}, u32[]{:S(2)}) copy-start(bf16[64,32]{1,0:T(8,128)(2,1)} %constant.24) | copy-start | bytes 12292
  17.5 6.8 %collective-permute-start.3 = (bf16[80,1024]{1,0:T(8,128)(2,1)S(1)}, bf16[80,1024]{1,0:T(8,128)(2,1)S(1)}, u32[]{:S(2)}, u32[]{:S(2)}) collective-permute-start(bf16[80,1024]{1,0:T(8,128)(2,1)S(1)} %pad_maximum_fusion.6), channel_id=1, source_target_pairs={{0,32},{16,48},{32,0},{48,16},{64,96},{80,112},{96,64},{112,80},{1... | collective-permute-start | bytes 491528 | tf_op jit(solution)/shard_map/ppermute | solution.py:23
  18.5 2.3 %copy-start.13 = (bf16[64,16]{1,0:T(8,128)(2,1)S(1)}, bf16[64,16]{1,0:T(8,128)(2,1)}, u32[]{:S(2)}) copy-start(bf16[64,16]{1,0:T(8,128)(2,1)} %constant.29) | copy-start | bytes 6148
  20.8 1.7 %copy-start.15 = (bf16[64,32]{1,0:T(8,128)(2,1)S(1)}, bf16[64,32]{1,0:T(8,128)(2,1)}, u32[]{:S(2)}) copy-start(bf16[64,32]{1,0:T(8,128)(2,1)} %constant.23) | copy-start | bytes 12292
  20.9 1.7 %copy-start.12 = (bf16[64,16]{1,0:T(8,128)(2,1)S(1)}, bf16[64,16]{1,0:T(8,128)(2,1)}, u32[]{:S(2)}) copy-start(bf16[64,16]{1,0:T(8,128)(2,1)} %constant.28) | copy-start | bytes 6148
  22.7 1.7 %copy-start.11 = (bf16[64,16]{1,0:T(8,128)(2,1)S(1)}, bf16[64,16]{1,0:T(8,128)(2,1)}, u32[]{:S(2)}) copy-start(bf16[64,16]{1,0:T(8,128)(2,1)} %constant.27) | copy-start | bytes 6148
  22.8 1.7 %copy-start.10 = (bf16[64,64]{1,0:T(8,128)(2,1)S(1)}, bf16[64,64]{1,0:T(8,128)(2,1)}, u32[]{:S(2)}) copy-start(bf16[64,64]{1,0:T(8,128)(2,1)} %constant.22) | copy-start | bytes 24580
  24.5 0.7 copy-start.9
  25.4 4.7 %collective-permute-start.7 = (bf16[32,1024]{1,0:T(8,128)(2,1)S(1)}, bf16[32,1024]{1,0:T(8,128)(2,1)S(1)}, u32[]{:S(2)}, u32[]{:S(2)}) collective-permute-start(bf16[32,1024]{1,0:T(8,128)(2,1)S(1)} %fusion.81), channel_id=1, source_target_pairs={{0,2},{1,3},{2,0},{3,1},{4,6},{5,7},{6,4},{7,5},{8,10},{9,11},{10,... | collective-permute-start | bytes 196616 | tf_op jit(solution)/shard_map/ppermute | solution.py:23
  28.0 4.5 %collective-permute-start.8 = (bf16[32,1024]{1,0:T(8,128)(2,1)S(1)}, bf16[32,1024]{1,0:T(8,128)(2,1)S(1)}, u32[]{:S(2)}, u32[]{:S(2)}) collective-permute-start(bf16[32,1024]{1,0:T(8,128)(2,1)S(1)} %fusion.81), channel_id=1, source_target_pairs={{0,3},{1,2},{2,1},{3,0},{4,7},{5,6},{6,5},{7,4},{8,11},{9,10},{10,... | collective-permute-start | bytes 196616 | tf_op jit(solution)/shard_map/ppermute | solution.py:23
  28.8 4.6 %collective-permute-start.6 = (bf16[64,1024]{1,0:T(8,128)(2,1)S(1)}, bf16[64,1024]{1,0:T(8,128)(2,1)S(1)}, u32[]{:S(2)}, u32[]{:S(2)}) collective-permute-start(bf16[64,1024]{1,0:T(8,128)(2,1)S(1)} %bitcast.129), channel_id=1, source_target_pairs={{0,1},{1,0},{2,3},{3,2},{4,5},{5,4},{6,7},{7,6},{8,9},{9,8},{10,11... | collective-permute-start | bytes 393224 | tf_op jit(solution)/shard_map/ppermute | solution.py:23
  33.4 7.2 %collective-permute-start.9 = (bf16[64,1024]{1,0:T(8,128)(2,1)S(1)}, bf16[64,1024]{1,0:T(8,128)(2,1)S(1)}, u32[]{:S(2)}, u32[]{:S(2)}) collective-permute-start(bf16[64,1024]{1,0:T(8,128)(2,1)S(1)} %pad_maximum_fusion.10), channel_id=1, source_target_pairs={{0,4},{1,5},{2,6},{3,7},{4,0},{5,1},{6,2},{7,3},{8,12},{9,13},{10,... | collective-permute-start | bytes 393224 | tf_op jit(solution)/shard_map/ppermute | solution.py:23
  34.3 3.0 %copy-start.3 = (bf16[256,512]{1,0:T(8,128)(2,1)S(1)}, bf16[256,512]{1,0:T(8,128)(2,1)}, u32[]{:S(2)}) copy-start(bf16[256,512]{1,0:T(8,128)(2,1)} %refs_3_.1) | copy-start | bytes 786436
  34.3 3.0 %copy-start.1 = (bf16[256,512]{1,0:T(8,128)(2,1)S(1)}, bf16[256,512]{1,0:T(8,128)(2,1)}, u32[]{:S(2)}) copy-start(bf16[256,512]{1,0:T(8,128)(2,1)} %do_ref.9) | copy-start | bytes 786436
  34.3 3.0 %copy-start.2 = (bf16[256,512]{1,0:T(8,128)(2,1)S(1)}, bf16[256,512]{1,0:T(8,128)(2,1)}, u32[]{:S(2)}) copy-start(bf16[256,512]{1,0:T(8,128)(2,1)} %refs_2_.1) | copy-start | bytes 786436
  34.4 3.0 %copy-start = (bf16[256,512]{1,0:T(8,128)(2,1)S(1)}, bf16[256,512]{1,0:T(8,128)(2,1)}, u32[]{:S(2)}) copy-start(bf16[256,512]{1,0:T(8,128)(2,1)} %q_ref.9) | copy-start | bytes 786436
  34.4 6.3 %collective-permute-start.10 = (bf16[32,1024]{1,0:T(8,128)(2,1)S(1)}, bf16[32,1024]{1,0:T(8,128)(2,1)S(1)}, u32[]{:S(2)}, u32[]{:S(2)}) collective-permute-start(bf16[32,1024]{1,0:T(8,128)(2,1)S(1)} %fusion.34), channel_id=1, source_target_pairs={{0,8},{1,9},{2,10},{3,11},{4,12},{5,13},{6,14},{7,15},{8,0},{9,1},... | collective-permute-start | bytes 196616 | tf_op jit(solution)/shard_map/ppermute | solution.py:23
  37.1 5.6 %collective-permute-start.11 = (bf16[32,1024]{1,0:T(8,128)(2,1)S(1)}, bf16[32,1024]{1,0:T(8,128)(2,1)S(1)}, u32[]{:S(2)}, u32[]{:S(2)}) collective-permute-start(bf16[32,1024]{1,0:T(8,128)(2,1)S(1)} %fusion.34), channel_id=1, source_target_pairs={{0,12},{1,13},{2,14},{3,15},{4,8},{5,9},{6,10},{7,11},{8,4},{9,5},... | collective-permute-start | bytes 196616 | tf_op jit(solution)/shard_map/ppermute | solution.py:23
  48.4 5.1 %collective-permute-start.14 = (bf16[32,1024]{1,0:T(8,128)(2,1)S(1)}, bf16[32,1024]{1,0:T(8,128)(2,1)S(1)}, u32[]{:S(2)}, u32[]{:S(2)}) collective-permute-start(bf16[32,1024]{1,0:T(8,128)(2,1)S(1)} %get-tuple-element.64), channel_id=1, source_target_pairs={{0,12},{1,13},{2,14},{3,15},{4,8},{5,9},{6,10},{7,11},{8,4},{9,5},... | collective-permute-start | bytes 196616 | tf_op jit(solution)/shard_map/ppermute | solution.py:23
  49.8 5.7 %collective-permute-start.13 = (bf16[32,1024]{1,0:T(8,128)(2,1)S(1)}, bf16[32,1024]{1,0:T(8,128)(2,1)S(1)}, u32[]{:S(2)}, u32[]{:S(2)}) collective-permute-start(bf16[32,1024]{1,0:T(8,128)(2,1)S(1)} %get-tuple-element.63), channel_id=1, source_target_pairs={{0,8},{1,9},{2,10},{3,11},{4,12},{5,13},{6,14},{7,15},{8,0},{9,1},... | collective-permute-start | bytes 196616 | tf_op jit(solution)/shard_map/ppermute | solution.py:23
  49.8 5.8 %collective-permute-start.12 = (bf16[64,1024]{1,0:T(8,128)(2,1)S(1)}, bf16[64,1024]{1,0:T(8,128)(2,1)S(1)}, u32[]{:S(2)}, u32[]{:S(2)}) collective-permute-start(bf16[64,1024]{1,0:T(8,128)(2,1)S(1)} %slice.272), channel_id=1, source_target_pairs={{0,4},{1,5},{2,6},{3,7},{4,0},{5,1},{6,2},{7,3},{8,12},{9,13},{10,... | collective-permute-start | bytes 393224 | tf_op jit(solution)/shard_map/ppermute | solution.py:23
  55.8 6.2 %collective-permute-start.17 = (bf16[32,1024]{1,0:T(8,128)(2,1)S(1)}, bf16[32,1024]{1,0:T(8,128)(2,1)S(1)}, u32[]{:S(2)}, u32[]{:S(2)}) collective-permute-start(bf16[32,1024]{1,0:T(8,128)(2,1)S(1)} %get-tuple-element.51), channel_id=1, source_target_pairs={{0,3},{1,2},{2,1},{3,0},{4,7},{5,6},{6,5},{7,4},{8,11},{9,10},{10,... | collective-permute-start | bytes 196616 | tf_op jit(solution)/shard_map/ppermute | solution.py:23
  57.4 4.6 %collective-permute-start.16 = (bf16[32,1024]{1,0:T(8,128)(2,1)S(1)}, bf16[32,1024]{1,0:T(8,128)(2,1)S(1)}, u32[]{:S(2)}, u32[]{:S(2)}) collective-permute-start(bf16[32,1024]{1,0:T(8,128)(2,1)S(1)} %get-tuple-element.50), channel_id=1, source_target_pairs={{0,2},{1,3},{2,0},{3,1},{4,6},{5,7},{6,4},{7,5},{8,10},{9,11},{10,... | collective-permute-start | bytes 196616 | tf_op jit(solution)/shard_map/ppermute | solution.py:23
  58.2 4.2 %collective-permute-start.15 = (bf16[64,1024]{1,0:T(8,128)(2,1)S(1)}, bf16[64,1024]{1,0:T(8,128)(2,1)S(1)}, u32[]{:S(2)}, u32[]{:S(2)}) collective-permute-start(bf16[64,1024]{1,0:T(8,128)(2,1)S(1)} %fusion.9), channel_id=1, source_target_pairs={{0,1},{1,0},{2,3},{3,2},{4,5},{5,4},{6,7},{7,6},{8,9},{9,8},{10,11... | collective-permute-start | bytes 393224 | tf_op jit(solution)/shard_map/ppermute | solution.py:23
  62.1 0.8 copy-start.8
  63.4 8.4 %collective-permute-start.20 = (bf16[48,1024]{1,0:T(8,128)(2,1)S(1)}, bf16[48,1024]{1,0:T(8,128)(2,1)S(1)}, u32[]{:S(2)}, u32[]{:S(2)}) collective-permute-start(bf16[48,1024]{1,0:T(8,128)(2,1)S(1)} %pad_maximum_fusion.16), channel_id=1, source_target_pairs={{0,96},{16,112},{32,64},{48,80},{64,32},{80,48},{96,0},{112,16},{1... | collective-permute-start | bytes 294920 | tf_op jit(solution)/shard_map/ppermute | solution.py:23
  66.2 5.6 %collective-permute-start.19 = (bf16[48,1024]{1,0:T(8,128)(2,1)S(1)}, bf16[48,1024]{1,0:T(8,128)(2,1)S(1)}, u32[]{:S(2)}, u32[]{:S(2)}) collective-permute-start(bf16[48,1024]{1,0:T(8,128)(2,1)S(1)} %pad_maximum_fusion.15), channel_id=1, source_target_pairs={{0,64},{16,80},{32,96},{48,112},{64,0},{80,16},{96,32},{112,48},{1... | collective-permute-start | bytes 294920 | tf_op jit(solution)/shard_map/ppermute | solution.py:23
  66.7 6.1 %collective-permute-start.18 = (bf16[80,1024]{1,0:T(8,128)(2,1)S(1)}, bf16[80,1024]{1,0:T(8,128)(2,1)S(1)}, u32[]{:S(2)}, u32[]{:S(2)}) collective-permute-start(bf16[80,1024]{1,0:T(8,128)(2,1)S(1)} %pad_maximum_fusion.7), channel_id=1, source_target_pairs={{0,32},{16,48},{32,0},{48,16},{64,96},{80,112},{96,64},{112,80},{1... | collective-permute-start | bytes 491528 | tf_op jit(solution)/shard_map/ppermute | solution.py:23
  71.7 0.8 copy-start.4
  71.7 1.0 %copy-start.5 = (f32[256,512]{1,0:T(8,128)}, f32[256,512]{1,0:T(8,128)S(1)}, u32[]{:S(2)}) copy-start(f32[256,512]{1,0:T(8,128)S(1)} %get-tuple-element.41.gv_ref) | copy-start | bytes 1572868
  73.0 8.4 %collective-permute-start.21 = (bf16[72,1024]{1,0:T(8,128)(2,1)S(1)}, bf16[72,1024]{1,0:T(8,128)(2,1)S(1)}, u32[]{:S(2)}, u32[]{:S(2)}) collective-permute-start(bf16[72,1024]{1,0:T(8,128)(2,1)S(1)} %pad_maximum_fusion.8), channel_id=1, source_target_pairs={{0,16},{16,0},{32,48},{48,32},{64,80},{80,64},{96,112},{112,96},{1... | collective-permute-start | bytes 442376 | tf_op jit(solution)/shard_map/ppermute | solution.py:23
  81.4 7.6 %collective-permute-start.22 = (bf16[8,1024]{1,0:T(8,128)(2,1)S(1)}, bf16[8,1024]{1,0:T(8,128)(2,1)S(1)}, u32[]{:S(2)}, u32[]{:S(2)}) collective-permute-start(bf16[8,1024]{1,0:T(8,128)(2,1)S(1)} %fusion.55), channel_id=1, source_target_pairs={{0,128},{16,144},{32,160},{48,176},{64,192},{80,208},{96,224},{112... | collective-permute-start | bytes 49160 | tf_op jit(solution)/shard_map/ppermute | solution.py:23
  89.0 1.9 %copy-start.6 = (f32[256,512]{1,0:T(8,128)S(1)}, f32[256,512]{1,0:T(8,128)}, u32[]{:S(2)}) copy-start(f32[256,512]{1,0:T(8,128)} %get-tuple-element.47) | copy-start | bytes 1572868

commit v2 on v1

v2 whole, which is shorter than its diff:
```python
import functools

import jax
import jax.numpy as jnp
from jax import lax
from jax.experimental import pallas as pl
from jax.experimental.pallas import tpu as pltpu
from jax.sharding import PartitionSpec as P

F32 = jnp.float32
BF16 = jnp.bfloat16
D = 512
TOK = 256
PAIRS = 4
LANES = 128
SCALE = 64**-0.5
NT = (((1,), (1,)), ((), ()))
TN = (((0,), (0,)), ((), ()))


def flip(value, axis, mask):
    return lax.ppermute(value, axis, [(source, source ^ mask) for source in range(16)])


def reverse(number, bits):
    parts = [((number >> bit) & 1) << (bits - 1 - bit) for bit in range(bits)]
    return functools.reduce(jnp.bitwise_or, parts)


def iota(shape, dim):
    return lax.broadcasted_iota(jnp.int32, shape, dim)


def grouping(shape, row_dim):
    out, column = iota(shape, row_dim), iota(shape, 1 - row_dim)

    def choose(level2, x1, x2, x3, far):
        return jnp.where(
            column < 32, level2,
            jnp.where(column < 96, x1, jnp.where(column < 128, x2, jnp.where(column < 160, x3, far))),
        )

    place = column - choose(0, 32, 96, 128, 160)
    near, wide_core, far_core = place >> 4, place >> 5, (place >> 3) & 1
    core = choose(near, wide_core, near, near, far_core)
    row = jnp.where(column < 160, place & 3, reverse((place & 7) >> 1, 2))
    across = choose(0, 1, 2, 3, place >> 4)
    half = jnp.where(column < 160, 0, 1)
    weight = choose(0.25, 0.125, 0.25, 0.25, 0.5)
    return jnp.where(out == row * 16 + core * 8 + half * 4 + across, weight, 0.0).astype(BF16)


def two_heads(block):
    first = lax.broadcasted_iota(jnp.int32, block.shape, 1) < 64
    zero = jnp.zeros_like(block)
    return jnp.concatenate([jnp.where(first, block, zero), jnp.where(first, zero, block)], axis=0)


def dot(left, right, dims=(((1,), (0,)), ((), ()))):
    return lax.dot_general(left, right, dims, preferred_element_type=F32)


def pool_kernel(keys_ref, values_ref, zero_ref, one_ref, three_ref, keys, values, sems):
    moves = [
        pltpu.make_async_copy(source, target, sems.at[place])
        for place, (source, target) in enumerate(((keys_ref, keys), (values_ref, values)))
    ]
    for move in moves:
        move.start()
    place, token = iota((104, TOK), 0), iota((104, TOK), 1)
    row = jnp.where(place < 64, reverse(place, 6), jnp.where(place < 96, reverse(place, 5), place - 96))
    shift = jnp.where(place < 64, 2, jnp.where(place < 96, 3, 5))
    weight = jnp.where(place < 64, 1 / 4, jnp.where(place < 96, 1 / 8, 1 / 32))
    table = jnp.where((token >> shift) == row, weight, 0.0).astype(BF16)
    for half, (move, ref) in enumerate(zip(moves, (keys, values))):
        move.wait()
        pooled = dot(table, ref[...]).astype(BF16)
        columns = slice(half * D, (half + 1) * D)
        zero_ref[:, columns] = pooled[:64]
        one_ref[:, columns] = pooled[64:96]
        three_ref[:, columns] = pooled[96:104]


def group_kernel(level2_ref, far_ref, x1_ref, x2_ref, x3_ref, level4_ref, level5_ref, low_ref):
    low_ref[:64] = x1_ref[:64]
    low_ref[64:96] = x2_ref[:32]
    low_ref[96:128] = x3_ref[:32]
    low_ref[128:144] = far_ref[...]
    low_ref[144:160] = x1_ref[64:]
    low_ref[160:176] = x2_ref[32:]
    low_ref[176:] = x3_ref[32:]
    level4 = dot(grouping((64, 224), 0), jnp.concatenate([level2_ref[...], low_ref[...]], axis=0)).astype(BF16)
    level4_ref[...] = level4
    level5_ref[...] = (0.5 * (level4[:32].astype(F32) + level4[32:].astype(F32))).astype(BF16)


def pair_columns(index, step):
    return slice(index * LANES, (index + 1) * LANES)


def store_pair(ref, index, step, gk, gv):
    start = (pl.program_id(0) * step + index) * LANES
    ref[:, pl.ds(pl.multiple_of(start, LANES), LANES)] = gk.astype(ref.dtype)
    ref[:, pl.ds(pl.multiple_of(start + D, LANES), LANES)] = gv.astype(ref.dtype)


def stats_kernel(step, count, q_ref, do_ref, *refs):
    out_ref = refs[-1]
    for index in range(step):
        columns = pair_columns(index, step)
        q2 = two_heads(q_ref[:, columns] * SCALE)
        d2 = two_heads(do_ref[:, columns])
        scores = [dot(ref[:, columns], q2, NT) for ref in refs[:count]]
        dprobs = [dot(ref[:, columns], d2, NT) for ref in refs[count : 2 * count]]
        largest = functools.reduce(
            jnp.maximum, [jnp.max(part, axis=0, keepdims=True) for part in scores]
        )
        total, inner = 0.0, 0.0
        for score, dprob in zip(scores, dprobs):
            expsc = jnp.exp(score - largest)
            total = total + jnp.sum(expsc, axis=0, keepdims=True)
            inner = inner + jnp.sum(expsc * dprob, axis=0, keepdims=True)
        out_ref[index, 0:1] = largest
        out_ref[index, 1:2] = total
        out_ref[index, 2:3] = inner


def top_kernel(step, q_ref, do_ref, k_ref, v_ref, low_ref, g_ref, out_ref):
    for index in range(step):
        columns = pair_columns(index, step)
        q2 = two_heads(q_ref[:, columns] * SCALE)
        d2 = two_heads(do_ref[:, columns])
        scores = dot(k_ref[:, columns], q2, NT)
        dprobs = dot(v_ref[:, columns], d2, NT)
        low_largest = low_ref[index, 0:1]
        largest = jnp.maximum(jnp.max(scores, axis=0, keepdims=True), low_largest)
        expsc = jnp.exp(scores - largest)
        low_part = jnp.exp(low_largest - largest)
        total = jnp.sum(expsc, axis=0, keepdims=True) + low_ref[index, 1:2] * low_part
        inner = jnp.sum(expsc * dprobs, axis=0, keepdims=True) + low_ref[index, 2:3] * low_part
        share = 1.0 / total
        inner = inner * share
        out_ref[index, 0:1] = largest
        out_ref[index, 1:2] = share
        out_ref[index, 2:3] = inner
        probs = expsc * share
        dscores = (probs * (dprobs - inner)).astype(BF16)
        store_pair(g_ref, index, step, dot(dscores, q2), dot(probs.astype(BF16), d2))


def grads_kernel(step, wanted, first, last, q_ref, do_ref, stats_ref, *refs):
    refs = list(refs)
    blocks = [(refs.pop(0), refs.pop(0)) for unused in wanted]
    before = [] if first else [refs.pop(0), refs.pop(0)]
    refs.pop(0)
    mixed_ref, gq_ref = refs.pop(0), refs.pop(0)
    g_refs = [refs.pop(0) if want else None for want in wanted]
    for index in range(step):
        columns = pair_columns(index, step)
        q2 = two_heads(q_ref[:, columns] * SCALE)
        d2 = two_heads(do_ref[:, columns])
        mixed, gq = 0.0, 0.0
        for g_ref, (k_ref, v_ref) in zip(g_refs, blocks):
            k, v = k_ref[:, columns], v_ref[:, columns]
            probs = jnp.exp(dot(k, q2, NT) - stats_ref[index, 0:1]) * stats_ref[index, 1:2]
            dscores = (probs * (dot(v, d2, NT) - stats_ref[index, 2:3])).astype(BF16)
            weights = probs.astype(BF16)
            mixed, gq = mixed + dot(v, weights, TN), gq + dot(k, dscores, TN)
            if g_ref is not None:
                store_pair(g_ref, index, step, dot(dscores, q2), dot(weights, d2))

        def pick(both):
            return jnp.concatenate([both[:64, :TOK], both[64:, TOK:]], axis=0)

        mixed, gq = pick(mixed), pick(gq)
        if before:
            mixed, gq = mixed + before[0][index], gq + before[1][index]
        if last:
            mixed_ref[:, columns] = mixed.T.astype(BF16)
            gq_ref[:, columns] = (gq * SCALE).T.astype(BF16)
        else:
            mixed_ref[index] = mixed
            gq_ref[index] = gq


def ungroup_kernel(b1_ref, b2_ref, b3_ref, g6_ref, x_ref, x1_ref, x2_ref, x3_ref, level2_ref, far_ref):
    def doubled(rows):
        half = 0.5 * rows
        return jnp.concatenate([half, half], axis=0)

    g5 = doubled(g6_ref[:16]) + b2_ref[...].astype(F32) + b3_ref[...].astype(F32)
    g4 = b1_ref[...].astype(F32) + doubled(g5)
    g = dot(grouping((224, 64), 1), g4.astype(BF16))
    level2_ref[...] = g[:32]
    x = x_ref[...] + g[32:]
    x1_ref[:64] = x[:64].astype(BF16)
    x1_ref[64:] = x[144:160].astype(BF16)
    x2_ref[:32] = x[64:96].astype(BF16)
    x2_ref[32:] = x[160:176].astype(BF16)
    x3_ref[:32] = x[96:128].astype(BF16)
    x3_ref[32:] = x[176:].astype(BF16)
    far_ref[...] = x[128:144]


def finish_kernel(first_ref, second_ref, zero_ref, out_ref):
    place = reverse(iota((TOK, 64), 1), 6)
    unpooling = jnp.where((iota((TOK, 64), 0) >> 2) == place, 0.25, 0.0).astype(BF16)
    high = zero_ref[...].astype(BF16)
    low = (zero_ref[...] - high.astype(F32)).astype(BF16)
    for half, ref in enumerate((first_ref, second_ref)):
        rows = slice(half * TOK // 2, (half + 1) * TOK // 2)
        table = unpooling[rows]
        out_ref[rows] = ref[...] + dot(table, high) + dot(table, low)


def last_kernel(near_ref, part_ref, keys_ref, values_ref):
    part = part_ref[...].astype(F32) * (8 / TOK)
    for group in range(8):
        rows = slice(group * (TOK // 8), (group + 1) * (TOK // 8))
        total = (near_ref[rows] + part[group : group + 1]).astype(BF16)
        keys_ref[rows] = total[:, :D]
        values_ref[rows] = total[:, D:]


POOL_VMEM = 536 * 2**20 // 10
STEP = 2
TOP_STEP = 4


def of_pairs(rows, shift=0, step=STEP, part=0):
    return pl.BlockSpec((rows, LANES * step), lambda pair: (part, pair + shift // step))


def per_pair(rows, columns, step=STEP):
    return pl.BlockSpec((step, rows, columns), lambda pair: (pair, 0, 0))


def resident(rows, columns):
    return pl.BlockSpec((rows, columns), lambda pair: (0, 0))


STATS = jax.ShapeDtypeStruct((PAIRS, 8, 2 * TOK), F32)
PARTIAL = jax.ShapeDtypeStruct((PAIRS, LANES, TOK), F32)


def call(kernel, in_specs, out_specs, out_shape, flops, name, step=STEP):
    return pl.pallas_call(
        functools.partial(kernel, step),
        grid=(PAIRS // step,),
        in_specs=in_specs,
        out_specs=out_specs,
        out_shape=out_shape,
        compiler_params=pltpu.CompilerParams(vmem_limit_bytes=40 * 2**20),
        cost_estimate=pl.CostEstimate(flops=flops, bytes_accessed=2**20, transcendentals=0),
        name=name,
    )


def matmul_cost(keys, count):
    return 2 * count * keys * 2 * TOK * LANES * PAIRS


def key_specs(block, step=STEP, rows=None, part=0):
    keys, values = block
    shift = PAIRS if keys is values else 0
    rows = rows or keys.shape[0]
    return [of_pairs(rows, 0, step, part), of_pairs(rows, shift, step, part)]


def low_stats(queries, cotangent, blocks):
    specs = [key_specs(block) for block in blocks]
    rows = sum(block[0].shape[0] for block in blocks)

    def kernel(step, *refs):
        stats_kernel(step, len(blocks), *refs)

    return call(
        kernel,
        [of_pairs(TOK), of_pairs(TOK)]
        + [spec[0] for spec in specs]
        + [spec[1] for spec in specs],
        per_pair(8, 2 * TOK), STATS,
        matmul_cost(rows, 2), "low_stats",
    )(queries, cotangent, *[k for k, v in blocks], *[v for k, v in blocks])


def top_part(queries, cotangent, top, low):
    rows = top.shape[0]
    step = TOP_STEP
    return call(
        top_kernel,
        [of_pairs(TOK, 0, step), of_pairs(TOK, 0, step)]
        + key_specs((top, top), step)
        + [per_pair(8, 2 * TOK, step)],
        [resident(rows, 2 * D), per_pair(8, 2 * TOK, step)],
        [jax.ShapeDtypeStruct((rows, 2 * D), BF16), STATS],
        matmul_cost(rows, 4), "top_part", step,
    )(queries, cotangent, top, top, low)


def grads_part(queries, cotangent, stats, blocks, wanted, before, after, last, name):
    in_specs = [of_pairs(TOK), of_pairs(TOK), per_pair(8, 2 * TOK)]
    operands = [queries, cotangent, stats]
    out_specs = [of_pairs(TOK)] * 2 if last else [per_pair(LANES, TOK)] * 2
    out_shape = [jax.ShapeDtypeStruct((TOK, D), BF16)] * 2 if last else [PARTIAL] * 2
    total = 0
    for (keys, values, rows, part), want in zip(blocks, wanted):
        in_specs = in_specs + key_specs((keys, values), STEP, rows, part)
        operands += [keys, values]
        total += rows
        if want:
            out_specs = out_specs + [resident(rows, 2 * D)]
            out_shape = out_shape + [jax.ShapeDtypeStruct((rows, 2 * D), F32)]
    in_specs = in_specs + [per_pair(LANES, TOK)] * len(before) + [resident(8, LANES)]
    operands += [*before, after]

    def kernel(step, *refs):
        grads_kernel(step, wanted, not before, last, *refs)

    return call(kernel, in_specs, out_specs, out_shape, matmul_cost(total, 6), name)(*operands)


def wide(rows):
    return jax.ShapeDtypeStruct((rows, 2 * D), BF16)


def wide_f32(rows):
    return jax.ShapeDtypeStruct((rows, 2 * D), F32)


def pool(keys, values):
    return pl.pallas_call(
        pool_kernel,
        in_specs=[pl.BlockSpec(memory_space=pl.ANY)] * 2,
        out_specs=[pl.BlockSpec(memory_space=pltpu.VMEM)] * 3,
        out_shape=[wide(64), wide(32), wide(8)],
        scratch_shapes=[
            pltpu.VMEM((TOK, D), BF16),
            pltpu.VMEM((TOK, D), BF16),
            pltpu.SemaphoreType.DMA((2,)),
        ],
        compiler_params=pltpu.CompilerParams(vmem_limit_bytes=POOL_VMEM),
        name="pool",
    )(keys, values)


def whole(kernel, out_shape, name):
    return pl.pallas_call(
        kernel,
        out_shape=out_shape,
        compiler_params=pltpu.CompilerParams(vmem_limit_bytes=16 * 2**20),
        name=name,
    )


def halves(rows, parts=1):
    count, width = rows.shape
    split = rows.reshape(parts, 2, count // (2 * parts), width).astype(F32)
    return (0.5 * (split[:, 0] + split[:, 1])).astype(BF16).reshape(count // 2, width)


def spread(gradient, parts=1):
    count, width = gradient.shape
    split = (0.5 * gradient).reshape(parts, 1, count // parts, width)
    return jnp.concatenate([split, split], axis=1).reshape(2 * count, width)


def joined(*blocks):
    return jnp.concatenate(blocks, axis=0)


def shards(queries, keys, values, cotangent):
    zero, one, three = pool(keys, values)
    far = flip(three, "lo", 8)
    sec0 = flip(zero, "lo", 1)
    far_pair = joined(far, flip(far, "lo", 1))
    level1 = joined(one, halves(sec0))
    level2 = halves(level1, 2)
    short = joined(level2, far_pair)
    x1 = flip(joined(level1, far_pair), "lo", 2)
    x2 = flip(short, "lo", 4)
    x3 = flip(short, "lo", 6)
    level4, level5, low_x = whole(group_kernel, [wide(64), wide(32), wide(192)], "group")(
        level2, far_pair, x1, x2, x3
    )
    y1 = flip(level4, "hi", 1)
    y2 = flip(level5, "hi", 2)
    y3 = flip(level5, "hi", 3)
    low_y = joined(y1, y2, y3)
    level6 = joined(halves(level5), halves(halves(y1)), halves(y2), halves(y3))
    level7 = halves(level6, 4)
    z1 = flip(level6, "hi", 4)
    z2 = flip(level7, "hi", 8)
    z3 = flip(level7, "hi", 12)
    own, sec0_block = (keys, values), (sec0, sec0)
    low = low_stats(queries, cotangent, [own, sec0_block, (low_x, low_x), (low_y, low_y)])
    top = joined(z1, z2, z3)

    top_g, stats = top_part(queries, cotangent, top, low)
    b1 = flip(top_g[:64], "hi", 4)
    b2 = flip(top_g[64:96], "hi", 8)
    b3 = flip(top_g[96:], "hi", 12)
    mixed, gq, y_g = grads_part(
        queries, cotangent, stats, [(low_y, low_y, 128, 0), (top, top, 128, 0)], (True, False), [], stats[0],
        False, "y_grads",
    )
    g6 = b1.astype(F32) + spread(b2.astype(F32) + b3.astype(F32), 4)
    b1 = flip((y_g[:64] + spread(spread(g6[16:32]))).astype(BF16), "hi", 1)
    b2 = flip((y_g[64:96] + spread(g6[32:48])).astype(BF16), "hi", 2)
    b3 = flip((y_g[96:] + spread(g6[48:64])).astype(BF16), "hi", 3)
    mixed, gq, x_g, own_g = grads_part(
        queries, cotangent, stats,
        [(low_x, low_x, 192, 0), (keys, values, TOK // 2, 0)], (True,) * 2,
        [mixed, gq], g6, False, "x_grads",
    )
    x1, x2, x3, level2_g, far_g = whole(
        ungroup_kernel, [wide(80), wide(48), wide(48), wide_f32(32), wide_f32(16)], "ungroup"
    )(b1, b2, b3, g6, x_g)
    b1 = flip(x1, "lo", 2)
    b2 = flip(x2, "lo", 4)
    b3 = flip(x3, "lo", 6)
    mixed, grad_queries, sec0_g, rest_g = grads_part(
        queries, cotangent, stats, [(sec0, sec0, 64, 0), (keys, values, TOK // 2, 1)],
        (True,) * 2, [mixed, gq], far_g, True, "own_grads",
    )
    b1, b2, b3 = b1.astype(F32), b2.astype(F32), b3.astype(F32)
    g2 = level2_g + b2[:32] + b3[:32]
    far_g = far_g + b1[64:] + b2[32:] + b3[32:]
    g1 = b1[:64] + spread(g2, 2)
    back = flip(joined(sec0_g + spread(g1[32:]), far_g[8:]).astype(BF16), "lo", 1).astype(F32)
    g0 = back[:64] + spread(g1[:32])
    last = flip((far_g[:8] + back[64:]).astype(BF16), "lo", 8)
    near = whole(finish_kernel, jax.ShapeDtypeStruct((TOK, 2 * D), F32), "finish")(
        own_g, rest_g, g0
    )
    grad_keys, grad_values = whole(
        last_kernel, [jax.ShapeDtypeStruct((TOK, D), BF16)] * 2, "add_last"
    )(near, last)
    return (mixed, grad_queries, grad_keys, grad_values)


def solution(mesh):
    spec = P(("hi", "lo"), None)
    return jax.shard_map(
        shards, mesh=mesh, in_specs=(spec,) * 4, out_specs=(spec,) * 4, check_vma=False
    )
```

time: 92.2 us -> 79.4 us (0.86)
  other arithmetic: 4.38 us -> 0.77 us
  Pallas kernels: 20.7 us -> 17.1 us
  local copies, waits for them, and re-layouts: 3.12 us -> 0.14 us
  matrix products: 1.68 us -> 0 us
  starting transfers between devices: 43.8 us -> 42.4 us
  waiting for transfers between devices: 16.5 us -> 17.7 us
    pallas_call x7 -> x10, Pallas kernels: 20.7 us -> 17.1 us  [the longest x3 9.71 us: grads_part(): call(kernel, in_specs, out_specs, out_shape, matmul_cost(total, 6), name)]
    unnamed x49 -> x12, local copies, waits for them, and re-layouts: 2.98 us -> 0.05 us
    convert_element_type x6 -> x3, other arithmetic: 2.66 us -> 0.06 us  [the longest x1 0.03 us: shards(): b3 = flip((y_g[96:] + spread(g6[48:64])).astype(BF16), 'hi', 3)]
    dot_general x10 -> x0, matrix products: 1.68 us -> none  [dot(): return lax.dot_general(left, right, dims, preferred_element_type=F32)]
    ppermute x23, starting transfers between devices: 43.8 us -> 42.4 us  [flip(): lax.ppermute(value, axis, [(source, source ^ mask) for source in range(16)])]
    ppermute x23, waiting for transfers between devices: 16.5 us -> 17.7 us  [flip(): lax.ppermute(value, axis, [(source, source ^ mask) for source in range(16)])]
  transfers between devices with their start and end apart: 23 -> 23, of which waited for: 12 -> 14; matrix products, arithmetic and copies ran while one was open for 3% -> 1% of each run, Pallas kernels for 14% -> 16%
where the time goes in v2:
time: 79.4 us; the launch traced here: 79.3 us
  starting transfers between devices  42.4 us (53%)
  waiting for transfers between devices  17.7 us (22%)
  Pallas kernels  17.1 us (22%)
  between operations  1.16 us (1%)
    ppermute x23, starting transfers between devices, flip(): lax.ppermute(value, axis, [(source, source ^ mask) for source in range(16)])  42.4 us
    ppermute x23, waiting for transfers between devices, flip(): lax.ppermute(value, axis, [(source, source ^ mask) for source in range(16)])  17.7 us
    pallas_call x3, Pallas kernels, grads_part(): call(kernel, in_specs, out_specs, out_shape, matmul_cost(total, 6), name)  9.71 us
    pallas_call x1, Pallas kernels, low_stats(): call(kernel, [of_pairs(TOK), of_pairs(TOK)] + [spec[0] for spec in specs]...  2.8 us
  transfers between devices with their start and end apart: 23, of which 14 were waited for; matrix products, arithmetic and copies ran while one was open for 1% of the time, Pallas kernels for 16%

profile of v2, /device:TPU:1, one launch (start us, length us, event | category | flops | bytes accessed | tf_op | source)
XLA Modules:
  0.0 79.3 jit_solution(3462673251229471600)
XLA Ops:
  0.6 1.3 %pool.1 = (bf16[64,1024]{1,0:T(8,128)(2,1)S(1)}, bf16[32,1024]{1,0:T(8,128)(2,1)S(1)}, bf16[8,1024]{1,0:T(8,128)(2,1)S(1)}) custom-call(bf16[256,512]{1,0:T(8,128)(2,1)} %refs_5_.3, bf16[256,512]{1,0:T(8,128)(2,1)} %refs_6_.5), custom_call_target="tpu_custom_call" | custom-call | tf_op jit(solution)/shard_map/pool/pallas_call | solution.py:332
  2.0 3.3 %collective-permute-start = (bf16[64,1024]{1,0:T(8,128)(2,1)S(1)}, bf16[64,1024]{1,0:T(8,128)(2,1)S(1)}, u32[]{:S(2)}, u32[]{:S(2)}) collective-permute-start(bf16[64,1024]{1,0:T(8,128)(2,1)S(1)} %get-tuple-element.31), channel_id=1, source_target_pairs={{0,16},{16,0},{32,48},{48,32},{64,80},{80,64},{96,112},{112,96},{1... | collective-permute-start | bytes 393224 | tf_op jit(solution)/shard_map/ppermute | solution.py:22
  5.3 5.2 %collective-permute-start.1 = (bf16[8,1024]{1,0:T(8,128)(2,1)S(1)}, bf16[8,1024]{1,0:T(8,128)(2,1)S(1)}, u32[]{:S(2)}, u32[]{:S(2)}) collective-permute-start(bf16[8,1024]{1,0:T(8,128)(2,1)S(1)} %get-tuple-element.32), channel_id=1, source_target_pairs={{0,128},{16,144},{32,160},{48,176},{64,192},{80,208},{96,224},{112... | collective-permute-start | bytes 49160 | tf_op jit(solution)/shard_map/ppermute | solution.py:22
  10.5 1.3 %collective-permute-done.1 = bf16[8,1024]{1,0:T(8,128)(2,1)S(1)} collective-permute-done((bf16[8,1024]{1,0:T(8,128)(2,1)S(1)}, bf16[8,1024]{1,0:T(8,128)(2,1)S(1)}, u32[]{:S(2)}, u32[]{:S(2)}) %collective-permute-start.1) | collective-permute-done | bytes 16416 | tf_op jit(solution)/shard_map/ppermute | solution.py:22
  11.8 1.2 %collective-permute-start.2 = (bf16[8,1024]{1,0:T(8,128)(2,1)S(1)}, bf16[8,1024]{1,0:T(8,128)(2,1)S(1)}, u32[]{:S(2)}, u32[]{:S(2)}) collective-permute-start(bf16[8,1024]{1,0:T(8,128)(2,1)S(1)} %collective-permute-done.1), channel_id=1, source_target_pairs={{0,16},{16,0},{32,48},{48,32},{64,80},{80,64},{96,112},{112,96},{1... | collective-permute-start | bytes 49160 | tf_op jit(solution)/shard_map/ppermute | solution.py:22
  13.2 0.7 collective-permute-done.2
  13.9 0.8 %collective-permute-start.3 = (bf16[80,1024]{1,0:T(8,128)(2,1)S(1)}, bf16[80,1024]{1,0:T(8,128)(2,1)S(1)}, u32[]{:S(2)}, u32[]{:S(2)}) collective-permute-start(bf16[80,1024]{1,0:T(8,128)(2,1)S(1)} %pad_maximum_fusion.5), channel_id=1, source_target_pairs={{0,32},{16,48},{32,0},{48,16},{64,96},{80,112},{96,64},{112,80},{1... | collective-permute-start | bytes 491528 | tf_op jit(solution)/shard_map/ppermute | solution.py:22
  14.7 1.9 %collective-permute-start.5 = (bf16[48,1024]{1,0:T(8,128)(2,1)S(1)}, bf16[48,1024]{1,0:T(8,128)(2,1)S(1)}, u32[]{:S(2)}, u32[]{:S(2)}) collective-permute-start(bf16[48,1024]{1,0:T(8,128)(2,1)S(1)} %pad_maximum_fusion.11), channel_id=1, source_target_pairs={{0,96},{16,112},{32,64},{48,80},{64,32},{80,48},{96,0},{112,16},{1... | collective-permute-start | bytes 294920 | tf_op jit(solution)/shard_map/ppermute | solution.py:22
  16.6 0.7 collective-permute-start.4
  17.4 2.1 %collective-permute-done.5.x3_ref = bf16[48,1024]{1,0:T(8,128)(2,1)S(1)} collective-permute-done((bf16[48,1024]{1,0:T(8,128)(2,1)S(1)}, bf16[48,1024]{1,0:T(8,128)(2,1)S(1)}, u32[]{:S(2)}, u32[]{:S(2)}) %collective-permute-start.5) | collective-permute-done | bytes 98336 | tf_op jit(solution)/shard_map/ppermute | solution.py:22
  19.5 3.8 %collective-permute-done.4.x2_ref = bf16[48,1024]{1,0:T(8,128)(2,1)S(1)} collective-permute-done((bf16[48,1024]{1,0:T(8,128)(2,1)S(1)}, bf16[48,1024]{1,0:T(8,128)(2,1)S(1)}, u32[]{:S(2)}, u32[]{:S(2)}) %collective-permute-start.4) | collective-permute-done | bytes 98336 | tf_op jit(solution)/shard_map/ppermute | solution.py:22
  23.3 0.2 group.1
  23.5 3.0 %collective-permute-start.7 = (bf16[32,1024]{1,0:T(8,128)(2,1)S(1)}, bf16[32,1024]{1,0:T(8,128)(2,1)S(1)}, u32[]{:S(2)}, u32[]{:S(2)}) collective-permute-start(bf16[32,1024]{1,0:T(8,128)(2,1)S(1)} %get-tuple-element.33), channel_id=1, source_target_pairs={{0,2},{1,3},{2,0},{3,1},{4,6},{5,7},{6,4},{7,5},{8,10},{9,11},{10,... | collective-permute-start | bytes 196616 | tf_op jit(solution)/shard_map/ppermute | solution.py:22
  26.5 0.8 collective-permute-start.8
  27.3 0.1 collective-permute-start.6
  27.4 0.8 %collective-permute-done.7 = bf16[32,1024]{1,0:T(8,128)(2,1)S(1)} collective-permute-done((bf16[32,1024]{1,0:T(8,128)(2,1)S(1)}, bf16[32,1024]{1,0:T(8,128)(2,1)S(1)}, u32[]{:S(2)}, u32[]{:S(2)}) %collective-permute-start.7) | collective-permute-done | bytes 65568 | tf_op jit(solution)/shard_map/ppermute | solution.py:22
  28.2 2.6 %collective-permute-done.8 = bf16[32,1024]{1,0:T(8,128)(2,1)S(1)} collective-permute-done((bf16[32,1024]{1,0:T(8,128)(2,1)S(1)}, bf16[32,1024]{1,0:T(8,128)(2,1)S(1)}, u32[]{:S(2)}, u32[]{:S(2)}) %collective-permute-start.8) | collective-permute-done | bytes 65568 | tf_op jit(solution)/shard_map/ppermute | solution.py:22
  30.9 0.7 collective-permute-done.6
  31.7 0.8 %collective-permute-start.9 = (bf16[64,1024]{1,0:T(8,128)(2,1)S(1)}, bf16[64,1024]{1,0:T(8,128)(2,1)S(1)}, u32[]{:S(2)}, u32[]{:S(2)}) collective-permute-start(bf16[64,1024]{1,0:T(8,128)(2,1)S(1)} %pad_maximum_fusion.8), channel_id=1, source_target_pairs={{0,4},{1,5},{2,6},{3,7},{4,0},{5,1},{6,2},{7,3},{8,12},{9,13},{10,... | collective-permute-start | bytes 393224 | tf_op jit(solution)/shard_map/ppermute | solution.py:22
  32.6 0.0 copy-start
  32.6 2.5 %collective-permute-start.11 = (bf16[32,1024]{1,0:T(8,128)(2,1)S(1)}, bf16[32,1024]{1,0:T(8,128)(2,1)S(1)}, u32[]{:S(2)}, u32[]{:S(2)}) collective-permute-start(bf16[32,1024]{1,0:T(8,128)(2,1)S(1)} %fusion.18), channel_id=1, source_target_pairs={{0,12},{1,13},{2,14},{3,15},{4,8},{5,9},{6,10},{7,11},{8,4},{9,5},... | collective-permute-start | bytes 196616 | tf_op jit(solution)/shard_map/ppermute | solution.py:22
  35.1 0.4 collective-permute-start.10
  35.5 2.8 %low_stats.1.low_ref = f32[4,8,512]{2,1,0:T(8,128)S(1)} custom-call(bf16[256,512]{1,0:T(8,128)(2,1)S(1)} %copy-done, bf16[256,512]{1,0:T(8,128)(2,1)S(1)} %copy-done.1, bf16[256,512]{1,0:T(8,128)(2,1)S(1)} %copy-done.2, bf16[64,1024]{1,0:T(8,128)(2,1)S(1)} %collective-permute-done.refs_3_.refs_7_.refs_4_, ...), custom_call_target="tpu_custom_call" | custom-call | flops 671088640 | bytes 1048576 | tf_op jit(solution)/shard_map/low_stats/pallas_call | solution.py:277
  38.3 1.5 %collective-permute-done.10 = bf16[32,1024]{1,0:T(8,128)(2,1)S(1)} collective-permute-done((bf16[32,1024]{1,0:T(8,128)(2,1)S(1)}, bf16[32,1024]{1,0:T(8,128)(2,1)S(1)}, u32[]{:S(2)}, u32[]{:S(2)}) %collective-permute-start.10) | collective-permute-done | bytes 65568 | tf_op jit(solution)/shard_map/ppermute | solution.py:22
  39.9 1.5 %top_part.1 = (bf16[128,1024]{1,0:T(8,128)(2,1)S(1)}, f32[4,8,512]{2,1,0:T(8,128)S(1)}) custom-call(bf16[256,512]{1,0:T(8,128)(2,1)S(1)} %copy-done, bf16[256,512]{1,0:T(8,128)(2,1)S(1)} %copy-done.1, bf16[128,1024]{1,0:T(8,128)(2,1)S(1)} %constant_dynamic-update-slice_fusion.k_ref.v_ref.refs_5_.refs_6_, ...), custom_call_target="tpu_custom_call" | custom-call | flops 268435456 | bytes 1048576 | tf_op jit(solution)/shard_map/top_part/pallas_call | solution.py:290
  41.4 1.1 %collective-permute-start.13 = (bf16[32,1024]{1,0:T(8,128)(2,1)S(1)}, bf16[32,1024]{1,0:T(8,128)(2,1)S(1)}, u32[]{:S(2)}, u32[]{:S(2)}) collective-permute-start(bf16[32,1024]{1,0:T(8,128)(2,1)S(1)} %get-tuple-element.63), channel_id=1, source_target_pairs={{0,8},{1,9},{2,10},{3,11},{4,12},{5,13},{6,14},{7,15},{8,0},{9,1},... | collective-permute-start | bytes 196616 | tf_op jit(solution)/shard_map/ppermute | solution.py:22
  42.5 1.5 %collective-permute-start.14 = (bf16[32,1024]{1,0:T(8,128)(2,1)S(1)}, bf16[32,1024]{1,0:T(8,128)(2,1)S(1)}, u32[]{:S(2)}, u32[]{:S(2)}) collective-permute-start(bf16[32,1024]{1,0:T(8,128)(2,1)S(1)} %get-tuple-element.64), channel_id=1, source_target_pairs={{0,12},{1,13},{2,14},{3,15},{4,8},{5,9},{6,10},{7,11},{8,4},{9,5},... | collective-permute-start | bytes 196616 | tf_op jit(solution)/shard_map/ppermute | solution.py:22
  44.1 0.1 collective-permute-start.12
  44.2 2.8 %y_grads.1 = (f32[4,128,256]{2,1,0:T(8,128)S(1)}, f32[4,128,256]{2,1,0:T(8,128)S(1)}, f32[128,1024]{1,0:T(8,128)S(1)}) custom-call(bf16[256,512]{1,0:T(8,128)(2,1)S(1)} %copy-done, bf16[256,512]{1,0:T(8,128)(2,1)S(1)} %copy-done.1, f32[4,8,512]{2,1,0:T(8,128)S(1)} %get-tuple-element.36.refs_2_, ...), custom_call_target="tpu_custom_call" | custom-call | flops 805306368 | bytes 1048576 | tf_op jit(solution)/shard_map/y_grads/pallas_call | solution.py:320
  47.0 0.6 collective-permute-done.14
  47.7 0.9 %collective-permute-done.12 = bf16[64,1024]{1,0:T(8,128)(2,1)S(1)} collective-permute-done((bf16[64,1024]{1,0:T(8,128)(2,1)S(1)}, bf16[64,1024]{1,0:T(8,128)(2,1)S(1)}, u32[]{:S(2)}, u32[]{:S(2)}) %collective-permute-start.12) | collective-permute-done | bytes 131104 | tf_op jit(solution)/shard_map/ppermute | solution.py:22
  48.8 1.3 %collective-permute-start.15 = (bf16[64,1024]{1,0:T(8,128)(2,1)S(1)}, bf16[64,1024]{1,0:T(8,128)(2,1)S(1)}, u32[]{:S(2)}, u32[]{:S(2)}) collective-permute-start(bf16[64,1024]{1,0:T(8,128)(2,1)S(1)} %fusion.1), channel_id=1, source_target_pairs={{0,1},{1,0},{2,3},{3,2},{4,5},{5,4},{6,7},{7,6},{8,9},{9,8},{10,11... | collective-permute-start | bytes 393224 | tf_op jit(solution)/shard_map/ppermute | solution.py:22
  50.1 0.9 %collective-permute-start.17 = (bf16[32,1024]{1,0:T(8,128)(2,1)S(1)}, bf16[32,1024]{1,0:T(8,128)(2,1)S(1)}, u32[]{:S(2)}, u32[]{:S(2)}) collective-permute-start(bf16[32,1024]{1,0:T(8,128)(2,1)S(1)} %get-tuple-element.56), channel_id=1, source_target_pairs={{0,3},{1,2},{2,1},{3,0},{4,7},{5,6},{6,5},{7,4},{8,11},{9,10},{10,... | collective-permute-start | bytes 196616 | tf_op jit(solution)/shard_map/ppermute | solution.py:22
  51.0 1.2 %collective-permute-start.16 = (bf16[32,1024]{1,0:T(8,128)(2,1)S(1)}, bf16[32,1024]{1,0:T(8,128)(2,1)S(1)}, u32[]{:S(2)}, u32[]{:S(2)}) collective-permute-start(bf16[32,1024]{1,0:T(8,128)(2,1)S(1)} %get-tuple-element.57), channel_id=1, source_target_pairs={{0,2},{1,3},{2,0},{3,1},{4,6},{5,7},{6,4},{7,5},{8,10},{9,11},{10,... | collective-permute-start | bytes 196616 | tf_op jit(solution)/shard_map/ppermute | solution.py:22
  52.2 3.3 %x_grads.1 = (f32[4,128,256]{2,1,0:T(8,128)S(1)}, f32[4,128,256]{2,1,0:T(8,128)S(1)}, f32[192,1024]{1,0:T(8,128)S(1)}, f32[128,1024]{1,0:T(8,128)S(1)}) custom-call(bf16[256,512]{1,0:T(8,128)(2,1)S(1)} %copy-done, bf16[256,512]{1,0:T(8,128)(2,1)S(1)} %copy-done.1, f32[4,8,512]{2,1,0:T(8,128)S(1)} %get-tuple-element.36.refs_2_, ...), custom_call_target="tpu_custom_call" | custom-call | flops 1006632960 | bytes 1048576 | tf_op jit(solution)/shard_map/x_grads/pallas_call | solution.py:320
  55.5 0.2 collective-permute-done.16.b2_ref
  55.6 0.3 ungroup.1
  55.9 0.7 collective-permute-start.19
  56.6 1.8 %collective-permute-start.20 = (bf16[48,1024]{1,0:T(8,128)(2,1)S(1)}, bf16[48,1024]{1,0:T(8,128)(2,1)S(1)}, u32[]{:S(2)}, u32[]{:S(2)}) collective-permute-start(bf16[48,1024]{1,0:T(8,128)(2,1)S(1)} %get-tuple-element.53), channel_id=1, source_target_pairs={{0,96},{16,112},{32,64},{48,80},{64,32},{80,48},{96,0},{112,16},{1... | collective-permute-start | bytes 294920 | tf_op jit(solution)/shard_map/ppermute | solution.py:22
  58.4 0.2 collective-permute-start.18
  58.7 3.7 %own_grads.1 = (bf16[256,512]{1,0:T(8,128)(2,1)}, bf16[256,512]{1,0:T(8,128)(2,1)}, f32[64,1024]{1,0:T(8,128)S(1)}, f32[128,1024]{1,0:T(8,128)S(1)}) custom-call(bf16[256,512]{1,0:T(8,128)(2,1)S(1)} %copy-done, bf16[256,512]{1,0:T(8,128)(2,1)S(1)} %copy-done.1, f32[4,8,512]{2,1,0:T(8,128)S(1)} %get-tuple-element.36.refs_2_, ...), custom_call_target="tpu_custom_call" | custom-call | flops 603979776 | bytes 1048576 | tf_op jit(solution)/shard_map/own_grads/pallas_call | solution.py:320
  62.5 0.1 collective-permute-done.18
  62.8 8.0 %collective-permute-start.21 = (bf16[72,1024]{1,0:T(8,128)(2,1)S(1)}, bf16[72,1024]{1,0:T(8,128)(2,1)S(1)}, u32[]{:S(2)}, u32[]{:S(2)}) collective-permute-start(bf16[72,1024]{1,0:T(8,128)(2,1)S(1)} %pad_maximum_fusion.6), channel_id=1, source_target_pairs={{0,16},{16,0},{32,48},{48,32},{64,80},{80,64},{96,112},{112,96},{1... | collective-permute-start | bytes 442376 | tf_op jit(solution)/shard_map/ppermute | solution.py:22
  70.8 1.0 %collective-permute-done.21 = bf16[72,1024]{1,0:T(8,128)(2,1)S(1)} collective-permute-done((bf16[72,1024]{1,0:T(8,128)(2,1)S(1)}, bf16[72,1024]{1,0:T(8,128)(2,1)S(1)}, u32[]{:S(2)}, u32[]{:S(2)}) %collective-permute-start.21) | collective-permute-done | bytes 147488 | tf_op jit(solution)/shard_map/ppermute | solution.py:22
  71.9 4.8 %collective-permute-start.22 = (bf16[8,1024]{1,0:T(8,128)(2,1)S(1)}, bf16[8,1024]{1,0:T(8,128)(2,1)S(1)}, u32[]{:S(2)}, u32[]{:S(2)}) collective-permute-start(bf16[8,1024]{1,0:T(8,128)(2,1)S(1)} %fusion.34), channel_id=1, source_target_pairs={{0,128},{16,144},{32,160},{48,176},{64,192},{80,208},{96,224},{112... | collective-permute-start | bytes 49160 | tf_op jit(solution)/shard_map/ppermute | solution.py:22
  76.7 0.4 finish.1.near_ref
  77.1 1.3 %collective-permute-done.22.part_ref = bf16[8,1024]{1,0:T(8,128)(2,1)S(1)} collective-permute-done((bf16[8,1024]{1,0:T(8,128)(2,1)S(1)}, bf16[8,1024]{1,0:T(8,128)(2,1)S(1)}, u32[]{:S(2)}, u32[]{:S(2)}) %collective-permute-start.22) | collective-permute-done | bytes 16416 | tf_op jit(solution)/shard_map/ppermute | solution.py:22
  78.5 0.9 %add_last.1 = (bf16[256,512]{1,0:T(8,128)(2,1)}, bf16[256,512]{1,0:T(8,128)(2,1)}) custom-call(f32[256,1024]{1,0:T(8,128)S(1)} %finish.1.near_ref, bf16[8,1024]{1,0:T(8,128)(2,1)S(1)} %collective-permute-done.22.part_ref), custom_call_target="tpu_custom_call" | custom-call | tf_op jit(solution)/shard_map/add_last/pallas_call | solution.py:436
  (72 shorter events, 0.9 us)
Async XLA Ops:
  2.0 11.1 %collective-permute-start = (bf16[64,1024]{1,0:T(8,128)(2,1)S(1)}, bf16[64,1024]{1,0:T(8,128)(2,1)S(1)}, u32[]{:S(2)}, u32[]{:S(2)}) collective-permute-start(bf16[64,1024]{1,0:T(8,128)(2,1)S(1)} %get-tuple-element.31), channel_id=1, source_target_pairs={{0,16},{16,0},{32,48},{48,32},{64,80},{80,64},{96,112},{112,96},{1... | collective-permute-start | bytes 393224 | tf_op jit(solution)/shard_map/ppermute | solution.py:22
  5.3 6.5 %collective-permute-start.1 = (bf16[8,1024]{1,0:T(8,128)(2,1)S(1)}, bf16[8,1024]{1,0:T(8,128)(2,1)S(1)}, u32[]{:S(2)}, u32[]{:S(2)}) collective-permute-start(bf16[8,1024]{1,0:T(8,128)(2,1)S(1)} %get-tuple-element.32), channel_id=1, source_target_pairs={{0,128},{16,144},{32,160},{48,176},{64,192},{80,208},{96,224},{112... | collective-permute-start | bytes 49160 | tf_op jit(solution)/shard_map/ppermute | solution.py:22
  11.8 2.1 %collective-permute-start.2 = (bf16[8,1024]{1,0:T(8,128)(2,1)S(1)}, bf16[8,1024]{1,0:T(8,128)(2,1)S(1)}, u32[]{:S(2)}, u32[]{:S(2)}) collective-permute-start(bf16[8,1024]{1,0:T(8,128)(2,1)S(1)} %collective-permute-done.1), channel_id=1, source_target_pairs={{0,16},{16,0},{32,48},{48,32},{64,80},{80,64},{96,112},{112,96},{1... | collective-permute-start | bytes 49160 | tf_op jit(solution)/shard_map/ppermute | solution.py:22
  13.9 9.4 %collective-permute-start.3 = (bf16[80,1024]{1,0:T(8,128)(2,1)S(1)}, bf16[80,1024]{1,0:T(8,128)(2,1)S(1)}, u32[]{:S(2)}, u32[]{:S(2)}) collective-permute-start(bf16[80,1024]{1,0:T(8,128)(2,1)S(1)} %pad_maximum_fusion.5), channel_id=1, source_target_pairs={{0,32},{16,48},{32,0},{48,16},{64,96},{80,112},{96,64},{112,80},{1... | collective-permute-start | bytes 491528 | tf_op jit(solution)/shard_map/ppermute | solution.py:22
  14.7 4.8 %collective-permute-start.5 = (bf16[48,1024]{1,0:T(8,128)(2,1)S(1)}, bf16[48,1024]{1,0:T(8,128)(2,1)S(1)}, u32[]{:S(2)}, u32[]{:S(2)}) collective-permute-start(bf16[48,1024]{1,0:T(8,128)(2,1)S(1)} %pad_maximum_fusion.11), channel_id=1, source_target_pairs={{0,96},{16,112},{32,64},{48,80},{64,32},{80,48},{96,0},{112,16},{1... | collective-permute-start | bytes 294920 | tf_op jit(solution)/shard_map/ppermute | solution.py:22
  16.6 6.6 %collective-permute-start.4 = (bf16[48,1024]{1,0:T(8,128)(2,1)S(1)}, bf16[48,1024]{1,0:T(8,128)(2,1)S(1)}, u32[]{:S(2)}, u32[]{:S(2)}) collective-permute-start(bf16[48,1024]{1,0:T(8,128)(2,1)S(1)} %pad_maximum_fusion.11), channel_id=1, source_target_pairs={{0,64},{16,80},{32,96},{48,112},{64,0},{80,16},{96,32},{112,48},{1... | collective-permute-start | bytes 294920 | tf_op jit(solution)/shard_map/ppermute | solution.py:22
  23.5 4.7 %collective-permute-start.7 = (bf16[32,1024]{1,0:T(8,128)(2,1)S(1)}, bf16[32,1024]{1,0:T(8,128)(2,1)S(1)}, u32[]{:S(2)}, u32[]{:S(2)}) collective-permute-start(bf16[32,1024]{1,0:T(8,128)(2,1)S(1)} %get-tuple-element.33), channel_id=1, source_target_pairs={{0,2},{1,3},{2,0},{3,1},{4,6},{5,7},{6,4},{7,5},{8,10},{9,11},{10,... | collective-permute-start | bytes 196616 | tf_op jit(solution)/shard_map/ppermute | solution.py:22
  26.5 4.3 %collective-permute-start.8 = (bf16[32,1024]{1,0:T(8,128)(2,1)S(1)}, bf16[32,1024]{1,0:T(8,128)(2,1)S(1)}, u32[]{:S(2)}, u32[]{:S(2)}) collective-permute-start(bf16[32,1024]{1,0:T(8,128)(2,1)S(1)} %get-tuple-element.33), channel_id=1, source_target_pairs={{0,3},{1,2},{2,1},{3,0},{4,7},{5,6},{6,5},{7,4},{8,11},{9,10},{10,... | collective-permute-start | bytes 196616 | tf_op jit(solution)/shard_map/ppermute | solution.py:22
  27.3 4.3 %collective-permute-start.6 = (bf16[64,1024]{1,0:T(8,128)(2,1)S(1)}, bf16[64,1024]{1,0:T(8,128)(2,1)S(1)}, u32[]{:S(2)}, u32[]{:S(2)}) collective-permute-start(bf16[64,1024]{1,0:T(8,128)(2,1)S(1)} %get-tuple-element.34), channel_id=1, source_target_pairs={{0,1},{1,0},{2,3},{3,2},{4,5},{5,4},{6,7},{7,6},{8,9},{9,8},{10,11... | collective-permute-start | bytes 393224 | tf_op jit(solution)/shard_map/ppermute | solution.py:22
  31.7 6.6 %collective-permute-start.9 = (bf16[64,1024]{1,0:T(8,128)(2,1)S(1)}, bf16[64,1024]{1,0:T(8,128)(2,1)S(1)}, u32[]{:S(2)}, u32[]{:S(2)}) collective-permute-start(bf16[64,1024]{1,0:T(8,128)(2,1)S(1)} %pad_maximum_fusion.8), channel_id=1, source_target_pairs={{0,4},{1,5},{2,6},{3,7},{4,0},{5,1},{6,2},{7,3},{8,12},{9,13},{10,... | collective-permute-start | bytes 393224 | tf_op jit(solution)/shard_map/ppermute | solution.py:22
  32.5 2.9 %copy-start.3 = (bf16[256,512]{1,0:T(8,128)(2,1)S(1)}, bf16[256,512]{1,0:T(8,128)(2,1)}, u32[]{:S(2)}) copy-start(bf16[256,512]{1,0:T(8,128)(2,1)} %refs_6_.5) | copy-start | bytes 786436
  32.5 2.9 %copy-start.2 = (bf16[256,512]{1,0:T(8,128)(2,1)S(1)}, bf16[256,512]{1,0:T(8,128)(2,1)}, u32[]{:S(2)}) copy-start(bf16[256,512]{1,0:T(8,128)(2,1)} %refs_5_.3) | copy-start | bytes 786436
  32.6 2.9 %copy-start = (bf16[256,512]{1,0:T(8,128)(2,1)S(1)}, bf16[256,512]{1,0:T(8,128)(2,1)}, u32[]{:S(2)}) copy-start(bf16[256,512]{1,0:T(8,128)(2,1)} %refs_0_.7) | copy-start | bytes 786436
  32.6 2.9 %copy-start.1 = (bf16[256,512]{1,0:T(8,128)(2,1)S(1)}, bf16[256,512]{1,0:T(8,128)(2,1)}, u32[]{:S(2)}) copy-start(bf16[256,512]{1,0:T(8,128)(2,1)} %refs_1_.7) | copy-start | bytes 786436
  32.6 7.3 %collective-permute-start.11 = (bf16[32,1024]{1,0:T(8,128)(2,1)S(1)}, bf16[32,1024]{1,0:T(8,128)(2,1)S(1)}, u32[]{:S(2)}, u32[]{:S(2)}) collective-permute-start(bf16[32,1024]{1,0:T(8,128)(2,1)S(1)} %fusion.18), channel_id=1, source_target_pairs={{0,12},{1,13},{2,14},{3,15},{4,8},{5,9},{6,10},{7,11},{8,4},{9,5},... | collective-permute-start | bytes 196616 | tf_op jit(solution)/shard_map/ppermute | solution.py:22
  35.1 4.8 %collective-permute-start.10 = (bf16[32,1024]{1,0:T(8,128)(2,1)S(1)}, bf16[32,1024]{1,0:T(8,128)(2,1)S(1)}, u32[]{:S(2)}, u32[]{:S(2)}) collective-permute-start(bf16[32,1024]{1,0:T(8,128)(2,1)S(1)} %fusion.18), channel_id=1, source_target_pairs={{0,8},{1,9},{2,10},{3,11},{4,12},{5,13},{6,14},{7,15},{8,0},{9,1},... | collective-permute-start | bytes 196616 | tf_op jit(solution)/shard_map/ppermute | solution.py:22
  41.4 5.5 %collective-permute-start.13 = (bf16[32,1024]{1,0:T(8,128)(2,1)S(1)}, bf16[32,1024]{1,0:T(8,128)(2,1)S(1)}, u32[]{:S(2)}, u32[]{:S(2)}) collective-permute-start(bf16[32,1024]{1,0:T(8,128)(2,1)S(1)} %get-tuple-element.63), channel_id=1, source_target_pairs={{0,8},{1,9},{2,10},{3,11},{4,12},{5,13},{6,14},{7,15},{8,0},{9,1},... | collective-permute-start | bytes 196616 | tf_op jit(solution)/shard_map/ppermute | solution.py:22
  42.5 5.1 %collective-permute-start.14 = (bf16[32,1024]{1,0:T(8,128)(2,1)S(1)}, bf16[32,1024]{1,0:T(8,128)(2,1)S(1)}, u32[]{:S(2)}, u32[]{:S(2)}) collective-permute-start(bf16[32,1024]{1,0:T(8,128)(2,1)S(1)} %get-tuple-element.64), channel_id=1, source_target_pairs={{0,12},{1,13},{2,14},{3,15},{4,8},{5,9},{6,10},{7,11},{8,4},{9,5},... | collective-permute-start | bytes 196616 | tf_op jit(solution)/shard_map/ppermute | solution.py:22
  44.1 4.5 %collective-permute-start.12 = (bf16[64,1024]{1,0:T(8,128)(2,1)S(1)}, bf16[64,1024]{1,0:T(8,128)(2,1)S(1)}, u32[]{:S(2)}, u32[]{:S(2)}) collective-permute-start(bf16[64,1024]{1,0:T(8,128)(2,1)S(1)} %slice.132), channel_id=1, source_target_pairs={{0,4},{1,5},{2,6},{3,7},{4,0},{5,1},{6,2},{7,3},{8,12},{9,13},{10,... | collective-permute-start | bytes 393224 | tf_op jit(solution)/shard_map/ppermute | solution.py:22
  48.8 6.9 %collective-permute-start.15 = (bf16[64,1024]{1,0:T(8,128)(2,1)S(1)}, bf16[64,1024]{1,0:T(8,128)(2,1)S(1)}, u32[]{:S(2)}, u32[]{:S(2)}) collective-permute-start(bf16[64,1024]{1,0:T(8,128)(2,1)S(1)} %fusion.1), channel_id=1, source_target_pairs={{0,1},{1,0},{2,3},{3,2},{4,5},{5,4},{6,7},{7,6},{8,9},{9,8},{10,11... | collective-permute-start | bytes 393224 | tf_op jit(solution)/shard_map/ppermute | solution.py:22
  50.1 5.4 %collective-permute-start.17 = (bf16[32,1024]{1,0:T(8,128)(2,1)S(1)}, bf16[32,1024]{1,0:T(8,128)(2,1)S(1)}, u32[]{:S(2)}, u32[]{:S(2)}) collective-permute-start(bf16[32,1024]{1,0:T(8,128)(2,1)S(1)} %get-tuple-element.56), channel_id=1, source_target_pairs={{0,3},{1,2},{2,1},{3,0},{4,7},{5,6},{6,5},{7,4},{8,11},{9,10},{10,... | collective-permute-start | bytes 196616 | tf_op jit(solution)/shard_map/ppermute | solution.py:22
  51.0 4.6 %collective-permute-start.16 = (bf16[32,1024]{1,0:T(8,128)(2,1)S(1)}, bf16[32,1024]{1,0:T(8,128)(2,1)S(1)}, u32[]{:S(2)}, u32[]{:S(2)}) collective-permute-start(bf16[32,1024]{1,0:T(8,128)(2,1)S(1)} %get-tuple-element.57), channel_id=1, source_target_pairs={{0,2},{1,3},{2,0},{3,1},{4,6},{5,7},{6,4},{7,5},{8,10},{9,11},{10,... | collective-permute-start | bytes 196616 | tf_op jit(solution)/shard_map/ppermute | solution.py:22
  55.9 6.4 %collective-permute-start.19 = (bf16[48,1024]{1,0:T(8,128)(2,1)S(1)}, bf16[48,1024]{1,0:T(8,128)(2,1)S(1)}, u32[]{:S(2)}, u32[]{:S(2)}) collective-permute-start(bf16[48,1024]{1,0:T(8,128)(2,1)S(1)} %get-tuple-element.52), channel_id=1, source_target_pairs={{0,64},{16,80},{32,96},{48,112},{64,0},{80,16},{96,32},{112,48},{1... | collective-permute-start | bytes 294920 | tf_op jit(solution)/shard_map/ppermute | solution.py:22
  56.6 5.8 %collective-permute-start.20 = (bf16[48,1024]{1,0:T(8,128)(2,1)S(1)}, bf16[48,1024]{1,0:T(8,128)(2,1)S(1)}, u32[]{:S(2)}, u32[]{:S(2)}) collective-permute-start(bf16[48,1024]{1,0:T(8,128)(2,1)S(1)} %get-tuple-element.53), channel_id=1, source_target_pairs={{0,96},{16,112},{32,64},{48,80},{64,32},{80,48},{96,0},{112,16},{1... | collective-permute-start | bytes 294920 | tf_op jit(solution)/shard_map/ppermute | solution.py:22
  58.4 4.2 %collective-permute-start.18 = (bf16[80,1024]{1,0:T(8,128)(2,1)S(1)}, bf16[80,1024]{1,0:T(8,128)(2,1)S(1)}, u32[]{:S(2)}, u32[]{:S(2)}) collective-permute-start(bf16[80,1024]{1,0:T(8,128)(2,1)S(1)} %get-tuple-element.50), channel_id=1, source_target_pairs={{0,32},{16,48},{32,0},{48,16},{64,96},{80,112},{96,64},{112,80},{1... | collective-permute-start | bytes 491528 | tf_op jit(solution)/shard_map/ppermute | solution.py:22
  62.8 9.0 %collective-permute-start.21 = (bf16[72,1024]{1,0:T(8,128)(2,1)S(1)}, bf16[72,1024]{1,0:T(8,128)(2,1)S(1)}, u32[]{:S(2)}, u32[]{:S(2)}) collective-permute-start(bf16[72,1024]{1,0:T(8,128)(2,1)S(1)} %pad_maximum_fusion.6), channel_id=1, source_target_pairs={{0,16},{16,0},{32,48},{48,32},{64,80},{80,64},{96,112},{112,96},{1... | collective-permute-start | bytes 442376 | tf_op jit(solution)/shard_map/ppermute | solution.py:22
  71.9 6.6 %collective-permute-start.22 = (bf16[8,1024]{1,0:T(8,128)(2,1)S(1)}, bf16[8,1024]{1,0:T(8,128)(2,1)S(1)}, u32[]{:S(2)}, u32[]{:S(2)}) collective-permute-start(bf16[8,1024]{1,0:T(8,128)(2,1)S(1)} %fusion.34), channel_id=1, source_target_pairs={{0,128},{16,144},{32,160},{48,176},{64,192},{80,208},{96,224},{112... | collective-permute-start | bytes 49160 | tf_op jit(solution)/shard_map/ppermute | solution.py:22

commit v3 on v2

v3 whole, which is shorter than its diff:
```python
import functools

import jax
import jax.numpy as jnp
from jax import lax
from jax.experimental import pallas as pl
from jax.experimental.pallas import tpu as pltpu
from jax.sharding import PartitionSpec as P

F32 = jnp.float32
BF16 = jnp.bfloat16
D = 512
TOK = 256
PAIRS = 4
LANES = 128
SCALE = 64**-0.5
NT = (((1,), (1,)), ((), ()))
TN = (((0,), (0,)), ((), ()))


def flip(value, axis, mask):
    return lax.ppermute(value, axis, [(source, source ^ mask) for source in range(16)])


def reverse(number, bits):
    parts = [((number >> bit) & 1) << (bits - 1 - bit) for bit in range(bits)]
    return functools.reduce(jnp.bitwise_or, parts)


def iota(shape, dim):
    return lax.broadcasted_iota(jnp.int32, shape, dim)


def grouping(shape, row_dim):
    out, column = iota(shape, row_dim), iota(shape, 1 - row_dim)

    def choose(level2, x1, x2, x3, far):
        return jnp.where(
            column < 16, level2,
            jnp.where(column < 48, x1, jnp.where(column < 64, x2, jnp.where(column < 80, x3, far))),
        )

    place = column - choose(0, 16, 48, 64, 80)
    row = jnp.where(column < 80, place & 3, reverse((place & 7) >> 1, 2))
    across = choose(0, 1, 2, 3, place >> 3)
    half = jnp.where(column < 80, 0, 1)
    weight = choose(0.25, 0.125, 0.25, 0.25, 0.5)
    return jnp.where(out == row * 8 + half * 4 + across, weight, 0.0).astype(BF16)


def two_heads(block):
    first = lax.broadcasted_iota(jnp.int32, block.shape, 1) < 64
    zero = jnp.zeros_like(block)
    return jnp.concatenate([jnp.where(first, block, zero), jnp.where(first, zero, block)], axis=0)


def dot(left, right, dims=(((1,), (0,)), ((), ()))):
    return lax.dot_general(left, right, dims, preferred_element_type=F32)


def pool_kernel(keys_ref, values_ref, zero_ref, one_ref, two_ref, three_ref, keys, values, sems):
    moves = [
        pltpu.make_async_copy(source, target, sems.at[place])
        for place, (source, target) in enumerate(((keys_ref, keys), (values_ref, values)))
    ]
    for move in moves:
        move.start()
    place, token = iota((128, TOK), 0), iota((128, TOK), 1)

    def choose(zero, one, two, three):
        return jnp.where(
            place < 64, zero, jnp.where(place < 96, one, jnp.where(place < 112, two, three))
        )

    row = choose(reverse(place, 6), reverse(place, 5), reverse(place, 4), place - 112)
    weight = choose(1 / 4, 1 / 8, 1 / 16, 1 / 32)
    table = jnp.where((token >> choose(2, 3, 4, 5)) == row, weight, 0.0).astype(BF16)
    for half, (move, ref) in enumerate(zip(moves, (keys, values))):
        move.wait()
        pooled = dot(table, ref[...]).astype(BF16)
        columns = slice(half * D, (half + 1) * D)
        zero_ref[:, columns] = pooled[:64]
        one_ref[:, columns] = pooled[64:96]
        two_ref[:, columns] = pooled[96:112]
        three_ref[:, columns] = pooled[112:120]


def doubled(rows):
    half = 0.5 * rows
    return jnp.concatenate([half, half], axis=0)


def near_kernel(z3_ref, z2_ref, z1_ref, after_ref, out_ref):
    out_ref[:32] = z1_ref[...]
    out_ref[32:64] = z2_ref[...]
    out_ref[64:] = z3_ref[...]


def level6_kernel(level5_ref, y3_ref, y2_ref, y1_ref, low_ref, level6_ref):
    low_ref[:32] = y1_ref[...]
    low_ref[32:48] = y2_ref[...]
    low_ref[48:] = y3_ref[...]
    level6_ref[:8] = pair_mean(level5_ref[...])
    level6_ref[8:16] = pair_mean(pair_mean(y1_ref[...]))
    level6_ref[16:24] = pair_mean(y2_ref[...])
    level6_ref[24:] = pair_mean(y3_ref[...])


def pair_mean(rows):
    half = rows.shape[0] // 2
    return (0.5 * (rows[:half].astype(F32) + rows[half:].astype(F32))).astype(BF16)


def group_kernel(two_ref, far_ref, x3_ref, x2_ref, x1_ref, level4_ref, level5_ref, low_ref):
    low_ref[:32] = x1_ref[:32]
    low_ref[32:48] = x2_ref[:16]
    low_ref[48:64] = x3_ref[:16]
    low_ref[64:72] = far_ref[...]
    low_ref[72:80] = x1_ref[32:]
    low_ref[80:88] = x2_ref[16:]
    low_ref[88:] = x3_ref[16:]
    level4 = dot(grouping((32, 112), 0), jnp.concatenate([two_ref[...], low_ref[...]], axis=0)).astype(BF16)
    level4_ref[...] = level4
    level5_ref[...] = (0.5 * (level4[:16].astype(F32) + level4[16:].astype(F32))).astype(BF16)


def y_send_kernel(b3_ref, b2_ref, b1_ref, own_ref, other_ref, y1_ref, y2_ref, y3_ref, g6_ref):
    shared = 0.5 * (b2_ref[...].astype(F32) + b3_ref[...].astype(F32))
    for core, y_ref in enumerate((own_ref, other_ref)):
        wide_rows, rows = slice(core * 32, core * 32 + 32), slice(core * 16, core * 16 + 16)
        g6 = b1_ref[wide_rows].astype(F32) + shared
        g6_ref[wide_rows] = g6
        y1_ref[wide_rows] = (y_ref[:32] + doubled(doubled(g6[8:16]))).astype(BF16)
        y2_ref[rows] = (y_ref[32:48] + doubled(g6[16:24])).astype(BF16)
        y3_ref[rows] = (y_ref[48:] + doubled(g6[24:])).astype(BF16)


def x_send_kernel(b3_ref, b2_ref, b1_ref, g6_ref, own_ref, other_ref, x1_ref, x2_ref, x3_ref, two_ref, far_ref
):
    table = grouping((112, 32), 1)
    for core, x_ref in enumerate((own_ref, other_ref)):
        wide_rows, rows = slice(core * 32, core * 32 + 32), slice(core * 16, core * 16 + 16)
        g5 = doubled(g6_ref[core * 32 : core * 32 + 8])
        g5 = g5 + b2_ref[rows].astype(F32) + b3_ref[rows].astype(F32)
        g = dot(table, (b1_ref[wide_rows].astype(F32) + doubled(g5)).astype(BF16))
        two_ref[rows] = g[:16]
        x = x_ref[...] + g[16:]
        far = slice(core * 8, core * 8 + 8)
        x1_ref[wide_rows] = x[:32].astype(BF16)
        x1_ref[64 + core * 8 : 72 + core * 8] = x[72:80].astype(BF16)
        for ref, first, second in ((x2_ref, 32, 80), (x3_ref, 48, 88)):
            ref[rows] = x[first : first + 16].astype(BF16)
            ref[32 + core * 8 : 40 + core * 8] = x[second : second + 8].astype(BF16)
        far_ref[far] = x[64:72]


def core_send_kernel(b3_ref, b2_ref, b1_ref, two_ref, far_ref, zero_ref, out_ref, one_ref, own_far_ref):
    for core in range(2):
        wide_rows, rows = slice(core * 32, core * 32 + 32), slice(core * 16, core * 16 + 16)
        near, far = slice(core * 8, core * 8 + 8), slice(32 + core * 8, 40 + core * 8)
        two = two_ref[rows] + b2_ref[rows].astype(F32) + b3_ref[rows].astype(F32)
        one = doubled(b1_ref[wide_rows].astype(F32) + doubled(two))
        last = b2_ref[far].astype(F32) + b3_ref[far].astype(F32)
        last = last + far_ref[near] + b1_ref[64 + core * 8 : 72 + core * 8].astype(F32)
        if core == 0:
            one_ref[...] = one
            own_far_ref[...] = last
        else:
            out_ref[:64] = (zero_ref[...] + one).astype(BF16)
            out_ref[64:] = last.astype(BF16)


def of_pair(ref, pair, rows=slice(None), shift=0):
    return ref[rows, shift + pair * LANES : shift + (pair + 1) * LANES]


def of_block(refs, pair, rows):
    return of_pair(refs[0], pair, rows), of_pair(refs[-1], pair, rows, 2 * D // len(refs) - D)


def of_blocks(blocks, pair, rows):
    parts = [of_block(block, pair, part) for block, part in zip(blocks, rows)]
    return [jnp.concatenate(side, axis=0) for side in zip(*parts)]


def store_pair(ref, pair, gk, gv):
    ref[:, pair * LANES : (pair + 1) * LANES] = gk.astype(ref.dtype)
    ref[:, D + pair * LANES : D + (pair + 1) * LANES] = gv.astype(ref.dtype)


def take(refs, counts):
    refs = iter(refs)
    return [[next(refs) for unused in range(count)] for count in counts]


def stats_kernel(counts, q_ref, do_ref, *refs):
    out_ref = refs[-1]
    blocks = take(refs, counts)
    for pair in range(PAIRS):
        q2 = two_heads(of_pair(q_ref, pair) * SCALE)
        d2 = two_heads(of_pair(do_ref, pair))
        k, v = of_blocks(blocks, pair, [slice(None)] * len(blocks))
        scores = dot(k, q2, NT)
        largest = jnp.max(scores, axis=0, keepdims=True)
        expsc = jnp.exp(scores - largest)
        out_ref[pair, 0:1] = largest
        out_ref[pair, 1:2] = jnp.sum(expsc, axis=0, keepdims=True)
        out_ref[pair, 2:3] = jnp.sum(expsc * dot(v, d2, NT), axis=0, keepdims=True)


def top_kernel(q_ref, do_ref, top_ref, low_ref, z1_ref, z2_ref, z3_ref, out_ref):
    for pair in range(PAIRS):
        q2 = two_heads(of_pair(q_ref, pair) * SCALE)
        d2 = two_heads(of_pair(do_ref, pair))
        k, v = of_block([top_ref], pair, slice(None))
        scores = dot(k, q2, NT)
        dprobs = dot(v, d2, NT)
        low_largest = low_ref[pair, 0:1]
        largest = jnp.maximum(jnp.max(scores, axis=0, keepdims=True), low_largest)
        expsc = jnp.exp(scores - largest)
        low_part = jnp.exp(low_largest - largest)
        total = jnp.sum(expsc, axis=0, keepdims=True) + low_ref[pair, 1:2] * low_part
        inner = jnp.sum(expsc * dprobs, axis=0, keepdims=True) + low_ref[pair, 2:3] * low_part
        share = 1.0 / total
        inner = inner * share
        out_ref[pair, 0:1] = largest
        out_ref[pair, 1:2] = share
        out_ref[pair, 2:3] = inner
        probs = expsc * share
        dscores = (probs * (dprobs - inner)).astype(BF16)
        gk, gv = dot(dscores, q2), dot(probs.astype(BF16), d2)
        store_pair(z1_ref, pair, gk[:64], gv[:64])
        store_pair(z2_ref, pair, gk[64:96], gv[64:96])
        store_pair(z3_ref, pair, gk[96:], gv[96:])


def grads_kernel(counts, rows, first, last, q_ref, do_ref, stats_ref, *refs):
    blocks = take(refs, counts)
    rest = list(refs[sum(counts) :])
    before = [] if first else [rest.pop(0), rest.pop(0)]
    rest.pop(0)
    mixed_ref, gq_ref = rest.pop(0), rest.pop(0)
    g_refs = rest
    for pair in range(PAIRS):
        q2 = two_heads(of_pair(q_ref, pair) * SCALE)
        d2 = two_heads(of_pair(do_ref, pair))
        k, v = of_blocks(blocks, pair, rows)
        probs = jnp.exp(dot(k, q2, NT) - stats_ref[pair, 0:1]) * stats_ref[pair, 1:2]
        dscores = (probs * (dot(v, d2, NT) - stats_ref[pair, 2:3])).astype(BF16)
        weights = probs.astype(BF16)
        mixed, gq = dot(v, weights, TN), dot(k, dscores, TN)
        count = sum(ref.shape[0] for ref in g_refs)
        gk, gv, start = dot(dscores[:count], q2), dot(weights[:count], d2), 0
        for ref in g_refs:
            store_pair(ref, pair, gk[start : start + ref.shape[0]], gv[start : start + ref.shape[0]])
            start += ref.shape[0]

        def pick(both):
            return jnp.concatenate([both[:64, :TOK], both[64:, TOK:]], axis=0)

        mixed, gq = pick(mixed), pick(gq)
        if before:
            mixed, gq = mixed + before[0][pair], gq + before[1][pair]
        if last:
            columns = slice(pair * LANES, (pair + 1) * LANES)
            mixed_ref[:, columns] = mixed.T.astype(BF16)
            gq_ref[:, columns] = (gq * SCALE).T.astype(BF16)
        else:
            mixed_ref[pair] = mixed
            gq_ref[pair] = gq


def finish_kernel(first_ref, second_ref, zero_ref, out_ref):
    place = reverse(iota((TOK, 64), 1), 6)
    unpooling = jnp.where((iota((TOK, 64), 0) >> 2) == place, 0.25, 0.0).astype(BF16)
    high = zero_ref[...].astype(BF16)
    low = (zero_ref[...] - high.astype(F32)).astype(BF16)
    for half, ref in enumerate((first_ref, second_ref)):
        rows = slice(half * TOK // 2, (half + 1) * TOK // 2)
        table = unpooling[rows]
        out_ref[rows] = ref[...] + dot(table, high) + dot(table, low)


def last_kernel(near_ref, part_ref, keys_ref, values_ref):
    part = part_ref[...].astype(F32) * (8 / TOK)
    for group in range(8):
        rows = slice(group * (TOK // 8), (group + 1) * (TOK // 8))
        total = (near_ref[rows] + part[group : group + 1]).astype(BF16)
        keys_ref[rows] = total[:, :D]
        values_ref[rows] = total[:, D:]


POOL_VMEM = 536 * 2**20 // 10
STATS = jax.ShapeDtypeStruct((PAIRS, 8, 2 * TOK), F32)
PARTIAL = jax.ShapeDtypeStruct((PAIRS, LANES, TOK), F32)


def call(kernel, operands, out_shape, flops, name, ordered=False):
    in_specs = [pl.BlockSpec(memory_space=pltpu.VMEM)] * len(operands)
    if ordered:
        in_specs[-1] = pl.BlockSpec(memory_space=pl.ANY)
    return pl.pallas_call(
        kernel,
        in_specs=in_specs,
        out_shape=out_shape,
        compiler_params=pltpu.CompilerParams(vmem_limit_bytes=40 * 2**20),
        cost_estimate=pl.CostEstimate(flops=flops, bytes_accessed=2**20, transcendentals=0),
        name=name,
    )(*operands)


def matmul_cost(keys, count):
    return 2 * count * keys * 2 * TOK * LANES * PAIRS


def low_stats(queries, cotangent, blocks):
    return call(
        functools.partial(stats_kernel, [len(block) for block in blocks]),
        [queries, cotangent] + [array for block in blocks for array in block],
        STATS, matmul_cost(5 * LANES, 2), "low_stats",
    )


def top_part(queries, cotangent, top, low):
    rows = top.shape[0]
    return call(
        top_kernel, [queries, cotangent, top, low], [wide(64), wide(32), wide(32), STATS],
        matmul_cost(rows, 4), "top_part",
    )


def grads_part(queries, cotangent, stats, blocks, wanted, before, after, last, name):
    operands = [queries, cotangent, stats]
    out_shape = [jax.ShapeDtypeStruct((TOK, D), BF16)] * 2 if last else [PARTIAL] * 2
    counts, rows, total = [], [], 0
    for (arrays, start, size), want in zip(blocks, wanted):
        operands += arrays
        counts.append(len(arrays))
        rows.append(slice(start, start + size))
        total += size
        if want:
            out_shape = out_shape + [jax.ShapeDtypeStruct((size, 2 * D), want)]
    return call(
        functools.partial(grads_kernel, counts, rows, not before, last),
        operands + [*before, after], out_shape, matmul_cost(total, 6), name, True,
    )


def wide(rows):
    return jax.ShapeDtypeStruct((rows, 2 * D), BF16)


def wide_f32(rows):
    return jax.ShapeDtypeStruct((rows, 2 * D), F32)


def pool(keys, values):
    return pl.pallas_call(
        pool_kernel,
        in_specs=[pl.BlockSpec(memory_space=pl.ANY)] * 2,
        out_specs=[pl.BlockSpec(memory_space=pltpu.VMEM)] * 4,
        out_shape=[wide(64), wide(32), wide(16), wide(8)],
        scratch_shapes=[
            pltpu.VMEM((TOK, D), BF16),
            pltpu.VMEM((TOK, D), BF16),
            pltpu.SemaphoreType.DMA((2,)),
        ],
        compiler_params=pltpu.CompilerParams(vmem_limit_bytes=POOL_VMEM),
        name="pool",
    )(keys, values)


def whole(kernel, out_shape, name, ordered=None):
    extra = {} if ordered is None else {
        "in_specs": [pl.BlockSpec(memory_space=pltpu.VMEM)] * ordered + [pl.BlockSpec(memory_space=pl.ANY)]
    }
    return pl.pallas_call(
        kernel,
        out_shape=out_shape,
        compiler_params=pltpu.CompilerParams(vmem_limit_bytes=16 * 2**20),
        name=name,
        **extra,
    )


def mean(one, two):
    return (0.5 * (one.astype(F32) + two.astype(F32))).astype(BF16)


def joined(*blocks):
    return jnp.concatenate(blocks, axis=0)


def other_core(value):
    return flip(value, "lo", 1)


def shards(queries, keys, values, cotangent):
    zero, one, two, three = pool(keys, values)
    far = flip(three, "lo", 8)
    sec0 = other_core(zero)
    short = joined(two, far)
    x1 = flip(joined(one, far), "lo", 2)
    x2 = flip(short, "lo", 4)
    x3 = flip(short, "lo", 6)
    level4, level5, low_x = whole(group_kernel, [wide(32), wide(16), wide(96)], "group")(
        two, far, x3, x2, x1
    )
    y1 = flip(level4, "hi", 1)
    y2 = flip(level5, "hi", 2)
    y3 = flip(level5, "hi", 3)
    low_x2 = other_core(low_x)
    low_y, level6 = whole(level6_kernel, [wide(64), wide(32)], "level6")(level5, y3, y2, y1)
    z1 = flip(level6, "hi", 4)
    z2 = flip(level6, "hi", 8)
    z3 = flip(level6, "hi", 12)
    low_y2 = other_core(low_y)
    low = low_stats(
        queries, cotangent,
        [(keys, values)] + [(rows,) for rows in (sec0, low_x, low_x2, low_y, low_y2)],
    )
    near = whole(near_kernel, wide(96), "near", 3)(z3, z2, z1, low)
    mate = other_core(near)
    top = joined(near[:32], mate[:32], mean(near[32:], mate[32:]))

    z1, z2, z3, stats = top_part(queries, cotangent, top, low)
    b1 = flip(z1, "hi", 4)
    b2 = flip(z2, "hi", 8)
    b3 = flip(z3, "hi", 12)
    mixed, gq, y_g, y_other = grads_part(
        queries, cotangent, stats, [([low_y], 0, 64), ([low_y2], 0, 64), ([top], 0, 128)],
        (F32, F32, None), [], z1, False, "y_grads",
    )
    y1, y2, y3, g6 = whole(y_send_kernel, [wide(64), wide(32), wide(32), wide_f32(64)], "y_send")(
        b3, b2, b1, y_g, y_other
    )
    b1 = flip(y1, "hi", 1)
    b2 = flip(y2, "hi", 2)
    b3 = flip(y3, "hi", 3)
    mixed, gq, x_g, x_other, first_g = grads_part(
        queries, cotangent, stats,
        [([low_x], 0, 96), ([low_x2], 0, 96), ([keys, values], 0, TOK // 2)],
        (F32,) * 3, [mixed, gq], y1, False, "x_grads",
    )
    x1, x2, x3, two_g, far_g = whole(
        x_send_kernel, [wide(80), wide(48), wide(48), wide_f32(32), wide_f32(16)], "x_send"
    )(b3, b2, b1, g6, x_g, x_other)
    b1 = flip(x1, "lo", 2)
    b2 = flip(x2, "lo", 4)
    b3 = flip(x3, "lo", 6)
    mixed, grad_queries, sec0_g, second_g = grads_part(
        queries, cotangent, stats, [([sec0], 0, 64), ([keys, values], TOK // 2, TOK // 2)],
        (F32,) * 2, [mixed, gq], x1, True, "own_grads",
    )
    mate_g, one_g, far_g = whole(core_send_kernel, [wide(72), wide_f32(64), wide_f32(8)], "core_send")(
        b3, b2, b1, two_g, far_g, sec0_g
    )
    back = other_core(mate_g).astype(F32)
    last = flip((far_g + back[64:]).astype(BF16), "lo", 8)
    near = whole(finish_kernel, jax.ShapeDtypeStruct((TOK, 2 * D), F32), "finish")(
        first_g, second_g, back[:64] + one_g
    )
    grad_keys, grad_values = whole(
        last_kernel, [jax.ShapeDtypeStruct((TOK, D), BF16)] * 2, "add_last"
    )(near, last)
    return (mixed, grad_queries, grad_keys, grad_values)


def solution(mesh):
    spec = P(("hi", "lo"), None)
    return jax.shard_map(
        shards, mesh=mesh, in_specs=(spec,) * 4, out_specs=(spec,) * 4, check_vma=False
    )
```

time: 79.4 us -> 78.1 us (0.984)
  Pallas kernels: 17.1 us -> 13.5 us
  waiting for transfers between devices: 17.7 us -> 20.9 us
    pallas_call x7 -> x11, Pallas kernels: 14.5 us -> 10.8 us  [the longest x5 10.1 us: call(): pl.pallas_call(kernel, in_specs=in_specs, out_shape=out_shape, compiler_p...]
    ppermute x23 -> x25, waiting for transfers between devices: 17.7 us -> 20.9 us  [flip(): lax.ppermute(value, axis, [(source, source ^ mask) for source in range(16)])]
    ppermute x23 -> x25, starting transfers between devices: 42.4 us -> 42.7 us  [flip(): lax.ppermute(value, axis, [(source, source ^ mask) for source in range(16)])]
  transfers between devices with their start and end apart: 23 -> 25, of which waited for: 14 -> 13; matrix products, arithmetic and copies ran while one was open for 1% -> 0% of each run, Pallas kernels for 16% -> 12%
where the time goes in v3:
time: 78.1 us; the launch traced here: 78 us
  starting transfers between devices  42.7 us (55%)
  waiting for transfers between devices  20.9 us (27%)
  Pallas kernels  13.5 us (17%)
  between operations  0.83 us (1%)
    ppermute x25, starting transfers between devices, flip(): lax.ppermute(value, axis, [(source, source ^ mask) for source in range(16)])  42.7 us
    ppermute x25, waiting for transfers between devices, flip(): lax.ppermute(value, axis, [(source, source ^ mask) for source in range(16)])  20.9 us
    pallas_call x5, Pallas kernels, call(): pl.pallas_call(kernel, in_specs=in_specs, out_shape=out_shape, compiler_p...  10.1 us
  transfers between devices with their start and end apart: 25, of which 13 were waited for; matrix products, arithmetic and copies ran while one was open for 0% of the time, Pallas kernels for 12%

profile of v3, /device:TPU:1, one launch (start us, length us, event | category | flops | bytes accessed | tf_op | source)
XLA Modules:
  0.0 78.0 jit_solution(16319038272034511251)
XLA Ops:
  0.7 1.4 %pool.1 = (bf16[64,1024]{1,0:T(8,128)(2,1)S(1)}, bf16[32,1024]{1,0:T(8,128)(2,1)S(1)}, bf16[16,1024]{1,0:T(8,128)(2,1)S(1)}, bf16[8,1024]{1,0:T(8,128)(2,1)S(1)}) custom-call(bf16[256,512]{1,0:T(8,128)(2,1)} %refs_1_.3, bf16[256,512]{1,0:T(8,128)(2,1)} %refs_2_.3), custom_call_target="tpu_custom_call" | custom-call | tf_op jit(solution)/shard_map/pool/pallas_call | solution.py:358
  2.1 7.8 %collective-permute-start = (bf16[8,1024]{1,0:T(8,128)(2,1)S(1)}, bf16[8,1024]{1,0:T(8,128)(2,1)S(1)}, u32[]{:S(2)}, u32[]{:S(2)}) collective-permute-start(bf16[8,1024]{1,0:T(8,128)(2,1)S(1)} %get-tuple-element.45), channel_id=1, source_target_pairs={{0,128},{16,144},{32,160},{48,176},{64,192},{80,208},{96,224},{112... | collective-permute-start | bytes 49160 | tf_op jit(solution)/shard_map/ppermute | solution.py:22
  9.9 1.1 %collective-permute-done.far_ref = bf16[8,1024]{1,0:T(8,128)(2,1)S(1)} collective-permute-done((bf16[8,1024]{1,0:T(8,128)(2,1)S(1)}, bf16[8,1024]{1,0:T(8,128)(2,1)S(1)}, u32[]{:S(2)}, u32[]{:S(2)}) %collective-permute-start) | collective-permute-done | bytes 16416 | tf_op jit(solution)/shard_map/ppermute | solution.py:22
  11.0 1.3 %collective-permute-start.3 = (bf16[40,1024]{1,0:T(8,128)(2,1)S(1)}, bf16[40,1024]{1,0:T(8,128)(2,1)S(1)}, u32[]{:S(2)}, u32[]{:S(2)}) collective-permute-start(bf16[40,1024]{1,0:T(8,128)(2,1)S(1)} %pad_maximum_fusion.1), channel_id=1, source_target_pairs={{0,32},{16,48},{32,0},{48,16},{64,96},{80,112},{96,64},{112,80},{1... | collective-permute-start | bytes 245768 | tf_op jit(solution)/shard_map/ppermute | solution.py:22
  12.3 1.8 %collective-permute-start.1 = (bf16[24,1024]{1,0:T(8,128)(2,1)S(1)}, bf16[24,1024]{1,0:T(8,128)(2,1)S(1)}, u32[]{:S(2)}, u32[]{:S(2)}) collective-permute-start(bf16[24,1024]{1,0:T(8,128)(2,1)S(1)} %constant_dynamic-update-slice_fusion), channel_id=1, source_target_pairs={{0,96},{16,112},{32,64},{48,80},{64,32},{80,48},{96,0},{112,16},{1... | collective-permute-start | bytes 147464 | tf_op jit(solution)/shard_map/ppermute | solution.py:22
  14.2 0.6 collective-permute-start.2
  14.8 1.7 %collective-permute-done.1.x3_ref = bf16[24,1024]{1,0:T(8,128)(2,1)S(1)} collective-permute-done((bf16[24,1024]{1,0:T(8,128)(2,1)S(1)}, bf16[24,1024]{1,0:T(8,128)(2,1)S(1)}, u32[]{:S(2)}, u32[]{:S(2)}) %collective-permute-start.1) | collective-permute-done | bytes 49184 | tf_op jit(solution)/shard_map/ppermute | solution.py:22
  16.5 2.6 %collective-permute-done.2.x2_ref = bf16[24,1024]{1,0:T(8,128)(2,1)S(1)} collective-permute-done((bf16[24,1024]{1,0:T(8,128)(2,1)S(1)}, bf16[24,1024]{1,0:T(8,128)(2,1)S(1)}, u32[]{:S(2)}, u32[]{:S(2)}) %collective-permute-start.2) | collective-permute-done | bytes 49184 | tf_op jit(solution)/shard_map/ppermute | solution.py:22
  19.1 0.2 group.1
  19.3 1.4 %collective-permute-start.6 = (bf16[32,1024]{1,0:T(8,128)(2,1)S(1)}, bf16[32,1024]{1,0:T(8,128)(2,1)S(1)}, u32[]{:S(2)}, u32[]{:S(2)}) collective-permute-start(bf16[32,1024]{1,0:T(8,128)(2,1)S(1)} %get-tuple-element.48), channel_id=1, source_target_pairs={{0,1},{1,0},{2,3},{3,2},{4,5},{5,4},{6,7},{7,6},{8,9},{9,8},{10,11... | collective-permute-start | bytes 196616 | tf_op jit(solution)/shard_map/ppermute | solution.py:22
  20.7 3.0 %collective-permute-start.11 = (bf16[96,1024]{1,0:T(8,128)(2,1)S(1)}, bf16[96,1024]{1,0:T(8,128)(2,1)S(1)}, u32[]{:S(2)}, u32[]{:S(2)}) collective-permute-start(bf16[96,1024]{1,0:T(8,128)(2,1)S(1)} %get-tuple-element.51.refs_3_.refs_0_), channel_id=1, source_target_pairs={{0,16},{16,0},{32,48},{48,32},{64,80},{80,64},{96,112},{112,96},{1... | collective-permute-start | bytes 589832 | tf_op jit(solution)/shard_map/ppermute | solution.py:22
  23.7 1.9 %collective-permute-start.4 = (bf16[16,1024]{1,0:T(8,128)(2,1)S(1)}, bf16[16,1024]{1,0:T(8,128)(2,1)S(1)}, u32[]{:S(2)}, u32[]{:S(2)}) collective-permute-start(bf16[16,1024]{1,0:T(8,128)(2,1)S(1)} %get-tuple-element.47.level5_ref), channel_id=1, source_target_pairs={{0,3},{1,2},{2,1},{3,0},{4,7},{5,6},{6,5},{7,4},{8,11},{9,10},{10,... | collective-permute-start | bytes 98312 | tf_op jit(solution)/shard_map/ppermute | solution.py:22
  25.6 0.7 collective-permute-start.5
  26.3 0.3 collective-permute-start.10
  26.6 1.1 %collective-permute-done.4.y3_ref = bf16[16,1024]{1,0:T(8,128)(2,1)S(1)} collective-permute-done((bf16[16,1024]{1,0:T(8,128)(2,1)S(1)}, bf16[16,1024]{1,0:T(8,128)(2,1)S(1)}, u32[]{:S(2)}, u32[]{:S(2)}) %collective-permute-start.4) | collective-permute-done | bytes 32800 | tf_op jit(solution)/shard_map/ppermute | solution.py:22
  27.7 2.2 %collective-permute-done.5.y2_ref = bf16[16,1024]{1,0:T(8,128)(2,1)S(1)} collective-permute-done((bf16[16,1024]{1,0:T(8,128)(2,1)S(1)}, bf16[16,1024]{1,0:T(8,128)(2,1)S(1)}, u32[]{:S(2)}, u32[]{:S(2)}) %collective-permute-start.5) | collective-permute-done | bytes 32800 | tf_op jit(solution)/shard_map/ppermute | solution.py:22
  29.9 1.5 %collective-permute-start.12 = (bf16[64,1024]{1,0:T(8,128)(2,1)S(1)}, bf16[64,1024]{1,0:T(8,128)(2,1)S(1)}, u32[]{:S(2)}, u32[]{:S(2)}) collective-permute-start(bf16[64,1024]{1,0:T(8,128)(2,1)S(1)} %get-tuple-element.52.refs_5_.refs_0_), channel_id=1, source_target_pairs={{0,16},{16,0},{32,48},{48,32},{64,80},{80,64},{96,112},{112,96},{1... | collective-permute-start | bytes 393224 | tf_op jit(solution)/shard_map/ppermute | solution.py:22
  31.4 3.1 %collective-permute-start.7 = (bf16[32,1024]{1,0:T(8,128)(2,1)S(1)}, bf16[32,1024]{1,0:T(8,128)(2,1)S(1)}, u32[]{:S(2)}, u32[]{:S(2)}) collective-permute-start(bf16[32,1024]{1,0:T(8,128)(2,1)S(1)} %get-tuple-element.49), channel_id=1, source_target_pairs={{0,12},{1,13},{2,14},{3,15},{4,8},{5,9},{6,10},{7,11},{8,4},{9,5},... | collective-permute-start | bytes 196616 | tf_op jit(solution)/shard_map/ppermute | solution.py:22
  34.5 0.5 collective-permute-start.9
  35.0 2.2 %low_stats.1.after_ref.low_ref = f32[4,8,512]{2,1,0:T(8,128)S(1)} custom-call(bf16[256,512]{1,0:T(8,128)(2,1)S(1)} %copy-done.2, bf16[256,512]{1,0:T(8,128)(2,1)S(1)} %copy-done.3, bf16[256,512]{1,0:T(8,128)(2,1)S(1)} %copy-done, bf16[256,512]{1,0:T(8,128)(2,1)S(1)} %copy-done.1, bf16[64,1024]{1,0:T(8,128)(2,1)S(1)} %collective-permute-done.10.refs_2_.refs_0_, ...), custom_call_target="tpu_custom_call" | custom-call | flops 671088640 | bytes 1048576 | tf_op jit(solution)/shard_map/low_stats/pallas_call | solution.py:302
  37.3 2.9 %collective-permute-done.8.z2_ref = bf16[32,1024]{1,0:T(8,128)(2,1)S(1)} collective-permute-done((bf16[32,1024]{1,0:T(8,128)(2,1)S(1)}, bf16[32,1024]{1,0:T(8,128)(2,1)S(1)}, u32[]{:S(2)}, u32[]{:S(2)}) %collective-permute-start.8) | collective-permute-done | bytes 65568 | tf_op jit(solution)/shard_map/ppermute | solution.py:22
  40.2 0.7 collective-permute-start.13
  40.9 1.1 %collective-permute-done.13 = bf16[96,1024]{1,0:T(8,128)(2,1)S(1)} collective-permute-done((bf16[96,1024]{1,0:T(8,128)(2,1)S(1)}, bf16[96,1024]{1,0:T(8,128)(2,1)S(1)}, u32[]{:S(2)}, u32[]{:S(2)}) %collective-permute-start.13) | collective-permute-done | bytes 196640 | tf_op jit(solution)/shard_map/ppermute | solution.py:22
  42.0 1.5 %top_part.1 = (bf16[64,1024]{1,0:T(8,128)(2,1)S(1)}, bf16[32,1024]{1,0:T(8,128)(2,1)S(1)}, bf16[32,1024]{1,0:T(8,128)(2,1)S(1)}, f32[4,8,512]{2,1,0:T(8,128)S(1)}) custom-call(bf16[256,512]{1,0:T(8,128)(2,1)S(1)} %copy-done.2, bf16[256,512]{1,0:T(8,128)(2,1)S(1)} %copy-done.3, bf16[128,1024]{1,0:T(8,128)(2,1)S(1)} %pad_maximum_fusion.top_ref.refs_2_, ...), custom_call_target="tpu_custom_call" | custom-call | flops 268435456 | bytes 1048576 | tf_op jit(solution)/shard_map/top_part/pallas_call | solution.py:302
  43.5 1.2 %collective-permute-start.16 = (bf16[64,1024]{1,0:T(8,128)(2,1)S(1)}, bf16[64,1024]{1,0:T(8,128)(2,1)S(1)}, u32[]{:S(2)}, u32[]{:S(2)}) collective-permute-start(bf16[64,1024]{1,0:T(8,128)(2,1)S(1)} %get-tuple-element.54.refs_3_), channel_id=1, source_target_pairs={{0,4},{1,5},{2,6},{3,7},{4,0},{5,1},{6,2},{7,3},{8,12},{9,13},{10,... | collective-permute-start | bytes 393224 | tf_op jit(solution)/shard_map/ppermute | solution.py:22
  44.7 1.3 %collective-permute-start.14 = (bf16[32,1024]{1,0:T(8,128)(2,1)S(1)}, bf16[32,1024]{1,0:T(8,128)(2,1)S(1)}, u32[]{:S(2)}, u32[]{:S(2)}) collective-permute-start(bf16[32,1024]{1,0:T(8,128)(2,1)S(1)} %get-tuple-element.57), channel_id=1, source_target_pairs={{0,12},{1,13},{2,14},{3,15},{4,8},{5,9},{6,10},{7,11},{8,4},{9,5},... | collective-permute-start | bytes 196616 | tf_op jit(solution)/shard_map/ppermute | solution.py:22
  46.1 0.2 collective-permute-start.15
  46.3 1.7 %y_grads.1 = (f32[4,128,256]{2,1,0:T(8,128)S(1)}, f32[4,128,256]{2,1,0:T(8,128)S(1)}, f32[64,1024]{1,0:T(8,128)S(1)}, f32[64,1024]{1,0:T(8,128)S(1)}) custom-call(bf16[256,512]{1,0:T(8,128)(2,1)S(1)} %copy-done.2, bf16[256,512]{1,0:T(8,128)(2,1)S(1)} %copy-done.3, f32[4,8,512]{2,1,0:T(8,128)S(1)} %get-tuple-element.53.stats_ref, ...), custom_call_target="tpu_custom_call" | custom-call | flops 805306368 | bytes 1048576 | tf_op jit(solution)/shard_map/y_grads/pallas_call | solution.py:302
  47.9 2.7 %collective-permute-done.14.b3_ref = bf16[32,1024]{1,0:T(8,128)(2,1)S(1)} collective-permute-done((bf16[32,1024]{1,0:T(8,128)(2,1)S(1)}, bf16[32,1024]{1,0:T(8,128)(2,1)S(1)}, u32[]{:S(2)}, u32[]{:S(2)}) %collective-permute-start.14) | collective-permute-done | bytes 65568 | tf_op jit(solution)/shard_map/ppermute | solution.py:22
  50.7 2.4 %collective-permute-done.15.b2_ref = bf16[32,1024]{1,0:T(8,128)(2,1)S(1)} collective-permute-done((bf16[32,1024]{1,0:T(8,128)(2,1)S(1)}, bf16[32,1024]{1,0:T(8,128)(2,1)S(1)}, u32[]{:S(2)}, u32[]{:S(2)}) %collective-permute-start.15) | collective-permute-done | bytes 65568 | tf_op jit(solution)/shard_map/ppermute | solution.py:22
  53.2 0.5 collective-permute-start.19
  53.6 0.5 collective-permute-start.17
  54.1 2.4 %collective-permute-start.18 = (bf16[32,1024]{1,0:T(8,128)(2,1)S(1)}, bf16[32,1024]{1,0:T(8,128)(2,1)S(1)}, u32[]{:S(2)}, u32[]{:S(2)}) collective-permute-start(bf16[32,1024]{1,0:T(8,128)(2,1)S(1)} %get-tuple-element.65), channel_id=1, source_target_pairs={{0,2},{1,3},{2,0},{3,1},{4,6},{5,7},{6,4},{7,5},{8,10},{9,11},{10,... | collective-permute-start | bytes 196616 | tf_op jit(solution)/shard_map/ppermute | solution.py:22
  56.5 2.4 %x_grads.1 = (f32[4,128,256]{2,1,0:T(8,128)S(1)}, f32[4,128,256]{2,1,0:T(8,128)S(1)}, f32[96,1024]{1,0:T(8,128)S(1)}, f32[96,1024]{1,0:T(8,128)S(1)}, f32[128,1024]{1,0:T(8,128)S(1)}) custom-call(bf16[256,512]{1,0:T(8,128)(2,1)S(1)} %copy-done.2, bf16[256,512]{1,0:T(8,128)(2,1)S(1)} %copy-done.3, f32[4,8,512]{2,1,0:T(8,128)S(1)} %get-tuple-element.53.stats_ref, ...), custom_call_target="tpu_custom_call" | custom-call | flops 1006632960 | bytes 1048576 | tf_op jit(solution)/shard_map/x_grads/pallas_call | solution.py:302
  58.9 0.5 collective-permute-done.18.b2_ref
  59.4 0.3 x_send.1
  59.7 0.4 collective-permute-start.22
  60.1 0.6 collective-permute-start.20
  60.7 2.3 %collective-permute-start.21 = (bf16[48,1024]{1,0:T(8,128)(2,1)S(1)}, bf16[48,1024]{1,0:T(8,128)(2,1)S(1)}, u32[]{:S(2)}, u32[]{:S(2)}) collective-permute-start(bf16[48,1024]{1,0:T(8,128)(2,1)S(1)} %get-tuple-element.75), channel_id=1, source_target_pairs={{0,64},{16,80},{32,96},{48,112},{64,0},{80,16},{96,32},{112,48},{1... | collective-permute-start | bytes 294920 | tf_op jit(solution)/shard_map/ppermute | solution.py:22
  63.0 2.4 %own_grads.1 = (bf16[256,512]{1,0:T(8,128)(2,1)}, bf16[256,512]{1,0:T(8,128)(2,1)}, f32[64,1024]{1,0:T(8,128)S(1)}, f32[128,1024]{1,0:T(8,128)S(1)}) custom-call(bf16[256,512]{1,0:T(8,128)(2,1)S(1)} %copy-done.2, bf16[256,512]{1,0:T(8,128)(2,1)S(1)} %copy-done.3, f32[4,8,512]{2,1,0:T(8,128)S(1)} %get-tuple-element.53.stats_ref, ...), custom_call_target="tpu_custom_call" | custom-call | flops 603979776 | bytes 1048576 | tf_op jit(solution)/shard_map/own_grads/pallas_call | solution.py:302
  65.4 0.9 %collective-permute-done.21.b2_ref = bf16[48,1024]{1,0:T(8,128)(2,1)S(1)} collective-permute-done((bf16[48,1024]{1,0:T(8,128)(2,1)S(1)}, bf16[48,1024]{1,0:T(8,128)(2,1)S(1)}, u32[]{:S(2)}, u32[]{:S(2)}) %collective-permute-start.21) | collective-permute-done | bytes 98336 | tf_op jit(solution)/shard_map/ppermute | solution.py:22
  66.3 0.1 core_send.1
  66.4 2.9 %collective-permute-start.23 = (bf16[72,1024]{1,0:T(8,128)(2,1)S(1)}, bf16[72,1024]{1,0:T(8,128)(2,1)S(1)}, u32[]{:S(2)}, u32[]{:S(2)}) collective-permute-start(bf16[72,1024]{1,0:T(8,128)(2,1)S(1)} %get-tuple-element.79), channel_id=1, source_target_pairs={{0,16},{16,0},{32,48},{48,32},{64,80},{80,64},{96,112},{112,96},{1... | collective-permute-start | bytes 442376 | tf_op jit(solution)/shard_map/ppermute | solution.py:22
  69.4 1.0 %collective-permute-done.23 = bf16[72,1024]{1,0:T(8,128)(2,1)S(1)} collective-permute-done((bf16[72,1024]{1,0:T(8,128)(2,1)S(1)}, bf16[72,1024]{1,0:T(8,128)(2,1)S(1)}, u32[]{:S(2)}, u32[]{:S(2)}) %collective-permute-start.23) | collective-permute-done | bytes 147488 | tf_op jit(solution)/shard_map/ppermute | solution.py:22
  70.4 5.6 %collective-permute-start.24 = (bf16[8,1024]{1,0:T(8,128)(2,1)S(1)}, bf16[8,1024]{1,0:T(8,128)(2,1)S(1)}, u32[]{:S(2)}, u32[]{:S(2)}) collective-permute-start(bf16[8,1024]{1,0:T(8,128)(2,1)S(1)} %fusion), channel_id=1, source_target_pairs={{0,128},{16,144},{32,160},{48,176},{64,192},{80,208},{96,224},{112... | collective-permute-start | bytes 49160 | tf_op jit(solution)/shard_map/ppermute | solution.py:22
  76.1 0.4 finish.1.near_ref
  76.5 0.7 collective-permute-done.24.part_ref
  77.2 0.9 %add_last.1 = (bf16[256,512]{1,0:T(8,128)(2,1)}, bf16[256,512]{1,0:T(8,128)(2,1)}) custom-call(f32[256,1024]{1,0:T(8,128)S(1)} %finish.1.near_ref, bf16[8,1024]{1,0:T(8,128)(2,1)S(1)} %collective-permute-done.24.part_ref), custom_call_target="tpu_custom_call" | custom-call | tf_op jit(solution)/shard_map/add_last/pallas_call | solution.py:463
  (34 shorter events, 0.3 us)
Async XLA Ops:
  0.6 34.4 %copy-start.2 = (bf16[256,512]{1,0:T(8,128)(2,1)S(1)}, bf16[256,512]{1,0:T(8,128)(2,1)}, u32[]{:S(2)}) copy-start(bf16[256,512]{1,0:T(8,128)(2,1)} %q_ref.9) | copy-start | bytes 786436
  0.6 34.4 %copy-start.3 = (bf16[256,512]{1,0:T(8,128)(2,1)S(1)}, bf16[256,512]{1,0:T(8,128)(2,1)}, u32[]{:S(2)}) copy-start(bf16[256,512]{1,0:T(8,128)(2,1)} %do_ref.9) | copy-start | bytes 786436
  2.1 9.0 %collective-permute-start = (bf16[8,1024]{1,0:T(8,128)(2,1)S(1)}, bf16[8,1024]{1,0:T(8,128)(2,1)S(1)}, u32[]{:S(2)}, u32[]{:S(2)}) collective-permute-start(bf16[8,1024]{1,0:T(8,128)(2,1)S(1)} %get-tuple-element.45), channel_id=1, source_target_pairs={{0,128},{16,144},{32,160},{48,176},{64,192},{80,208},{96,224},{112... | collective-permute-start | bytes 49160 | tf_op jit(solution)/shard_map/ppermute | solution.py:22
  11.0 24.0 %copy-start = (bf16[256,512]{1,0:T(8,128)(2,1)S(1)}, bf16[256,512]{1,0:T(8,128)(2,1)}, u32[]{:S(2)}) copy-start(bf16[256,512]{1,0:T(8,128)(2,1)} %refs_1_.3) | copy-start | bytes 786436
  11.0 24.0 %copy-start.1 = (bf16[256,512]{1,0:T(8,128)(2,1)S(1)}, bf16[256,512]{1,0:T(8,128)(2,1)}, u32[]{:S(2)}) copy-start(bf16[256,512]{1,0:T(8,128)(2,1)} %refs_2_.3) | copy-start | bytes 786436
  11.0 8.1 %collective-permute-start.3 = (bf16[40,1024]{1,0:T(8,128)(2,1)S(1)}, bf16[40,1024]{1,0:T(8,128)(2,1)S(1)}, u32[]{:S(2)}, u32[]{:S(2)}) collective-permute-start(bf16[40,1024]{1,0:T(8,128)(2,1)S(1)} %pad_maximum_fusion.1), channel_id=1, source_target_pairs={{0,32},{16,48},{32,0},{48,16},{64,96},{80,112},{96,64},{112,80},{1... | collective-permute-start | bytes 245768 | tf_op jit(solution)/shard_map/ppermute | solution.py:22
  12.3 4.2 %collective-permute-start.1 = (bf16[24,1024]{1,0:T(8,128)(2,1)S(1)}, bf16[24,1024]{1,0:T(8,128)(2,1)S(1)}, u32[]{:S(2)}, u32[]{:S(2)}) collective-permute-start(bf16[24,1024]{1,0:T(8,128)(2,1)S(1)} %constant_dynamic-update-slice_fusion), channel_id=1, source_target_pairs={{0,96},{16,112},{32,64},{48,80},{64,32},{80,48},{96,0},{112,16},{1... | collective-permute-start | bytes 147464 | tf_op jit(solution)/shard_map/ppermute | solution.py:22
  14.2 5.0 %collective-permute-start.2 = (bf16[24,1024]{1,0:T(8,128)(2,1)S(1)}, bf16[24,1024]{1,0:T(8,128)(2,1)S(1)}, u32[]{:S(2)}, u32[]{:S(2)}) collective-permute-start(bf16[24,1024]{1,0:T(8,128)(2,1)S(1)} %constant_dynamic-update-slice_fusion), channel_id=1, source_target_pairs={{0,64},{16,80},{32,96},{48,112},{64,0},{80,16},{96,32},{112,48},{1... | collective-permute-start | bytes 147464 | tf_op jit(solution)/shard_map/ppermute | solution.py:22
  19.3 10.6 %collective-permute-start.6 = (bf16[32,1024]{1,0:T(8,128)(2,1)S(1)}, bf16[32,1024]{1,0:T(8,128)(2,1)S(1)}, u32[]{:S(2)}, u32[]{:S(2)}) collective-permute-start(bf16[32,1024]{1,0:T(8,128)(2,1)S(1)} %get-tuple-element.48), channel_id=1, source_target_pairs={{0,1},{1,0},{2,3},{3,2},{4,5},{5,4},{6,7},{7,6},{8,9},{9,8},{10,11... | collective-permute-start | bytes 196616 | tf_op jit(solution)/shard_map/ppermute | solution.py:22
  20.7 14.3 %collective-permute-start.11 = (bf16[96,1024]{1,0:T(8,128)(2,1)S(1)}, bf16[96,1024]{1,0:T(8,128)(2,1)S(1)}, u32[]{:S(2)}, u32[]{:S(2)}) collective-permute-start(bf16[96,1024]{1,0:T(8,128)(2,1)S(1)} %get-tuple-element.51.refs_3_.refs_0_), channel_id=1, source_target_pairs={{0,16},{16,0},{32,48},{48,32},{64,80},{80,64},{96,112},{112,96},{1... | collective-permute-start | bytes 589832 | tf_op jit(solution)/shard_map/ppermute | solution.py:22
  23.7 4.0 %collective-permute-start.4 = (bf16[16,1024]{1,0:T(8,128)(2,1)S(1)}, bf16[16,1024]{1,0:T(8,128)(2,1)S(1)}, u32[]{:S(2)}, u32[]{:S(2)}) collective-permute-start(bf16[16,1024]{1,0:T(8,128)(2,1)S(1)} %get-tuple-element.47.level5_ref), channel_id=1, source_target_pairs={{0,3},{1,2},{2,1},{3,0},{4,7},{5,6},{6,5},{7,4},{8,11},{9,10},{10,... | collective-permute-start | bytes 98312 | tf_op jit(solution)/shard_map/ppermute | solution.py:22
  25.6 4.3 %collective-permute-start.5 = (bf16[16,1024]{1,0:T(8,128)(2,1)S(1)}, bf16[16,1024]{1,0:T(8,128)(2,1)S(1)}, u32[]{:S(2)}, u32[]{:S(2)}) collective-permute-start(bf16[16,1024]{1,0:T(8,128)(2,1)S(1)} %get-tuple-element.47.level5_ref), channel_id=1, source_target_pairs={{0,2},{1,3},{2,0},{3,1},{4,6},{5,7},{6,4},{7,5},{8,10},{9,11},{10,... | collective-permute-start | bytes 98312 | tf_op jit(solution)/shard_map/ppermute | solution.py:22
  26.3 8.2 %collective-permute-start.10 = (bf16[64,1024]{1,0:T(8,128)(2,1)S(1)}, bf16[64,1024]{1,0:T(8,128)(2,1)S(1)}, u32[]{:S(2)}, u32[]{:S(2)}) collective-permute-start(bf16[64,1024]{1,0:T(8,128)(2,1)S(1)} %get-tuple-element.50), channel_id=1, source_target_pairs={{0,16},{16,0},{32,48},{48,32},{64,80},{80,64},{96,112},{112,96},{1... | collective-permute-start | bytes 393224 | tf_op jit(solution)/shard_map/ppermute | solution.py:22
  29.9 5.1 %collective-permute-start.12 = (bf16[64,1024]{1,0:T(8,128)(2,1)S(1)}, bf16[64,1024]{1,0:T(8,128)(2,1)S(1)}, u32[]{:S(2)}, u32[]{:S(2)}) collective-permute-start(bf16[64,1024]{1,0:T(8,128)(2,1)S(1)} %get-tuple-element.52.refs_5_.refs_0_), channel_id=1, source_target_pairs={{0,16},{16,0},{32,48},{48,32},{64,80},{80,64},{96,112},{112,96},{1... | collective-permute-start | bytes 393224 | tf_op jit(solution)/shard_map/ppermute | solution.py:22
  31.4 5.8 %collective-permute-start.7 = (bf16[32,1024]{1,0:T(8,128)(2,1)S(1)}, bf16[32,1024]{1,0:T(8,128)(2,1)S(1)}, u32[]{:S(2)}, u32[]{:S(2)}) collective-permute-start(bf16[32,1024]{1,0:T(8,128)(2,1)S(1)} %get-tuple-element.49), channel_id=1, source_target_pairs={{0,12},{1,13},{2,14},{3,15},{4,8},{5,9},{6,10},{7,11},{8,4},{9,5},... | collective-permute-start | bytes 196616 | tf_op jit(solution)/shard_map/ppermute | solution.py:22
  34.5 5.6 %collective-permute-start.8 = (bf16[32,1024]{1,0:T(8,128)(2,1)S(1)}, bf16[32,1024]{1,0:T(8,128)(2,1)S(1)}, u32[]{:S(2)}, u32[]{:S(2)}) collective-permute-start(bf16[32,1024]{1,0:T(8,128)(2,1)S(1)} %get-tuple-element.49), channel_id=1, source_target_pairs={{0,8},{1,9},{2,10},{3,11},{4,12},{5,13},{6,14},{7,15},{8,0},{9,1},... | collective-permute-start | bytes 196616 | tf_op jit(solution)/shard_map/ppermute | solution.py:22
  34.5 5.6 %collective-permute-start.9 = (bf16[32,1024]{1,0:T(8,128)(2,1)S(1)}, bf16[32,1024]{1,0:T(8,128)(2,1)S(1)}, u32[]{:S(2)}, u32[]{:S(2)}) collective-permute-start(bf16[32,1024]{1,0:T(8,128)(2,1)S(1)} %get-tuple-element.49), channel_id=1, source_target_pairs={{0,4},{1,5},{2,6},{3,7},{4,0},{5,1},{6,2},{7,3},{8,12},{9,13},{10,... | collective-permute-start | bytes 196616 | tf_op jit(solution)/shard_map/ppermute | solution.py:22
  40.2 1.8 %collective-permute-start.13 = (bf16[96,1024]{1,0:T(8,128)(2,1)S(1)}, bf16[96,1024]{1,0:T(8,128)(2,1)S(1)}, u32[]{:S(2)}, u32[]{:S(2)}) collective-permute-start(bf16[96,1024]{1,0:T(8,128)(2,1)S(1)} %near.1), channel_id=1, source_target_pairs={{0,16},{16,0},{32,48},{48,32},{64,80},{80,64},{96,112},{112,96},{1... | collective-permute-start | bytes 589832 | tf_op jit(solution)/shard_map/ppermute | solution.py:22
  43.5 9.6 %collective-permute-start.16 = (bf16[64,1024]{1,0:T(8,128)(2,1)S(1)}, bf16[64,1024]{1,0:T(8,128)(2,1)S(1)}, u32[]{:S(2)}, u32[]{:S(2)}) collective-permute-start(bf16[64,1024]{1,0:T(8,128)(2,1)S(1)} %get-tuple-element.54.refs_3_), channel_id=1, source_target_pairs={{0,4},{1,5},{2,6},{3,7},{4,0},{5,1},{6,2},{7,3},{8,12},{9,13},{10,... | collective-permute-start | bytes 393224 | tf_op jit(solution)/shard_map/ppermute | solution.py:22
  44.7 5.9 %collective-permute-start.14 = (bf16[32,1024]{1,0:T(8,128)(2,1)S(1)}, bf16[32,1024]{1,0:T(8,128)(2,1)S(1)}, u32[]{:S(2)}, u32[]{:S(2)}) collective-permute-start(bf16[32,1024]{1,0:T(8,128)(2,1)S(1)} %get-tuple-element.57), channel_id=1, source_target_pairs={{0,12},{1,13},{2,14},{3,15},{4,8},{5,9},{6,10},{7,11},{8,4},{9,5},... | collective-permute-start | bytes 196616 | tf_op jit(solution)/shard_map/ppermute | solution.py:22
  46.1 7.0 %collective-permute-start.15 = (bf16[32,1024]{1,0:T(8,128)(2,1)S(1)}, bf16[32,1024]{1,0:T(8,128)(2,1)S(1)}, u32[]{:S(2)}, u32[]{:S(2)}) collective-permute-start(bf16[32,1024]{1,0:T(8,128)(2,1)S(1)} %get-tuple-element.58), channel_id=1, source_target_pairs={{0,8},{1,9},{2,10},{3,11},{4,12},{5,13},{6,14},{7,15},{8,0},{9,1},... | collective-permute-start | bytes 196616 | tf_op jit(solution)/shard_map/ppermute | solution.py:22
  53.2 6.2 %collective-permute-start.19 = (bf16[64,1024]{1,0:T(8,128)(2,1)S(1)}, bf16[64,1024]{1,0:T(8,128)(2,1)S(1)}, u32[]{:S(2)}, u32[]{:S(2)}) collective-permute-start(bf16[64,1024]{1,0:T(8,128)(2,1)S(1)} %get-tuple-element.61.refs_6_), channel_id=1, source_target_pairs={{0,1},{1,0},{2,3},{3,2},{4,5},{5,4},{6,7},{7,6},{8,9},{9,8},{10,11... | collective-permute-start | bytes 393224 | tf_op jit(solution)/shard_map/ppermute | solution.py:22
  53.6 5.3 %collective-permute-start.17 = (bf16[32,1024]{1,0:T(8,128)(2,1)S(1)}, bf16[32,1024]{1,0:T(8,128)(2,1)S(1)}, u32[]{:S(2)}, u32[]{:S(2)}) collective-permute-start(bf16[32,1024]{1,0:T(8,128)(2,1)S(1)} %get-tuple-element.64), channel_id=1, source_target_pairs={{0,3},{1,2},{2,1},{3,0},{4,7},{5,6},{6,5},{7,4},{8,11},{9,10},{10,... | collective-permute-start | bytes 196616 | tf_op jit(solution)/shard_map/ppermute | solution.py:22
  54.1 5.2 %collective-permute-start.18 = (bf16[32,1024]{1,0:T(8,128)(2,1)S(1)}, bf16[32,1024]{1,0:T(8,128)(2,1)S(1)}, u32[]{:S(2)}, u32[]{:S(2)}) collective-permute-start(bf16[32,1024]{1,0:T(8,128)(2,1)S(1)} %get-tuple-element.65), channel_id=1, source_target_pairs={{0,2},{1,3},{2,0},{3,1},{4,6},{5,7},{6,4},{7,5},{8,10},{9,11},{10,... | collective-permute-start | bytes 196616 | tf_op jit(solution)/shard_map/ppermute | solution.py:22
  59.7 6.7 %collective-permute-start.22 = (bf16[80,1024]{1,0:T(8,128)(2,1)S(1)}, bf16[80,1024]{1,0:T(8,128)(2,1)S(1)}, u32[]{:S(2)}, u32[]{:S(2)}) collective-permute-start(bf16[80,1024]{1,0:T(8,128)(2,1)S(1)} %get-tuple-element.69.refs_5_), channel_id=1, source_target_pairs={{0,32},{16,48},{32,0},{48,16},{64,96},{80,112},{96,64},{112,80},{1... | collective-permute-start | bytes 491528 | tf_op jit(solution)/shard_map/ppermute | solution.py:22
  60.1 5.4 %collective-permute-start.20 = (bf16[48,1024]{1,0:T(8,128)(2,1)S(1)}, bf16[48,1024]{1,0:T(8,128)(2,1)S(1)}, u32[]{:S(2)}, u32[]{:S(2)}) collective-permute-start(bf16[48,1024]{1,0:T(8,128)(2,1)S(1)} %get-tuple-element.74), channel_id=1, source_target_pairs={{0,96},{16,112},{32,64},{48,80},{64,32},{80,48},{96,0},{112,16},{1... | collective-permute-start | bytes 294920 | tf_op jit(solution)/shard_map/ppermute | solution.py:22
  60.7 5.6 %collective-permute-start.21 = (bf16[48,1024]{1,0:T(8,128)(2,1)S(1)}, bf16[48,1024]{1,0:T(8,128)(2,1)S(1)}, u32[]{:S(2)}, u32[]{:S(2)}) collective-permute-start(bf16[48,1024]{1,0:T(8,128)(2,1)S(1)} %get-tuple-element.75), channel_id=1, source_target_pairs={{0,64},{16,80},{32,96},{48,112},{64,0},{80,16},{96,32},{112,48},{1... | collective-permute-start | bytes 294920 | tf_op jit(solution)/shard_map/ppermute | solution.py:22
  66.4 3.9 %collective-permute-start.23 = (bf16[72,1024]{1,0:T(8,128)(2,1)S(1)}, bf16[72,1024]{1,0:T(8,128)(2,1)S(1)}, u32[]{:S(2)}, u32[]{:S(2)}) collective-permute-start(bf16[72,1024]{1,0:T(8,128)(2,1)S(1)} %get-tuple-element.79), channel_id=1, source_target_pairs={{0,16},{16,0},{32,48},{48,32},{64,80},{80,64},{96,112},{112,96},{1... | collective-permute-start | bytes 442376 | tf_op jit(solution)/shard_map/ppermute | solution.py:22
  70.4 6.8 %collective-permute-start.24 = (bf16[8,1024]{1,0:T(8,128)(2,1)S(1)}, bf16[8,1024]{1,0:T(8,128)(2,1)S(1)}, u32[]{:S(2)}, u32[]{:S(2)}) collective-permute-start(bf16[8,1024]{1,0:T(8,128)(2,1)S(1)} %fusion), channel_id=1, source_target_pairs={{0,128},{16,144},{32,160},{48,176},{64,192},{80,208},{96,224},{112... | collective-permute-start | bytes 49160 | tf_op jit(solution)/shard_map/ppermute | solution.py:22

commit v4 on v3

--- a/solution.py
+++ b/solution.py
@@ -96,10 +96,11 @@
     out_ref[64:] = z3_ref[...]
 
 
-def level6_kernel(level5_ref, y3_ref, y2_ref, y1_ref, low_ref, level6_ref):
-    low_ref[:32] = y1_ref[...]
-    low_ref[32:48] = y2_ref[...]
-    low_ref[48:] = y3_ref[...]
+def level6_kernel(level5_ref, y3_ref, y2_ref, y1_ref, low_x_ref, low_ref, level6_ref):
+    low_ref[:96] = low_x_ref[...]
+    low_ref[96:128] = y1_ref[...]
+    low_ref[128:144] = y2_ref[...]
+    low_ref[144:] = y3_ref[...]
     level6_ref[:8] = pair_mean(level5_ref[...])
     level6_ref[8:16] = pair_mean(pair_mean(y1_ref[...]))
     level6_ref[16:24] = pair_mean(y2_ref[...])
@@ -409,26 +410,25 @@
     y1 = flip(level4, "hi", 1)
     y2 = flip(level5, "hi", 2)
     y3 = flip(level5, "hi", 3)
-    low_x2 = other_core(low_x)
-    low_y, level6 = whole(level6_kernel, [wide(64), wide(32)], "level6")(level5, y3, y2, y1)
+    low, level6 = whole(level6_kernel, [wide(160), wide(32)], "level6")(level5, y3, y2, y1, low_x)
     z1 = flip(level6, "hi", 4)
     z2 = flip(level6, "hi", 8)
     z3 = flip(level6, "hi", 12)
-    low_y2 = other_core(low_y)
-    low = low_stats(
+    low2 = other_core(low)
+    low_stat = low_stats(
         queries, cotangent,
-        [(keys, values)] + [(rows,) for rows in (sec0, low_x, low_x2, low_y, low_y2)],
-    )
-    near = whole(near_kernel, wide(96), "near", 3)(z3, z2, z1, low)
+        [(keys, values)] + [(rows,) for rows in (sec0, low, low2)],
+    )
+    near = whole(near_kernel, wide(96), "near", 3)(z3, z2, z1, low_stat)
     mate = other_core(near)
     top = joined(near[:32], mate[:32], mean(near[32:], mate[32:]))
 
-    z1, z2, z3, stats = top_part(queries, cotangent, top, low)
+    z1, z2, z3, stats = top_part(queries, cotangent, top, low_stat)
     b1 = flip(z1, "hi", 4)
     b2 = flip(z2, "hi", 8)
     b3 = flip(z3, "hi", 12)
     mixed, gq, y_g, y_other = grads_part(
-        queries, cotangent, stats, [([low_y], 0, 64), ([low_y2], 0, 64), ([top], 0, 128)],
+        queries, cotangent, stats, [([low], 96, 64), ([low2], 96, 64), ([top], 0, 128)],
         (F32, F32, None), [], z1, False, "y_grads",
     )
     y1, y2, y3, g6 = whole(y_send_kernel, [wide(64), wide(32), wide(32), wide_f32(64)], "y_send")(
@@ -439,7 +439,7 @@
     b3 = flip(y3, "hi", 3)
     mixed, gq, x_g, x_other, first_g = grads_part(
         queries, cotangent, stats,
-        [([low_x], 0, 96), ([low_x2], 0, 96), ([keys, values], 0, TOK // 2)],
+        [([low], 0, 96), ([low2], 0, 96), ([keys, values], 0, TOK // 2)],
         (F32,) * 3, [mixed, gq], y1, False, "x_grads",
     )
     x1, x2, x3, two_g, far_g = whole(

time: 78.1 us -> 78.3 us (level)
  starting transfers between devices: 42.7 us -> 45.9 us
  waiting for transfers between devices: 20.9 us -> 17.9 us
    ppermute x25 -> x24, starting transfers between devices: 42.7 us -> 45.9 us  [flip(): lax.ppermute(value, axis, [(source, source ^ mask) for source in range(16)])]
    ppermute x25 -> x24, waiting for transfers between devices: 20.9 us -> 17.9 us  [flip(): lax.ppermute(value, axis, [(source, source ^ mask) for source in range(16)])]
  transfers between devices with their start and end apart: 25 -> 24, of which waited for: 13 -> 12; matrix products, arithmetic and copies ran while one was open for 0% -> 0% of each run, Pallas kernels for 12% -> 12%
where the time goes in v4:
time: 78.3 us; the launch traced here: 78.2 us
  starting transfers between devices  45.9 us (59%)
  waiting for transfers between devices  17.9 us (23%)
  Pallas kernels  13.4 us (17%)
  between operations  0.83 us (1%)
    ppermute x24, starting transfers between devices, flip(): lax.ppermute(value, axis, [(source, source ^ mask) for source in range(16)])  45.9 us
    ppermute x24, waiting for transfers between devices, flip(): lax.ppermute(value, axis, [(source, source ^ mask) for source in range(16)])  17.9 us
    pallas_call x5, Pallas kernels, call(): pl.pallas_call(kernel, in_specs=in_specs, out_shape=out_shape, compiler_p...  10.1 us
  transfers between devices with their start and end apart: 24, of which 12 were waited for; matrix products, arithmetic and copies ran while one was open for 0% of the time, Pallas kernels for 12%

profile of v4, /device:TPU:1, one launch (start us, length us, event | category | flops | bytes accessed | tf_op | source)
XLA Modules:
  0.0 78.2 jit_solution(15941898252109053625)
XLA Ops:
  0.6 1.4 %pool.1 = (bf16[64,1024]{1,0:T(8,128)(2,1)S(1)}, bf16[32,1024]{1,0:T(8,128)(2,1)S(1)}, bf16[16,1024]{1,0:T(8,128)(2,1)S(1)}, bf16[8,1024]{1,0:T(8,128)(2,1)S(1)}) custom-call(bf16[256,512]{1,0:T(8,128)(2,1)} %refs_1_.3, bf16[256,512]{1,0:T(8,128)(2,1)} %refs_2_.3), custom_call_target="tpu_custom_call" | custom-call | tf_op jit(solution)/shard_map/pool/pallas_call | solution.py:359
  2.0 7.8 %collective-permute-start = (bf16[8,1024]{1,0:T(8,128)(2,1)S(1)}, bf16[8,1024]{1,0:T(8,128)(2,1)S(1)}, u32[]{:S(2)}, u32[]{:S(2)}) collective-permute-start(bf16[8,1024]{1,0:T(8,128)(2,1)S(1)} %get-tuple-element.45), channel_id=1, source_target_pairs={{0,128},{16,144},{32,160},{48,176},{64,192},{80,208},{96,224},{112... | collective-permute-start | bytes 49160 | tf_op jit(solution)/shard_map/ppermute | solution.py:22
  9.9 1.1 %collective-permute-done.far_ref = bf16[8,1024]{1,0:T(8,128)(2,1)S(1)} collective-permute-done((bf16[8,1024]{1,0:T(8,128)(2,1)S(1)}, bf16[8,1024]{1,0:T(8,128)(2,1)S(1)}, u32[]{:S(2)}, u32[]{:S(2)}) %collective-permute-start) | collective-permute-done | bytes 16416 | tf_op jit(solution)/shard_map/ppermute | solution.py:22
  11.0 1.3 %collective-permute-start.3 = (bf16[40,1024]{1,0:T(8,128)(2,1)S(1)}, bf16[40,1024]{1,0:T(8,128)(2,1)S(1)}, u32[]{:S(2)}, u32[]{:S(2)}) collective-permute-start(bf16[40,1024]{1,0:T(8,128)(2,1)S(1)} %pad_maximum_fusion.1), channel_id=1, source_target_pairs={{0,32},{16,48},{32,0},{48,16},{64,96},{80,112},{96,64},{112,80},{1... | collective-permute-start | bytes 245768 | tf_op jit(solution)/shard_map/ppermute | solution.py:22
  12.3 1.8 %collective-permute-start.1 = (bf16[24,1024]{1,0:T(8,128)(2,1)S(1)}, bf16[24,1024]{1,0:T(8,128)(2,1)S(1)}, u32[]{:S(2)}, u32[]{:S(2)}) collective-permute-start(bf16[24,1024]{1,0:T(8,128)(2,1)S(1)} %constant_dynamic-update-slice_fusion), channel_id=1, source_target_pairs={{0,96},{16,112},{32,64},{48,80},{64,32},{80,48},{96,0},{112,16},{1... | collective-permute-start | bytes 147464 | tf_op jit(solution)/shard_map/ppermute | solution.py:22
  14.1 0.7 collective-permute-start.2
  14.9 1.6 %collective-permute-done.1.x3_ref = bf16[24,1024]{1,0:T(8,128)(2,1)S(1)} collective-permute-done((bf16[24,1024]{1,0:T(8,128)(2,1)S(1)}, bf16[24,1024]{1,0:T(8,128)(2,1)S(1)}, u32[]{:S(2)}, u32[]{:S(2)}) %collective-permute-start.1) | collective-permute-done | bytes 49184 | tf_op jit(solution)/shard_map/ppermute | solution.py:22
  16.5 2.6 %collective-permute-done.2.x2_ref = bf16[24,1024]{1,0:T(8,128)(2,1)S(1)} collective-permute-done((bf16[24,1024]{1,0:T(8,128)(2,1)S(1)}, bf16[24,1024]{1,0:T(8,128)(2,1)S(1)}, u32[]{:S(2)}, u32[]{:S(2)}) %collective-permute-start.2) | collective-permute-done | bytes 49184 | tf_op jit(solution)/shard_map/ppermute | solution.py:22
  19.1 0.0 collective-permute-done.3.x1_ref
  19.1 0.2 group.1
  19.3 1.4 %collective-permute-start.6 = (bf16[32,1024]{1,0:T(8,128)(2,1)S(1)}, bf16[32,1024]{1,0:T(8,128)(2,1)S(1)}, u32[]{:S(2)}, u32[]{:S(2)}) collective-permute-start(bf16[32,1024]{1,0:T(8,128)(2,1)S(1)} %get-tuple-element.48), channel_id=1, source_target_pairs={{0,1},{1,0},{2,3},{3,2},{4,5},{5,4},{6,7},{7,6},{8,9},{9,8},{10,11... | collective-permute-start | bytes 196616 | tf_op jit(solution)/shard_map/ppermute | solution.py:22
  20.7 1.9 %collective-permute-start.4 = (bf16[16,1024]{1,0:T(8,128)(2,1)S(1)}, bf16[16,1024]{1,0:T(8,128)(2,1)S(1)}, u32[]{:S(2)}, u32[]{:S(2)}) collective-permute-start(bf16[16,1024]{1,0:T(8,128)(2,1)S(1)} %get-tuple-element.47.level5_ref), channel_id=1, source_target_pairs={{0,3},{1,2},{2,1},{3,0},{4,7},{5,6},{6,5},{7,4},{8,11},{9,10},{10,... | collective-permute-start | bytes 98312 | tf_op jit(solution)/shard_map/ppermute | solution.py:22
  22.6 0.7 collective-permute-start.5
  23.3 1.3 %collective-permute-done.4.y3_ref = bf16[16,1024]{1,0:T(8,128)(2,1)S(1)} collective-permute-done((bf16[16,1024]{1,0:T(8,128)(2,1)S(1)}, bf16[16,1024]{1,0:T(8,128)(2,1)S(1)}, u32[]{:S(2)}, u32[]{:S(2)}) %collective-permute-start.4) | collective-permute-done | bytes 32800 | tf_op jit(solution)/shard_map/ppermute | solution.py:22
  24.6 2.2 %collective-permute-done.5.y2_ref = bf16[16,1024]{1,0:T(8,128)(2,1)S(1)} collective-permute-done((bf16[16,1024]{1,0:T(8,128)(2,1)S(1)}, bf16[16,1024]{1,0:T(8,128)(2,1)S(1)}, u32[]{:S(2)}, u32[]{:S(2)}) %collective-permute-start.5) | collective-permute-done | bytes 32800 | tf_op jit(solution)/shard_map/ppermute | solution.py:22
  26.9 4.5 %collective-permute-start.11 = (bf16[160,1024]{1,0:T(8,128)(2,1)S(1)}, bf16[160,1024]{1,0:T(8,128)(2,1)S(1)}, u32[]{:S(2)}, u32[]{:S(2)}) collective-permute-start(bf16[160,1024]{1,0:T(8,128)(2,1)S(1)} %get-tuple-element.52.refs_3_.refs_0_), channel_id=1, source_target_pairs={{0,16},{16,0},{32,48},{48,32},{64,80},{80,64},{96,112},{112,96},{1... | collective-permute-start | bytes 983048 | tf_op jit(solution)/shard_map/ppermute | solution.py:22
  31.4 0.1 collective-permute-start.10
  31.5 3.1 %collective-permute-start.7 = (bf16[32,1024]{1,0:T(8,128)(2,1)S(1)}, bf16[32,1024]{1,0:T(8,128)(2,1)S(1)}, u32[]{:S(2)}, u32[]{:S(2)}) collective-permute-start(bf16[32,1024]{1,0:T(8,128)(2,1)S(1)} %get-tuple-element.50), channel_id=1, source_target_pairs={{0,12},{1,13},{2,14},{3,15},{4,8},{5,9},{6,10},{7,11},{8,4},{9,5},... | collective-permute-start | bytes 196616 | tf_op jit(solution)/shard_map/ppermute | solution.py:22
  34.6 0.5 collective-permute-start.9
  35.1 2.2 %low_stats.1.after_ref.low_ref = f32[4,8,512]{2,1,0:T(8,128)S(1)} custom-call(bf16[256,512]{1,0:T(8,128)(2,1)S(1)} %copy-done.2, bf16[256,512]{1,0:T(8,128)(2,1)S(1)} %copy-done.3, bf16[256,512]{1,0:T(8,128)(2,1)S(1)} %copy-done, bf16[256,512]{1,0:T(8,128)(2,1)S(1)} %copy-done.1, bf16[64,1024]{1,0:T(8,128)(2,1)S(1)} %collective-permute-done.10.refs_2_.refs_0_, ...), custom_call_target="tpu_custom_call" | custom-call | flops 671088640 | bytes 1048576 | tf_op jit(solution)/shard_map/low_stats/pallas_call | solution.py:303
  37.3 2.9 %collective-permute-done.8.z2_ref = bf16[32,1024]{1,0:T(8,128)(2,1)S(1)} collective-permute-done((bf16[32,1024]{1,0:T(8,128)(2,1)S(1)}, bf16[32,1024]{1,0:T(8,128)(2,1)S(1)}, u32[]{:S(2)}, u32[]{:S(2)}) %collective-permute-start.8) | collective-permute-done | bytes 65568 | tf_op jit(solution)/shard_map/ppermute | solution.py:22
  40.2 0.9 %collective-permute-start.12 = (bf16[96,1024]{1,0:T(8,128)(2,1)S(1)}, bf16[96,1024]{1,0:T(8,128)(2,1)S(1)}, u32[]{:S(2)}, u32[]{:S(2)}) collective-permute-start(bf16[96,1024]{1,0:T(8,128)(2,1)S(1)} %near.1), channel_id=1, source_target_pairs={{0,16},{16,0},{32,48},{48,32},{64,80},{80,64},{96,112},{112,96},{1... | collective-permute-start | bytes 589832 | tf_op jit(solution)/shard_map/ppermute | solution.py:22
  41.1 1.1 %collective-permute-done.12 = bf16[96,1024]{1,0:T(8,128)(2,1)S(1)} collective-permute-done((bf16[96,1024]{1,0:T(8,128)(2,1)S(1)}, bf16[96,1024]{1,0:T(8,128)(2,1)S(1)}, u32[]{:S(2)}, u32[]{:S(2)}) %collective-permute-start.12) | collective-permute-done | bytes 196640 | tf_op jit(solution)/shard_map/ppermute | solution.py:22
  42.3 1.5 %top_part.1 = (bf16[64,1024]{1,0:T(8,128)(2,1)S(1)}, bf16[32,1024]{1,0:T(8,128)(2,1)S(1)}, bf16[32,1024]{1,0:T(8,128)(2,1)S(1)}, f32[4,8,512]{2,1,0:T(8,128)S(1)}) custom-call(bf16[256,512]{1,0:T(8,128)(2,1)S(1)} %copy-done.2, bf16[256,512]{1,0:T(8,128)(2,1)S(1)} %copy-done.3, bf16[128,1024]{1,0:T(8,128)(2,1)S(1)} %pad_maximum_fusion.top_ref.refs_2_, ...), custom_call_target="tpu_custom_call" | custom-call | flops 268435456 | bytes 1048576 | tf_op jit(solution)/shard_map/top_part/pallas_call | solution.py:303
  43.8 1.0 %collective-permute-start.15 = (bf16[64,1024]{1,0:T(8,128)(2,1)S(1)}, bf16[64,1024]{1,0:T(8,128)(2,1)S(1)}, u32[]{:S(2)}, u32[]{:S(2)}) collective-permute-start(bf16[64,1024]{1,0:T(8,128)(2,1)S(1)} %get-tuple-element.54.refs_3_), channel_id=1, source_target_pairs={{0,4},{1,5},{2,6},{3,7},{4,0},{5,1},{6,2},{7,3},{8,12},{9,13},{10,... | collective-permute-start | bytes 393224 | tf_op jit(solution)/shard_map/ppermute | solution.py:22
  44.8 1.4 %collective-permute-start.13 = (bf16[32,1024]{1,0:T(8,128)(2,1)S(1)}, bf16[32,1024]{1,0:T(8,128)(2,1)S(1)}, u32[]{:S(2)}, u32[]{:S(2)}) collective-permute-start(bf16[32,1024]{1,0:T(8,128)(2,1)S(1)} %get-tuple-element.57), channel_id=1, source_target_pairs={{0,12},{1,13},{2,14},{3,15},{4,8},{5,9},{6,10},{7,11},{8,4},{9,5},... | collective-permute-start | bytes 196616 | tf_op jit(solution)/shard_map/ppermute | solution.py:22
  46.2 0.3 collective-permute-start.14
  46.5 1.7 %y_grads.1 = (f32[4,128,256]{2,1,0:T(8,128)S(1)}, f32[4,128,256]{2,1,0:T(8,128)S(1)}, f32[64,1024]{1,0:T(8,128)S(1)}, f32[64,1024]{1,0:T(8,128)S(1)}) custom-call(bf16[256,512]{1,0:T(8,128)(2,1)S(1)} %copy-done.2, bf16[256,512]{1,0:T(8,128)(2,1)S(1)} %copy-done.3, f32[4,8,512]{2,1,0:T(8,128)S(1)} %get-tuple-element.53.stats_ref, ...), custom_call_target="tpu_custom_call" | custom-call | flops 805306368 | bytes 1048576 | tf_op jit(solution)/shard_map/y_grads/pallas_call | solution.py:303
  48.2 2.4 %collective-permute-done.13.b3_ref = bf16[32,1024]{1,0:T(8,128)(2,1)S(1)} collective-permute-done((bf16[32,1024]{1,0:T(8,128)(2,1)S(1)}, bf16[32,1024]{1,0:T(8,128)(2,1)S(1)}, u32[]{:S(2)}, u32[]{:S(2)}) %collective-permute-start.13) | collective-permute-done | bytes 65568 | tf_op jit(solution)/shard_map/ppermute | solution.py:22
  50.6 0.6 collective-permute-done.14.b2_ref
  51.2 0.1 y_send.1
  51.3 0.5 collective-permute-start.18
  51.7 0.5 collective-permute-start.16
  52.2 2.4 %collective-permute-start.17 = (bf16[32,1024]{1,0:T(8,128)(2,1)S(1)}, bf16[32,1024]{1,0:T(8,128)(2,1)S(1)}, u32[]{:S(2)}, u32[]{:S(2)}) collective-permute-start(bf16[32,1024]{1,0:T(8,128)(2,1)S(1)} %get-tuple-element.65), channel_id=1, source_target_pairs={{0,2},{1,3},{2,0},{3,1},{4,6},{5,7},{6,4},{7,5},{8,10},{9,11},{10,... | collective-permute-start | bytes 196616 | tf_op jit(solution)/shard_map/ppermute | solution.py:22
  54.6 2.4 %x_grads.1 = (f32[4,128,256]{2,1,0:T(8,128)S(1)}, f32[4,128,256]{2,1,0:T(8,128)S(1)}, f32[96,1024]{1,0:T(8,128)S(1)}, f32[96,1024]{1,0:T(8,128)S(1)}, f32[128,1024]{1,0:T(8,128)S(1)}) custom-call(bf16[256,512]{1,0:T(8,128)(2,1)S(1)} %copy-done.2, bf16[256,512]{1,0:T(8,128)(2,1)S(1)} %copy-done.3, f32[4,8,512]{2,1,0:T(8,128)S(1)} %get-tuple-element.53.stats_ref, ...), custom_call_target="tpu_custom_call" | custom-call | flops 1006632960 | bytes 1048576 | tf_op jit(solution)/shard_map/x_grads/pallas_call | solution.py:303
  57.0 0.3 x_send.1
  57.3 0.4 collective-permute-start.21
  57.7 0.6 collective-permute-start.19
  58.3 2.3 %collective-permute-start.20 = (bf16[48,1024]{1,0:T(8,128)(2,1)S(1)}, bf16[48,1024]{1,0:T(8,128)(2,1)S(1)}, u32[]{:S(2)}, u32[]{:S(2)}) collective-permute-start(bf16[48,1024]{1,0:T(8,128)(2,1)S(1)} %get-tuple-element.75), channel_id=1, source_target_pairs={{0,64},{16,80},{32,96},{48,112},{64,0},{80,16},{96,32},{112,48},{1... | collective-permute-start | bytes 294920 | tf_op jit(solution)/shard_map/ppermute | solution.py:22
  60.6 2.4 %own_grads.1 = (bf16[256,512]{1,0:T(8,128)(2,1)}, bf16[256,512]{1,0:T(8,128)(2,1)}, f32[64,1024]{1,0:T(8,128)S(1)}, f32[128,1024]{1,0:T(8,128)S(1)}) custom-call(bf16[256,512]{1,0:T(8,128)(2,1)S(1)} %copy-done.2, bf16[256,512]{1,0:T(8,128)(2,1)S(1)} %copy-done.3, f32[4,8,512]{2,1,0:T(8,128)S(1)} %get-tuple-element.53.stats_ref, ...), custom_call_target="tpu_custom_call" | custom-call | flops 603979776 | bytes 1048576 | tf_op jit(solution)/shard_map/own_grads/pallas_call | solution.py:303
  63.0 0.4 collective-permute-done.19.b3_ref
  63.4 0.1 core_send.1
  63.5 6.0 %collective-permute-start.22 = (bf16[72,1024]{1,0:T(8,128)(2,1)S(1)}, bf16[72,1024]{1,0:T(8,128)(2,1)S(1)}, u32[]{:S(2)}, u32[]{:S(2)}) collective-permute-start(bf16[72,1024]{1,0:T(8,128)(2,1)S(1)} %get-tuple-element.79), channel_id=1, source_target_pairs={{0,16},{16,0},{32,48},{48,32},{64,80},{80,64},{96,112},{112,96},{1... | collective-permute-start | bytes 442376 | tf_op jit(solution)/shard_map/ppermute | solution.py:22
  69.5 1.0 %collective-permute-done.22 = bf16[72,1024]{1,0:T(8,128)(2,1)S(1)} collective-permute-done((bf16[72,1024]{1,0:T(8,128)(2,1)S(1)}, bf16[72,1024]{1,0:T(8,128)(2,1)S(1)}, u32[]{:S(2)}, u32[]{:S(2)}) %collective-permute-start.22) | collective-permute-done | bytes 147488 | tf_op jit(solution)/shard_map/ppermute | solution.py:22
  70.5 5.7 %collective-permute-start.23 = (bf16[8,1024]{1,0:T(8,128)(2,1)S(1)}, bf16[8,1024]{1,0:T(8,128)(2,1)S(1)}, u32[]{:S(2)}, u32[]{:S(2)}) collective-permute-start(bf16[8,1024]{1,0:T(8,128)(2,1)S(1)} %fusion), channel_id=1, source_target_pairs={{0,128},{16,144},{32,160},{48,176},{64,192},{80,208},{96,224},{112... | collective-permute-start | bytes 49160 | tf_op jit(solution)/shard_map/ppermute | solution.py:22
  76.3 0.4 finish.1.near_ref
  76.7 0.7 collective-permute-done.23.part_ref
  77.4 0.9 %add_last.1 = (bf16[256,512]{1,0:T(8,128)(2,1)}, bf16[256,512]{1,0:T(8,128)(2,1)}) custom-call(f32[256,1024]{1,0:T(8,128)S(1)} %finish.1.near_ref, bf16[8,1024]{1,0:T(8,128)(2,1)S(1)} %collective-permute-done.23.part_ref), custom_call_target="tpu_custom_call" | custom-call | tf_op jit(solution)/shard_map/add_last/pallas_call | solution.py:463
  (32 shorter events, 0.3 us)
Async XLA Ops:
  0.6 34.4 %copy-start.3 = (bf16[256,512]{1,0:T(8,128)(2,1)S(1)}, bf16[256,512]{1,0:T(8,128)(2,1)}, u32[]{:S(2)}) copy-start(bf16[256,512]{1,0:T(8,128)(2,1)} %do_ref.9) | copy-start | bytes 786436
  2.0 8.9 %collective-permute-start = (bf16[8,1024]{1,0:T(8,128)(2,1)S(1)}, bf16[8,1024]{1,0:T(8,128)(2,1)S(1)}, u32[]{:S(2)}, u32[]{:S(2)}) collective-permute-start(bf16[8,1024]{1,0:T(8,128)(2,1)S(1)} %get-tuple-element.45), channel_id=1, source_target_pairs={{0,128},{16,144},{32,160},{48,176},{64,192},{80,208},{96,224},{112... | collective-permute-start | bytes 49160 | tf_op jit(solution)/shard_map/ppermute | solution.py:22
  11.0 24.1 %copy-start.2 = (bf16[256,512]{1,0:T(8,128)(2,1)S(1)}, bf16[256,512]{1,0:T(8,128)(2,1)}, u32[]{:S(2)}) copy-start(bf16[256,512]{1,0:T(8,128)(2,1)} %q_ref.9) | copy-start | bytes 786436
  11.0 8.1 %collective-permute-start.3 = (bf16[40,1024]{1,0:T(8,128)(2,1)S(1)}, bf16[40,1024]{1,0:T(8,128)(2,1)S(1)}, u32[]{:S(2)}, u32[]{:S(2)}) collective-permute-start(bf16[40,1024]{1,0:T(8,128)(2,1)S(1)} %pad_maximum_fusion.1), channel_id=1, source_target_pairs={{0,32},{16,48},{32,0},{48,16},{64,96},{80,112},{96,64},{112,80},{1... | collective-permute-start | bytes 245768 | tf_op jit(solution)/shard_map/ppermute | solution.py:22
  12.3 22.8 %copy-start = (bf16[256,512]{1,0:T(8,128)(2,1)S(1)}, bf16[256,512]{1,0:T(8,128)(2,1)}, u32[]{:S(2)}) copy-start(bf16[256,512]{1,0:T(8,128)(2,1)} %refs_1_.3) | copy-start | bytes 786436
  12.3 22.8 %copy-start.1 = (bf16[256,512]{1,0:T(8,128)(2,1)S(1)}, bf16[256,512]{1,0:T(8,128)(2,1)}, u32[]{:S(2)}) copy-start(bf16[256,512]{1,0:T(8,128)(2,1)} %refs_2_.3) | copy-start | bytes 786436
  12.3 4.2 %collective-permute-start.1 = (bf16[24,1024]{1,0:T(8,128)(2,1)S(1)}, bf16[24,1024]{1,0:T(8,128)(2,1)S(1)}, u32[]{:S(2)}, u32[]{:S(2)}) collective-permute-start(bf16[24,1024]{1,0:T(8,128)(2,1)S(1)} %constant_dynamic-update-slice_fusion), channel_id=1, source_target_pairs={{0,96},{16,112},{32,64},{48,80},{64,32},{80,48},{96,0},{112,16},{1... | collective-permute-start | bytes 147464 | tf_op jit(solution)/shard_map/ppermute | solution.py:22
  14.1 5.0 %collective-permute-start.2 = (bf16[24,1024]{1,0:T(8,128)(2,1)S(1)}, bf16[24,1024]{1,0:T(8,128)(2,1)S(1)}, u32[]{:S(2)}, u32[]{:S(2)}) collective-permute-start(bf16[24,1024]{1,0:T(8,128)(2,1)S(1)} %constant_dynamic-update-slice_fusion), channel_id=1, source_target_pairs={{0,64},{16,80},{32,96},{48,112},{64,0},{80,16},{96,32},{112,48},{1... | collective-permute-start | bytes 147464 | tf_op jit(solution)/shard_map/ppermute | solution.py:22
  19.3 7.6 %collective-permute-start.6 = (bf16[32,1024]{1,0:T(8,128)(2,1)S(1)}, bf16[32,1024]{1,0:T(8,128)(2,1)S(1)}, u32[]{:S(2)}, u32[]{:S(2)}) collective-permute-start(bf16[32,1024]{1,0:T(8,128)(2,1)S(1)} %get-tuple-element.48), channel_id=1, source_target_pairs={{0,1},{1,0},{2,3},{3,2},{4,5},{5,4},{6,7},{7,6},{8,9},{9,8},{10,11... | collective-permute-start | bytes 196616 | tf_op jit(solution)/shard_map/ppermute | solution.py:22
  20.7 4.0 %collective-permute-start.4 = (bf16[16,1024]{1,0:T(8,128)(2,1)S(1)}, bf16[16,1024]{1,0:T(8,128)(2,1)S(1)}, u32[]{:S(2)}, u32[]{:S(2)}) collective-permute-start(bf16[16,1024]{1,0:T(8,128)(2,1)S(1)} %get-tuple-element.47.level5_ref), channel_id=1, source_target_pairs={{0,3},{1,2},{2,1},{3,0},{4,7},{5,6},{6,5},{7,4},{8,11},{9,10},{10,... | collective-permute-start | bytes 98312 | tf_op jit(solution)/shard_map/ppermute | solution.py:22
  22.6 4.3 %collective-permute-start.5 = (bf16[16,1024]{1,0:T(8,128)(2,1)S(1)}, bf16[16,1024]{1,0:T(8,128)(2,1)S(1)}, u32[]{:S(2)}, u32[]{:S(2)}) collective-permute-start(bf16[16,1024]{1,0:T(8,128)(2,1)S(1)} %get-tuple-element.47.level5_ref), channel_id=1, source_target_pairs={{0,2},{1,3},{2,0},{3,1},{4,6},{5,7},{6,4},{7,5},{8,10},{9,11},{10,... | collective-permute-start | bytes 98312 | tf_op jit(solution)/shard_map/ppermute | solution.py:22
  26.9 8.2 %collective-permute-start.11 = (bf16[160,1024]{1,0:T(8,128)(2,1)S(1)}, bf16[160,1024]{1,0:T(8,128)(2,1)S(1)}, u32[]{:S(2)}, u32[]{:S(2)}) collective-permute-start(bf16[160,1024]{1,0:T(8,128)(2,1)S(1)} %get-tuple-element.52.refs_3_.refs_0_), channel_id=1, source_target_pairs={{0,16},{16,0},{32,48},{48,32},{64,80},{80,64},{96,112},{112,96},{1... | collective-permute-start | bytes 983048 | tf_op jit(solution)/shard_map/ppermute | solution.py:22
  31.4 3.7 %collective-permute-start.10 = (bf16[64,1024]{1,0:T(8,128)(2,1)S(1)}, bf16[64,1024]{1,0:T(8,128)(2,1)S(1)}, u32[]{:S(2)}, u32[]{:S(2)}) collective-permute-start(bf16[64,1024]{1,0:T(8,128)(2,1)S(1)} %get-tuple-element.51), channel_id=1, source_target_pairs={{0,16},{16,0},{32,48},{48,32},{64,80},{80,64},{96,112},{112,96},{1... | collective-permute-start | bytes 393224 | tf_op jit(solution)/shard_map/ppermute | solution.py:22
  31.5 5.8 %collective-permute-start.7 = (bf16[32,1024]{1,0:T(8,128)(2,1)S(1)}, bf16[32,1024]{1,0:T(8,128)(2,1)S(1)}, u32[]{:S(2)}, u32[]{:S(2)}) collective-permute-start(bf16[32,1024]{1,0:T(8,128)(2,1)S(1)} %get-tuple-element.50), channel_id=1, source_target_pairs={{0,12},{1,13},{2,14},{3,15},{4,8},{5,9},{6,10},{7,11},{8,4},{9,5},... | collective-permute-start | bytes 196616 | tf_op jit(solution)/shard_map/ppermute | solution.py:22
  34.6 5.6 %collective-permute-start.8 = (bf16[32,1024]{1,0:T(8,128)(2,1)S(1)}, bf16[32,1024]{1,0:T(8,128)(2,1)S(1)}, u32[]{:S(2)}, u32[]{:S(2)}) collective-permute-start(bf16[32,1024]{1,0:T(8,128)(2,1)S(1)} %get-tuple-element.50), channel_id=1, source_target_pairs={{0,8},{1,9},{2,10},{3,11},{4,12},{5,13},{6,14},{7,15},{8,0},{9,1},... | collective-permute-start | bytes 196616 | tf_op jit(solution)/shard_map/ppermute | solution.py:22
  34.6 5.6 %collective-permute-start.9 = (bf16[32,1024]{1,0:T(8,128)(2,1)S(1)}, bf16[32,1024]{1,0:T(8,128)(2,1)S(1)}, u32[]{:S(2)}, u32[]{:S(2)}) collective-permute-start(bf16[32,1024]{1,0:T(8,128)(2,1)S(1)} %get-tuple-element.50), channel_id=1, source_target_pairs={{0,4},{1,5},{2,6},{3,7},{4,0},{5,1},{6,2},{7,3},{8,12},{9,13},{10,... | collective-permute-start | bytes 196616 | tf_op jit(solution)/shard_map/ppermute | solution.py:22
  40.2 2.0 %collective-permute-start.12 = (bf16[96,1024]{1,0:T(8,128)(2,1)S(1)}, bf16[96,1024]{1,0:T(8,128)(2,1)S(1)}, u32[]{:S(2)}, u32[]{:S(2)}) collective-permute-start(bf16[96,1024]{1,0:T(8,128)(2,1)S(1)} %near.1), channel_id=1, source_target_pairs={{0,16},{16,0},{32,48},{48,32},{64,80},{80,64},{96,112},{112,96},{1... | collective-permute-start | bytes 589832 | tf_op jit(solution)/shard_map/ppermute | solution.py:22
  43.8 7.4 %collective-permute-start.15 = (bf16[64,1024]{1,0:T(8,128)(2,1)S(1)}, bf16[64,1024]{1,0:T(8,128)(2,1)S(1)}, u32[]{:S(2)}, u32[]{:S(2)}) collective-permute-start(bf16[64,1024]{1,0:T(8,128)(2,1)S(1)} %get-tuple-element.54.refs_3_), channel_id=1, source_target_pairs={{0,4},{1,5},{2,6},{3,7},{4,0},{5,1},{6,2},{7,3},{8,12},{9,13},{10,... | collective-permute-start | bytes 393224 | tf_op jit(solution)/shard_map/ppermute | solution.py:22
  44.8 5.8 %collective-permute-start.13 = (bf16[32,1024]{1,0:T(8,128)(2,1)S(1)}, bf16[32,1024]{1,0:T(8,128)(2,1)S(1)}, u32[]{:S(2)}, u32[]{:S(2)}) collective-permute-start(bf16[32,1024]{1,0:T(8,128)(2,1)S(1)} %get-tuple-element.57), channel_id=1, source_target_pairs={{0,12},{1,13},{2,14},{3,15},{4,8},{5,9},{6,10},{7,11},{8,4},{9,5},... | collective-permute-start | bytes 196616 | tf_op jit(solution)/shard_map/ppermute | solution.py:22
  46.2 4.9 %collective-permute-start.14 = (bf16[32,1024]{1,0:T(8,128)(2,1)S(1)}, bf16[32,1024]{1,0:T(8,128)(2,1)S(1)}, u32[]{:S(2)}, u32[]{:S(2)}) collective-permute-start(bf16[32,1024]{1,0:T(8,128)(2,1)S(1)} %get-tuple-element.58), channel_id=1, source_target_pairs={{0,8},{1,9},{2,10},{3,11},{4,12},{5,13},{6,14},{7,15},{8,0},{9,1},... | collective-permute-start | bytes 196616 | tf_op jit(solution)/shard_map/ppermute | solution.py:22
  51.3 5.7 %collective-permute-start.18 = (bf16[64,1024]{1,0:T(8,128)(2,1)S(1)}, bf16[64,1024]{1,0:T(8,128)(2,1)S(1)}, u32[]{:S(2)}, u32[]{:S(2)}) collective-permute-start(bf16[64,1024]{1,0:T(8,128)(2,1)S(1)} %get-tuple-element.61.refs_6_), channel_id=1, source_target_pairs={{0,1},{1,0},{2,3},{3,2},{4,5},{5,4},{6,7},{7,6},{8,9},{9,8},{10,11... | collective-permute-start | bytes 393224 | tf_op jit(solution)/shard_map/ppermute | solution.py:22
  51.7 5.2 %collective-permute-start.16 = (bf16[32,1024]{1,0:T(8,128)(2,1)S(1)}, bf16[32,1024]{1,0:T(8,128)(2,1)S(1)}, u32[]{:S(2)}, u32[]{:S(2)}) collective-permute-start(bf16[32,1024]{1,0:T(8,128)(2,1)S(1)} %get-tuple-element.64), channel_id=1, source_target_pairs={{0,3},{1,2},{2,1},{3,0},{4,7},{5,6},{6,5},{7,4},{8,11},{9,10},{10,... | collective-permute-start | bytes 196616 | tf_op jit(solution)/shard_map/ppermute | solution.py:22
  52.2 4.8 %collective-permute-start.17 = (bf16[32,1024]{1,0:T(8,128)(2,1)S(1)}, bf16[32,1024]{1,0:T(8,128)(2,1)S(1)}, u32[]{:S(2)}, u32[]{:S(2)}) collective-permute-start(bf16[32,1024]{1,0:T(8,128)(2,1)S(1)} %get-tuple-element.65), channel_id=1, source_target_pairs={{0,2},{1,3},{2,0},{3,1},{4,6},{5,7},{6,4},{7,5},{8,10},{9,11},{10,... | collective-permute-start | bytes 196616 | tf_op jit(solution)/shard_map/ppermute | solution.py:22
  57.3 6.1 %collective-permute-start.21 = (bf16[80,1024]{1,0:T(8,128)(2,1)S(1)}, bf16[80,1024]{1,0:T(8,128)(2,1)S(1)}, u32[]{:S(2)}, u32[]{:S(2)}) collective-permute-start(bf16[80,1024]{1,0:T(8,128)(2,1)S(1)} %get-tuple-element.69.refs_5_), channel_id=1, source_target_pairs={{0,32},{16,48},{32,0},{48,16},{64,96},{80,112},{96,64},{112,80},{1... | collective-permute-start | bytes 491528 | tf_op jit(solution)/shard_map/ppermute | solution.py:22
  57.7 5.7 %collective-permute-start.19 = (bf16[48,1024]{1,0:T(8,128)(2,1)S(1)}, bf16[48,1024]{1,0:T(8,128)(2,1)S(1)}, u32[]{:S(2)}, u32[]{:S(2)}) collective-permute-start(bf16[48,1024]{1,0:T(8,128)(2,1)S(1)} %get-tuple-element.74), channel_id=1, source_target_pairs={{0,96},{16,112},{32,64},{48,80},{64,32},{80,48},{96,0},{112,16},{1... | collective-permute-start | bytes 294920 | tf_op jit(solution)/shard_map/ppermute | solution.py:22
  58.3 5.1 %collective-permute-start.20 = (bf16[48,1024]{1,0:T(8,128)(2,1)S(1)}, bf16[48,1024]{1,0:T(8,128)(2,1)S(1)}, u32[]{:S(2)}, u32[]{:S(2)}) collective-permute-start(bf16[48,1024]{1,0:T(8,128)(2,1)S(1)} %get-tuple-element.75), channel_id=1, source_target_pairs={{0,64},{16,80},{32,96},{48,112},{64,0},{80,16},{96,32},{112,48},{1... | collective-permute-start | bytes 294920 | tf_op jit(solution)/shard_map/ppermute | solution.py:22
  63.5 7.0 %collective-permute-start.22 = (bf16[72,1024]{1,0:T(8,128)(2,1)S(1)}, bf16[72,1024]{1,0:T(8,128)(2,1)S(1)}, u32[]{:S(2)}, u32[]{:S(2)}) collective-permute-start(bf16[72,1024]{1,0:T(8,128)(2,1)S(1)} %get-tuple-element.79), channel_id=1, source_target_pairs={{0,16},{16,0},{32,48},{48,32},{64,80},{80,64},{96,112},{112,96},{1... | collective-permute-start | bytes 442376 | tf_op jit(solution)/shard_map/ppermute | solution.py:22
  70.5 6.8 %collective-permute-start.23 = (bf16[8,1024]{1,0:T(8,128)(2,1)S(1)}, bf16[8,1024]{1,0:T(8,128)(2,1)S(1)}, u32[]{:S(2)}, u32[]{:S(2)}) collective-permute-start(bf16[8,1024]{1,0:T(8,128)(2,1)S(1)} %fusion), channel_id=1, source_target_pairs={{0,128},{16,144},{32,160},{48,176},{64,192},{80,208},{96,224},{112... | collective-permute-start | bytes 49160 | tf_op jit(solution)/shard_map/ppermute | solution.py:22
